TPU v7x, 256 devices: a whole 4x4x8 slice. The times are simulated.
256 devices in a mesh: dap: 128 (over x_lo, y, z, core), heads: 2 (over x_hi).
Axes of the slice: x: 4 (x_hi: 2, x_lo: 2; x = x_hi * 2 + x_lo), y: 4, z: 8, core: 2. Of those that a mesh axis runs over, the one named last changes fastest.
Arguments:
- pair: bfloat16 [768, 768, 128], P('dap'), may hold values from -6 to 6
- ln_gain: float32 [128], replicated, may hold values from 0.1 to 1.9
- ln_shift: float32 [128], replicated, may hold values from -3 to 3
- w_project: bfloat16 [128, 4, 128], P(None, None, 'heads'), may hold values from -0.5 to 0.5
- w_bias: bfloat16 [128, 4], P(None, 'heads'), may hold values from -2 to 2
- w_out: bfloat16 [128, 128], P('heads'), may hold values from -0.5 to 0.5
Outputs:
- update: bfloat16 [768, 768, 128], P(('dap', 'heads'))
All inputs are finite; a program needn't handle non-finite values.
Results may differ from a plain program's by a relative error of at most 0.0039.
The roundings to bfloat16 on the way count: a program that leaves them out, or rounds other values in their place, can miss the bound.
Values may be sent and summed in bfloat16 or wider, within the bound.
No kernel may reach another device: no remote copies, remote signals or barrier semaphores. Data moves between devices by JAX's collectives and lax.ppermute only.
A program may use at most 64 MiB of HBM per device.

v0:
```python
import math

import jax
import jax.numpy as jnp
from jax import lax
from jax.sharding import PartitionSpec as P


def normalize(pair, ln_gain, ln_shift):
    values_f = pair.astype(jnp.float32)
    average = jnp.mean(values_f, axis=-1, keepdims=True)
    centred = values_f - average
    variance = jnp.mean(centred * centred, axis=-1, keepdims=True)
    return (centred * lax.rsqrt(variance + 1e-05) * ln_gain + ln_shift).astype(jnp.bfloat16)


def project_entries(normed, flat_w):
    projected = jnp.dot(normed, flat_w, preferred_element_type=jnp.float32)
    head_width = flat_w.shape[1] // 4
    head_part = projected[..., : 3 * head_width].astype(jnp.bfloat16)
    gating = jax.nn.sigmoid(projected[..., 3 * head_width :]).astype(jnp.bfloat16)
    return jnp.concatenate([head_part, gating], axis=-1)


def local(pair, ln_gain, ln_shift, w_project, w_bias, w_out):
    row_count, width_n, channels = pair.shape
    heads_here = w_bias.shape[1]
    head_size = w_project.shape[2] // heads_here
    flat_w = w_project.reshape(channels, -1)
    normed_rows = normalize(pair, ln_gain, ln_shift)
    bias_rows = jnp.einsum("abc,ch->hab", normed_rows, w_bias, preferred_element_type=jnp.float32)
    bias_all = lax.all_gather(bias_rows, "dap", axis=1, tiled=True)
    bias_key_last = jnp.swapaxes(bias_all, 1, 2)
    dap_count = lax.axis_size("dap")
    blocks = pair.reshape(row_count, dap_count, width_n // dap_count, channels)
    packed = project_entries(
        normalize(
            lax.all_to_all(blocks, "dap", split_axis=1, concat_axis=0, tiled=True),
            ln_gain,
            ln_shift,
        ),
        flat_w,
    )
    packed = packed.reshape(width_n, row_count, -1)

    def attend(index):
        column_data = lax.dynamic_index_in_dim(packed, index, 1, keepdims=False)
        pieces = column_data.reshape(width_n, 4, heads_here, head_size)
        scores = jnp.einsum(
            "ihc,khc->hik", pieces[:, 0], pieces[:, 1], preferred_element_type=jnp.float32
        )
        scores = scores * (1.0 / math.sqrt(head_size)) + bias_key_last
        highest = jnp.max(scores, axis=-1, keepdims=True)
        exponent = jnp.exp(scores - highest)
        totals = jnp.sum(exponent, axis=-1)
        weights = exponent.astype(jnp.bfloat16)
        attended = jnp.einsum(
            "hik,khc->ihc", weights, pieces[:, 2], preferred_element_type=jnp.float32
        )
        attended = attended / jnp.swapaxes(totals, 0, 1)[..., None]
        gated_out = (attended * pieces[:, 3].astype(jnp.float32)).astype(jnp.bfloat16)
        return gated_out.reshape(width_n, heads_here * head_size)

    gated_cols = lax.map(attend, jnp.arange(row_count, dtype=jnp.int32))
    returned = lax.all_to_all(
        gated_cols.reshape(row_count, -1), "dap", split_axis=1, concat_axis=0, tiled=True
    )
    returned = returned.reshape(width_n, row_count, heads_here * head_size)
    update = lax.psum_scatter(
        jnp.einsum("jic,cd->ijd", returned, w_out, preferred_element_type=jnp.float32),
        "heads",
        scatter_dimension=0,
        tiled=True,
    )
    return update.astype(jnp.bfloat16)


def solution(mesh):
    in_specs = (
        P("dap", None, None),
        P(),
        P(),
        P(None, None, "heads"),
        P(None, "heads"),
        P("heads", None),
    )
    out_specs = P(("dap", "heads"), None, None)
    return jax.shard_map(local, mesh=mesh, in_specs=in_specs, out_specs=out_specs, check_vma=False)
```

profile of v0, /device:TPU:2, one launch (start us, length us, event | category | flops | bytes accessed | tf_op | source)
XLA Modules:
  0.0 372.7 jit_solution(17273534349222239416)
XLA Ops:
  6.5 0.0 copy-start
  6.5 0.0 copy-start.1
  6.5 0.0 copy-start.3
  6.5 0.0 all-gather.2.cloned.1.call-start
  6.6 1.7 convert_reduce_fusion
  8.4 2.5 fusion.27
  10.9 0.0 copy-done.1
  10.9 0.0 copy-done.3
  10.9 0.0 copy-done.4
  10.9 0.0 copy-done.5
  10.9 2.7 fusion.39
  13.6 0.0 all-gather.2.cloned.1.call-update
  13.6 0.4 reshape.99
  14.1 1.4 copy.17
  15.5 14.2 %all-to-all-start = ((bf16[6,128,6,128]{3,2,0,1:T(8,128)(2,1)}), bf16[6,128,6,128]{3,2,0,1:T(8,128)(2,1)S(1)}, u32[]{:S(2)}, u32[]{:S(2)}) async-start(bf16[6,128,6,128]{3,2,0,1:T(8,128)(2,1)} %copy.17), calls=%async_computation | async-start | bytes 3145728 | tf_op jit(solution)/shard_map/all_to_all | solution.py:38
  29.7 0.0 reduce-scatter.2.cloned.1.call-start
  29.8 42.9 %all-to-all-done = bf16[6,128,6,128]{3,2,0,1:T(8,128)(2,1)S(1)} async-done(((bf16[6,128,6,128]{3,2,0,1:T(8,128)(2,1)}), bf16[6,128,6,128]{3,2,0,1:T(8,128)(2,1)S(1)}, u32[]{:S(2)}, u32[]{:S(2)}) %all-to-all-start) | async-done | bytes 1179680 | tf_op jit(solution)/shard_map/all_to_all | solution.py:38
  72.6 0.9 fusion.18
  73.6 1.9 fusion.21
  75.5 0.1 add_rsqrt_fusion
  75.6 1.9 fusion.24
  77.6 0.0 copy-done
  77.6 0.8 convolution_bitcast_fusion
  78.4 0.2 slice.46
  78.6 0.3 fusion.36
  78.9 0.2 maximum_bitcast_fusion
  79.0 158.6 %all-gather.2.cloned.1.call-done = f32[2,768,768]{2,0,1:T(2,128)} async-done(((f32[2,6,768]{2,0,1:T(2,128)}), f32[2,768,768]{2,0,1:T(2,128)}) %all-gather.2.cloned.1.call-update) | async-done | bytes 4718608 | tf_op jit(solution)/shard_map/all_gather | solution.py:32
  237.7 4.8 %copy.19 = f32[2,768,768]{1,2,0:T(8,128)} copy(f32[2,768,768]{1,0,2:T(2,128)} %bitcast.97) | data formatting | bytes 9437184 | tf_op jit(solution)/shard_map/while | solution.py:64
  242.5 43.5 %while.10 = (s32[]{:T(128)}, bf16[6,768,64]{1,2,0:T(8,128)(2,1)S(1)}, s32[6]{0:T(128)S(1)}, bf16[768,6,256]{0,2,1:T(8,128)(2,1)S(1)}, f32[2,768,768]{1,2,0:T(8,128)}, /*index=5*/s32[]{:T(128)}, s32[]{:T(128)}, s32[]{:T(128)}) while((s32[]{:T(128)}, bf16[6,768,64]{1,2,0:T(8,128)(2,1)S(1)}, s32[6]{0:T(128)S(1)}, ...), condition=%wide.region_7.8_spmd, body=%wide.region_4.7_spmd.sunk | while | flops 159446016 | bytes 20379788 | solution.py:64
  242.5 0.6 dynamic_slice.12
  245.1 3.2 fusion.51
  248.3 0.6 fusion.52
  248.9 0.8 fusion.53
  249.8 0.6 dynamic_slice.12
  252.4 3.2 fusion.51
  255.5 0.6 fusion.52
  256.2 0.8 fusion.53
  257.0 0.6 dynamic_slice.12
  259.6 3.2 fusion.51
  262.8 0.6 fusion.52
  263.4 0.8 fusion.53
  264.3 0.6 dynamic_slice.12
  266.9 3.2 fusion.51
  270.1 0.6 fusion.52
  270.7 0.8 fusion.53
  271.6 0.6 dynamic_slice.12
  274.1 3.2 fusion.51
  277.3 0.6 fusion.52
  278.0 0.8 fusion.53
  278.8 0.6 dynamic_slice.12
  281.4 3.2 fusion.51
  284.6 0.6 fusion.52
  285.2 0.8 fusion.53
  286.1 0.7 copy.20
  286.8 0.7 all_to_all.20
  287.5 0.0 copy-start.2
  287.5 0.4 copy.21
  287.9 33.6 %all_to_all.25 = bf16[6,128,384]{2,0,1:T(8,128)(2,1)S(1)} all-to-all(bf16[6,128,384]{2,0,1:T(8,128)(2,1)S(1)} %copy.21), channel_id=1, replica_groups=mesh['dap'=128,'heads'=2] {'dap'}, dimensions={1} | all-to-all | bytes 1179648 | tf_op jit(solution)/shard_map/all_to_all | solution.py:65
  321.5 1.0 reshape.102
  322.5 0.0 copy-done.2
  322.5 1.9 convolution_bitcast_fusion.1
  324.4 0.0 reduce-scatter.2.cloned.1.call-update
  324.4 39.3 %reduce-scatter.2.cloned.1.call-done = f32[3,768,128]{2,1,0:T(8,128)} async-done(((f32[6,768,128]{2,1,0:T(8,128)}), f32[3,768,128]{2,1,0:T(8,128)}) %reduce-scatter.2.cloned.1.call-update) | async-done | bytes 1179664 | tf_op jit(solution)/shard_map/reduce_scatter | solution.py:69
  363.7 2.2 convert_element_type.59
  (19 shorter events, 0.4 us)
Async XLA Ops:
  6.5 71.0 %copy-start = (bf16[128,4,64]{0,2,1:T(8,128)(2,1)S(1)}, bf16[128,4,64]{0,2,1:T(8,128)(2,1)}, u32[]{:S(2)}) copy-start(bf16[128,4,64]{0,2,1:T(8,128)(2,1)} %param.11) | copy-start | bytes 196612
  6.5 4.3 %copy-start.1 = (bf16[6,768,128]{2,1,0:T(8,128)(2,1)S(1)}, bf16[6,768,128]{2,1,0:T(8,128)(2,1)}, u32[]{:S(2)}) copy-start(bf16[6,768,128]{2,1,0:T(8,128)(2,1)} %param.8) | copy-start | bytes 3538948
  6.5 4.3 %copy-start.3 = (f32[128]{0:T(128)S(1)}, f32[128]{0:T(128)}, u32[]{:S(2)}) copy-start(f32[128]{0:T(128)} %param.10) | copy-start | bytes 1540
  6.5 4.4 %copy-start.4 = (f32[128]{0:T(128)S(1)}, f32[128]{0:T(128)}, u32[]{:S(2)}) copy-start(f32[128]{0:T(128)} %param.9) | copy-start | bytes 1540
  6.5 4.4 %copy-start.5 = (bf16[128,2]{0,1:T(2,128)(2,1)S(1)}, bf16[128,2]{0,1:T(2,128)(2,1)}, u32[]{:S(2)}) copy-start(bf16[128,2]{0,1:T(2,128)(2,1)} %param.12) | copy-start | bytes 1540
  6.5 231.1 %all-gather.2.cloned.1.call-start = ((), (), s32[]{:S(2)}) async-start(), calls=%async_computation.3 | async-start | bytes 4755456 | tf_op jit(solution)/shard_map/all_gather | solution.py:32
  15.5 57.2 %all-to-all-start = ((bf16[6,128,6,128]{3,2,0,1:T(8,128)(2,1)}), bf16[6,128,6,128]{3,2,0,1:T(8,128)(2,1)S(1)}, u32[]{:S(2)}, u32[]{:S(2)}) async-start(bf16[6,128,6,128]{3,2,0,1:T(8,128)(2,1)} %copy.17), calls=%async_computation | async-start | bytes 3145728 | tf_op jit(solution)/shard_map/all_to_all | solution.py:38
  29.7 334.0 %reduce-scatter.2.cloned.1.call-start = ((), (), s32[]{:S(2)}) async-start(), calls=%async_computation.4 | async-start | bytes 3538944 | tf_op jit(solution)/shard_map/reduce_scatter | solution.py:69
  287.5 35.0 %copy-start.2 = (bf16[64,128]{1,0:T(8,128)(2,1)S(1)}, bf16[64,128]{1,0:T(8,128)(2,1)}, u32[]{:S(2)}) copy-start(bf16[64,128]{1,0:T(8,128)(2,1)} %param.13) | copy-start | bytes 49156
Sparse Core Ops, SparseCore 0:
  13.8 223.8 all-gather.1
  324.6 39.0 reduce-scatter.1
where the time goes:
time: 375 us; the launch traced here: 373 us
  waiting for transfers between devices  241 us (64%)
  blocking collectives  33.6 us (9%)
  matrix products  29.4 us (8%)
  other arithmetic  15.6 us (4%)
  starting transfers between devices  14.3 us (4%)
  between operations  13.6 us (4%)
  local copies, waits for them, and re-layouts  13.5 us (4%)
  loops' own time  11.9 us (3%)
    all_gather x1, waiting for transfers between devices, local(): bias_all = lax.all_gather(bias_rows, 'dap', axis=1, tiled=True)  159 us
    all_to_all x1, waiting for transfers between devices, local(): lax.all_to_all(blocks, 'dap', split_axis=1, concat_axis=0, tiled=True)  42.9 us
    reduce_scatter x1, waiting for transfers between devices, local(): lax.psum_scatter(jnp.einsum('jic,cd->ijd', returned, w_out, preferred_ele...  39.3 us
    all_to_all x1, blocking collectives, local(): lax.all_to_all(gated_cols.reshape(row_count, -1), 'dap', split_axis=1, co...  33.6 us
    dot_general x6, matrix products, attend(): jnp.einsum('ihc,khc->hik', pieces[:, 0], pieces[:, 1], preferred_element_...  19 us
    all_to_all x1, starting transfers between devices, local(): lax.all_to_all(blocks, 'dap', split_axis=1, concat_axis=0, tiled=True)  14.2 us
    another operation x1, loops' own time, local(): gated_cols = lax.map(attend, jnp.arange(row_count, dtype=jnp.int32))  11.9 us
  transfers between devices with their start and end apart: 3, of which 3 were waited for; matrix products, arithmetic and copies ran while one was open for 2% of the time, Pallas kernels for 0%

commit v1 on v0

v1 whole, which is shorter than its diff:
```python
import functools
import math

import jax
import jax.numpy as jnp
from jax import lax
from jax.experimental import pallas as pl
from jax.experimental.pallas import tpu as pltpu
from jax.sharding import Mesh
from jax.sharding import PartitionSpec as P

F32 = jnp.float32
BF16 = jnp.bfloat16
CHIP = ("xl", "y", "z")
DAP = ("xl", "y", "z", "c")
N, C, H, DH = 768, 128, 4, 32
CHIPS, COLS, ROWS = 64, 12, 6
QR = 3 * CHIPS
KH = ROWS * CHIPS
PIECE = 40
ROOT = math.sqrt(DH)
NT = (((1,), (1,)), ((), ()))


def params(mb):
    return pltpu.CompilerParams(vmem_limit_bytes=mb * 2**20)


def norm_kernel(pair_ref, gain_ref, shift_ref, rows_ref, split_ref, held):
    x = pair_ref[0].astype(F32)
    average = jnp.mean(x, axis=-1, keepdims=True)
    centred = x - average
    variance = jnp.mean(centred * centred, axis=-1, keepdims=True)
    normed = (centred * lax.rsqrt(variance + 1e-05) * gain_ref[...] + shift_ref[...]).astype(BF16)
    rows_ref[0] = normed
    held[...] = normed.astype(F32)
    for m in range(COLS):
        split_ref[0, m] = held[pl.ds(m, CHIPS, stride=COLS), :].astype(BF16)


def normalize(pair, gain, shift):
    return pl.pallas_call(
        norm_kernel,
        grid=(ROWS,),
        in_specs=[
            pl.BlockSpec((1, N, C), lambda a: (a, 0, 0)),
            pl.BlockSpec((1, C), lambda a: (0, 0)),
            pl.BlockSpec((1, C), lambda a: (0, 0)),
        ],
        out_specs=[
            pl.BlockSpec((1, N, C), lambda a: (a, 0, 0)),
            pl.BlockSpec((1, COLS, CHIPS, C), lambda a: (a, 0, 0, 0)),
        ],
        out_shape=[
            jax.ShapeDtypeStruct((ROWS, N, C), BF16),
            jax.ShapeDtypeStruct((ROWS, COLS, CHIPS, C), BF16),
        ],
        scratch_shapes=[pltpu.VMEM((N, C), F32)],
        compiler_params=params(24),
        name="norm",
    )(pair, gain, shift)


def bias_kernel(head_ref, split_ref, own_ref, other_ref, out_ref):
    for a in range(ROWS):
        entries = split_ref[a, :, 0].reshape(2 * QR, C)
        own = lax.dot_general(own_ref[...], entries, NT, preferred_element_type=F32) * ROOT
        other = lax.dot_general(other_ref[...], entries, NT, preferred_element_type=F32) * ROOT
        for core in range(2):
            at = core * QR
            row = jnp.concatenate(
                [part[g : g + 1, at : at + QR] for part in (own, other) for g in range(2)], axis=1
            )
            for s in range(6):
                out_ref[core, a * 6 + s : a * 6 + s + 1, :] = row[:, s * C : (s + 1) * C]
    out_ref[:, 36:, :] = jnp.zeros((2, PIECE - 36, C), F32)


def bias_pieces(head, split, own, other):
    return pl.pallas_call(
        bias_kernel,
        grid_spec=pltpu.PrefetchScalarGridSpec(
            num_scalar_prefetch=1,
            grid=(1,),
            in_specs=[
                pl.BlockSpec((ROWS, 2, 1, QR, C), lambda g, head: (0, 0, head[0], 0, 0)),
                pl.BlockSpec((16, C), lambda g, head: (0, 0)),
                pl.BlockSpec((16, C), lambda g, head: (0, 0)),
            ],
            out_specs=pl.BlockSpec((2, PIECE, C), lambda g, head: (0, 0, 0)),
        ),
        out_shape=jax.ShapeDtypeStruct((2, PIECE, C), F32),
        compiler_params=params(24),
        name="bias",
    )(head, split.reshape(ROWS, 2, 2, QR, C), own, other)


def place_kernel(where_ref, *refs):
    parts, out_ref = refs[:4], refs[4]
    y, core = where_ref[0], where_ref[1]
    for step, part in enumerate(parts):
        source = lax.rem(y - step + 4, 4)
        for other in range(2):
            from_core = lax.rem(core + other, 2)
            for a in range(ROWS):
                for xl in range(2):
                    to = (other * ROWS + a) * CHIPS + xl * 32 + source * 8
                    to = pl.multiple_of(to, 8)
                    for s in range(6):
                        at = xl * 16 * PIECE + from_core * PIECE + a * 6 + s
                        out_ref[pl.ds(to, 8), s * C : (s + 1) * C] = part[
                            pl.ds(at, 8, stride=2 * PIECE), :
                        ]


def place_bias(where, parts):
    return pl.pallas_call(
        place_kernel,
        grid_spec=pltpu.PrefetchScalarGridSpec(
            num_scalar_prefetch=1,
            grid=(1,),
            in_specs=[pl.BlockSpec((32 * PIECE, C), lambda g, w: (0, 0))] * 4,
            out_specs=pl.BlockSpec((N, 4 * QR), lambda g, w: (0, 0)),
        ),
        out_shape=jax.ShapeDtypeStruct((N, 4 * QR), F32),
        compiler_params=params(32),
        name="place",
    )(where, *parts)


def attend_kernel(
    head_ref, own_ref, other_ref, query_ref, bias_ref, wk_ref, wv_ref, wq_ref, wg_ref, wo_ref, out_ref
):
    entries = jnp.concatenate([own_ref[0], other_ref[0]], axis=0)
    asked = jnp.concatenate([query_ref[0], query_ref[0]], axis=0)
    keys = jnp.dot(entries, wk_ref[...], preferred_element_type=F32).astype(BF16)
    values = lax.dot_general(wv_ref[...], entries, NT, preferred_element_type=F32).astype(BF16)
    queries = lax.dot_general(wq_ref[...], asked, NT, preferred_element_type=F32)
    gates = jax.nn.sigmoid(lax.dot_general(wg_ref[...], asked, NT, preferred_element_type=F32))
    gates = gates.astype(BF16).astype(F32)
    head_of_channel = lax.broadcasted_iota(jnp.int32, (C, 2 * QR), 0) // DH
    second = (lax.broadcasted_iota(jnp.int32, (C, 2 * QR), 1) >= QR).astype(jnp.int32)
    masked = [jnp.where(head_of_channel == 2 * g + second, queries, 0.0).astype(BF16) for g in range(2)]
    masked = jnp.concatenate(masked, axis=1)
    factor = 1.0 / (ROOT * math.log(2.0))
    sums, totals = [], []
    for n in range(3):
        lanes = slice(n * 256, (n + 1) * 256)
        scores = jnp.dot(keys, masked[:, lanes], preferred_element_type=F32) + bias_ref[:, lanes]
        highest = jnp.max(scores, axis=0, keepdims=True)
        exponent = jnp.exp2((scores - highest) * factor)
        totals.append(jnp.sum(exponent, axis=0, keepdims=True))
        sums.append(jnp.dot(values, exponent.astype(BF16), preferred_element_type=F32))
    sums = jnp.concatenate(sums, axis=1)
    totals = jnp.concatenate(totals, axis=1)
    first = lax.broadcasted_iota(jnp.int32, (DH, 2 * QR), 1) < QR
    gated = []
    for g in range(2):
        lanes = slice(g * 2 * QR, (g + 1) * 2 * QR)
        low, high = slice(2 * g * DH, (2 * g + 1) * DH), slice((2 * g + 1) * DH, (2 * g + 2) * DH)
        attended = jnp.where(first, sums[low, lanes], sums[high, lanes]) / totals[:, lanes]
        gated.append(attended * jnp.where(first, gates[low], gates[high]))
    gated = jnp.concatenate(gated, axis=0)
    turned = gated.T.astype(BF16)
    turned = jnp.concatenate([turned[:QR], turned[QR:]], axis=1)
    update = jnp.dot(turned, wo_ref[...], preferred_element_type=F32).astype(BF16)
    out_ref[0] = update


def attend(head, own, other, bias, wk, wv, wq, wg, wo):
    weight = pl.BlockSpec((C, C), lambda m, head: (0, 0))
    return pl.pallas_call(
        attend_kernel,
        grid_spec=pltpu.PrefetchScalarGridSpec(
            num_scalar_prefetch=1,
            grid=(COLS,),
            in_specs=[
                pl.BlockSpec((1, KH, C), lambda m, head: (m, 0, 0)),
                pl.BlockSpec((1, KH, C), lambda m, head: (m, 0, 0)),
                pl.BlockSpec((1, QR, C), lambda m, head: (m, head[0], 0)),
                pl.BlockSpec((N, 4 * QR), lambda m, head: (0, 0)),
                weight,
                weight,
                weight,
                weight,
                weight,
            ],
            out_specs=pl.BlockSpec((1, QR, C), lambda m, head: (m, 0, 0)),
        ),
        out_shape=jax.ShapeDtypeStruct((COLS, QR, C), BF16),
        compiler_params=params(48),
        name="attend",
    )(head, own, other, own, bias, wk, wv, wq, wg, wo)


def local(pair, ln_gain, ln_shift, w_project, w_bias, w_out):
    swap_heads = functools.partial(lax.ppermute, axis_name="h", perm=[(0, 1), (1, 0)])
    swap_cores = functools.partial(lax.ppermute, axis_name="c", perm=[(0, 1), (1, 0)])
    head = lax.axis_index("h").astype(jnp.int32).reshape(1)
    where = jnp.stack([lax.axis_index("y"), lax.axis_index("c")]).astype(jnp.int32)

    bias_own = jnp.pad(w_bias.T, ((0, 14), (0, 0)))
    bias_other = swap_heads(bias_own)
    weights = jnp.concatenate([w_project.reshape(C, 4 * 64), w_out.T], axis=1)
    weights_other = swap_heads(weights)

    rows, split = normalize(pair, ln_gain.reshape(1, C), ln_shift.reshape(1, C))
    pieces = bias_pieces(head, split, bias_own, bias_other)
    spread = jnp.broadcast_to(pieces[None], (16, 2, PIECE, C)).reshape(32, PIECE, C)
    near = lax.all_to_all(spread, ("xl", "z", "c"), 0, 0, tiled=True)
    parts = [near] + [lax.ppermute(near, "y", [(i, (i + o) % 4) for i in range(4)]) for o in (1, 2, 3)]
    bias = place_bias(where, [part.reshape(32 * PIECE, C) for part in parts])

    blocks = rows.reshape(ROWS, CHIPS, COLS, C).transpose(1, 0, 2, 3).reshape(CHIPS, ROWS * COLS, C)
    arrived = lax.all_to_all(blocks, CHIP, 0, 0, tiled=True)
    own = arrived.reshape(CHIPS, ROWS, COLS, C).transpose(2, 1, 0, 3).reshape(COLS, KH, C)
    other = swap_cores(own)

    full = [
        jnp.concatenate([weights[:, t * 64 : (t + 1) * 64], weights_other[:, t * 64 : (t + 1) * 64]], axis=1)
        for t in range(5)
    ]
    wo = full[4].T.reshape(2, 2, DH, C).transpose(1, 0, 2, 3).reshape(C, C)
    done = attend(head, own, other, bias, full[1], full[2].T, full[0].T, full[3].T, wo)

    sent = done.reshape(COLS, 3, CHIPS, C).transpose(2, 1, 0, 3).reshape(CHIPS, 3 * COLS, C)
    returned = lax.all_to_all(sent, CHIP, 0, 0, tiled=True)
    return returned.reshape(CHIPS, 3, COLS, C).transpose(1, 0, 2, 3).reshape(3, N, C)


def solution(mesh):
    fine = Mesh(mesh.devices.reshape(2, 4, 8, 2, 2), DAP + ("h",))
    in_specs = (P(DAP, None, None), P(), P(), P(None, None, "h"), P(None, "h"), P("h", None))
    out_specs = P(DAP + ("h",), None, None)
    return jax.shard_map(local, mesh=fine, in_specs=in_specs, out_specs=out_specs, check_vma=False)
```

time: 375 us -> 174 us (0.46)
  waiting for transfers between devices: 241 us -> 71.4 us
  Pallas kernels: 0 us -> 32.8 us
  matrix products: 29.4 us -> 0 us
  other arithmetic: 15.6 us -> 0.1 us
  between operations: 13.6 us -> 0.18 us
  loops' own time: 11.9 us -> 0 us
  starting transfers between devices: 14.3 us -> 26.2 us
    all_gather x1 -> x0, waiting for transfers between devices: 159 us -> none  [local(): bias_all = lax.all_gather(bias_rows, 'dap', axis=1, tiled=True)]
    reduce_scatter x1 -> x0, waiting for transfers between devices: 39.3 us -> none  [local(): lax.psum_scatter(jnp.einsum('jic,cd->ijd', returned, w_out, preferred_ele...]
    pallas_call x0 -> x4, Pallas kernels: none -> 32.8 us  [the longest x1 27.6 us: attend(): pl.pallas_call(attend_kernel, grid_spec=pltpu.PrefetchScalarGridSpec(num_...]
    ppermute x0 -> x6, waiting for transfers between devices: none -> 29.9 us  [the longest x3 26.8 us: local(): lax.ppermute(near, 'y', [(i, (i + o) % 4) for i in range(4)])]
    dot_general x15 -> x0, matrix products: 29.4 us -> none  [the longest x6 19 us: attend(): jnp.einsum('ihc,khc->hik', pieces[:, 0], pieces[:, 1], preferred_element_...]
    another operation x1 -> x0, loops' own time: 11.9 us -> none  [local(): gated_cols = lax.map(attend, jnp.arange(row_count, dtype=jnp.int32))]
    reduce_sum x10 -> x0, other arithmetic: 10.9 us -> none  [the longest x2 4.39 us: normalize(): variance = jnp.mean(centred * centred, axis=-1, keepdims=True)]
    ppermute x0 -> x6, starting transfers between devices: none -> 8.5 us  [the longest x3 3.84 us: local(): lax.ppermute(near, 'y', [(i, (i + o) % 4) for i in range(4)])]
  transfers between devices with their start and end apart: 3 -> 8, of which waited for: 3 -> 6; matrix products, arithmetic and copies ran while one was open for 2% -> 1% of each run, Pallas kernels for 0% -> 2%
where the time goes in v1:
time: 174 us
  waiting for transfers between devices  71.4 us (41%)
  Pallas kernels  32.8 us (19%)
  blocking collectives  30.1 us (17%)
  starting transfers between devices  26.2 us (15%)
  local copies, waits for them, and re-layouts  12.9 us (7%)
    all_to_all x1, blocking collectives, local(): returned = lax.all_to_all(sent, CHIP, 0, 0, tiled=True)  30.1 us
    pallas_call x1, Pallas kernels, attend(): pl.pallas_call(attend_kernel, grid_spec=pltpu.PrefetchScalarGridSpec(num_...  27.6 us
    ppermute x3, waiting for transfers between devices, local(): lax.ppermute(near, 'y', [(i, (i + o) % 4) for i in range(4)])  26.8 us
    all_to_all x1, waiting for transfers between devices, local(): arrived = lax.all_to_all(blocks, CHIP, 0, 0, tiled=True)  26.3 us
    all_to_all x1, waiting for transfers between devices, local(): near = lax.all_to_all(spread, ('xl', 'z', 'c'), 0, 0, tiled=True)  15.2 us
    all_to_all x1, starting transfers between devices, local(): arrived = lax.all_to_all(blocks, CHIP, 0, 0, tiled=True)  13.3 us
    all_to_all x1, starting transfers between devices, local(): near = lax.all_to_all(spread, ('xl', 'z', 'c'), 0, 0, tiled=True)  4.36 us
    ppermute x3, starting transfers between devices, local(): lax.ppermute(near, 'y', [(i, (i + o) % 4) for i in range(4)])  3.84 us
  transfers between devices with their start and end apart: 8, of which 6 were waited for; matrix products, arithmetic and copies ran while one was open for 1% of the time, Pallas kernels for 2%

profile of v1, /device:TPU:2, one launch (start us, length us, event | category | flops | bytes accessed | tf_op | source)
XLA Modules:
  0.0 173.6 jit_solution(9147649320737616616)
XLA Ops:
  0.0 0.0 copy-start
  0.0 1.3 copy-done
  1.3 0.0 copy-start.1
  1.3 0.7 copy-done.1
  1.9 0.0 copy-start.2
  1.9 0.7 copy-done.2
  2.6 1.9 %norm.1 = (bf16[6,768,128]{2,1,0:T(8,128)(2,1)S(1)}, bf16[6,12,64,128]{3,2,1,0:T(8,128)(2,1)S(1)}) custom-call(bf16[6,768,128]{2,1,0:T(8,128)(2,1)S(1)} %copy-done, f32[1,128]{1,0:T(1,128)S(1)} %bitcast.46, f32[1,128]{1,0:T(1,128)S(1)} %bitcast.47), custom_call_target="tpu_custom_call" | custom-call | tf_op jit(solution)/shard_map/norm/pallas_call | solution.py:42
  4.5 1.3 reshape.64
  5.8 1.7 copy.15
  7.5 1.8 %copy.16 = bf16[64,72,128]{2,1,0:T(8,128)(2,1)} copy(bf16[64,72,128]{2,0,1:T(8,128)(2,1)S(1)} %bitcast.50) | data formatting | bytes 2359296 | tf_op jit(solution)/shard_map/reshape | solution.py:214
  9.4 0.0 copy-start.6
  9.4 13.3 %all-to-all-start = ((bf16[64,72,128]{2,1,0:T(8,128)(2,1)}), bf16[64,72,128]{2,1,0:T(8,128)(2,1)S(1)}, u32[]{:S(2)}, u32[]{:S(2)}) async-start(bf16[64,72,128]{2,1,0:T(8,128)(2,1)} %copy.16), calls=%async_computation | async-start | bytes 2359296 | tf_op jit(solution)/shard_map/all_to_all | solution.py:215
  22.7 0.0 copy-done.6
  22.7 2.2 %collective-permute-start.1 = (bf16[16,128]{1,0:T(8,128)(2,1)S(1)}, bf16[16,128]{1,0:T(8,128)(2,1)S(1)}, u32[]{:S(2)}, u32[]{:S(2)}) collective-permute-start(bf16[16,128]{1,0:T(8,128)(2,1)S(1)} %pad.4.own_ref), channel_id=1, source_target_pairs={{0,1},{1,0},{2,3},{3,2},{4,5},{5,4},{6,7},{7,6},{8,9},{9,8},{10,11... | collective-permute-start | bytes 12296 | tf_op jit(solution)/shard_map/ppermute | solution.py:203
  24.9 3.1 %collective-permute-done.1.other_ref = bf16[16,128]{1,0:T(8,128)(2,1)S(1)} collective-permute-done((bf16[16,128]{1,0:T(8,128)(2,1)S(1)}, bf16[16,128]{1,0:T(8,128)(2,1)S(1)}, u32[]{:S(2)}, u32[]{:S(2)}) %collective-permute-start.1) | collective-permute-done | bytes 4128 | tf_op jit(solution)/shard_map/ppermute | solution.py:203
  28.1 0.6 bias.1
  28.7 26.3 %all-to-all-done = bf16[64,72,128]{2,1,0:T(8,128)(2,1)S(1)} async-done(((bf16[64,72,128]{2,1,0:T(8,128)(2,1)}), bf16[64,72,128]{2,1,0:T(8,128)(2,1)S(1)}, u32[]{:S(2)}, u32[]{:S(2)}) %all-to-all-start) | async-done | bytes 1179680 | tf_op jit(solution)/shard_map/all_to_all | solution.py:215
  55.0 0.0 copy-start.3
  55.0 0.9 broadcast_in_dim.2
  55.9 0.3 copy-done.3
  56.2 4.4 %all-to-all-start.1 = ((f32[32,40,128]{2,1,0:T(8,128)}), f32[32,40,128]{2,1,0:T(8,128)S(1)}, u32[]{:S(2)}, u32[]{:S(2)}) async-start(f32[32,40,128]{2,1,0:T(8,128)} %bitcast.12), calls=%async_computation.1 | async-start | bytes 1310720 | tf_op jit(solution)/shard_map/all_to_all | solution.py:210
  60.6 1.6 copy.17
  62.2 0.0 copy-start.4
  62.2 0.0 copy-start.5
  62.2 0.1 copy.18
  62.3 0.2 collective-permute-start
  62.5 0.5 copy-done.4
  63.0 0.0 copy-done.5
  63.0 2.2 %collective-permute-start.5 = (bf16[128,320]{0,1:T(8,128)(2,1)S(1)}, bf16[128,320]{0,1:T(8,128)(2,1)S(1)}, u32[]{:S(2)}, u32[]{:S(2)}) collective-permute-start(bf16[128,320]{0,1:T(8,128)(2,1)S(1)} %pad_maximum_fusion), channel_id=1, source_target_pairs={{0,1},{1,0},{2,3},{3,2},{4,5},{5,4},{6,7},{7,6},{8,9},{9,8},{10,11... | collective-permute-start | bytes 245768 | tf_op jit(solution)/shard_map/ppermute | solution.py:205
  65.2 15.2 %all-to-all-done.1 = f32[32,40,128]{2,1,0:T(8,128)S(1)} async-done(((f32[32,40,128]{2,1,0:T(8,128)}), f32[32,40,128]{2,1,0:T(8,128)S(1)}, u32[]{:S(2)}, u32[]{:S(2)}) %all-to-all-start.1) | async-done | bytes 655392 | tf_op jit(solution)/shard_map/all_to_all | solution.py:210
  80.4 0.6 collective-permute-start.2
  81.0 2.6 %collective-permute-start.3 = (f32[32,40,128]{2,1,0:T(8,128)S(1)}, f32[32,40,128]{2,1,0:T(8,128)}, u32[]{:S(2)}, u32[]{:S(2)}) collective-permute-start(f32[32,40,128]{2,1,0:T(8,128)S(1)} %all-to-all-done.1), channel_id=1, source_target_pairs={{0,64},{32,96},{64,0},{96,32},{1,65},{33,97},{65,1},{97,33},{2,66}... | collective-permute-start | bytes 1966088 | tf_op jit(solution)/shard_map/ppermute | solution.py:211
  83.7 0.6 collective-permute-start.4
  84.2 0.1 pad_add_fusion.where_ref
  84.3 0.0 collective-permute-done.5
  84.4 0.1 copy.20.wk_ref
  84.5 14.9 %collective-permute-done.2 = f32[32,40,128]{2,1,0:T(8,128)} collective-permute-done((f32[32,40,128]{2,1,0:T(8,128)S(1)}, f32[32,40,128]{2,1,0:T(8,128)}, u32[]{:S(2)}, u32[]{:S(2)}) %collective-permute-start.2) | collective-permute-done | bytes 655392 | tf_op jit(solution)/shard_map/ppermute | solution.py:211
  99.4 11.3 %collective-permute-done.3 = f32[32,40,128]{2,1,0:T(8,128)} collective-permute-done((f32[32,40,128]{2,1,0:T(8,128)S(1)}, f32[32,40,128]{2,1,0:T(8,128)}, u32[]{:S(2)}, u32[]{:S(2)}) %collective-permute-start.3) | collective-permute-done | bytes 655392 | tf_op jit(solution)/shard_map/ppermute | solution.py:211
  110.7 0.6 collective-permute-done.4
  111.3 2.8 %place.1.bias_ref = f32[768,768]{1,0:T(8,128)S(1)} custom-call(s32[2]{0:T(128)S(1)} %pad_add_fusion.where_ref, f32[1280,128]{1,0:T(8,128)S(1)} %bitcast.42, f32[1280,128]{1,0:T(8,128)} %bitcast.14.refs_1_, f32[1280,128]{1,0:T(8,128)} %bitcast.15.refs_2_, f32[1280,128]{1,0:T(8,128)} %bitcast.16.refs_3_), custom_call_target="tpu_custom_call" | custom-call | tf_op jit(solution)/shard_map/place/pallas_call | solution.py:117
  114.0 0.0 collective-permute-done.other_ref
  114.0 27.6 %attend.1 = bf16[12,192,128]{2,1,0:T(8,128)(2,1)S(1)} custom-call(s32[1]{0:T(128)} %bitcast.head_ref, bf16[12,384,128]{2,1,0:T(8,128)(2,1)S(1)} %bitcast.40, bf16[12,384,128]{2,1,0:T(8,128)(2,1)S(1)} %collective-permute-done.other_ref, bf16[12,384,128]{2,1,0:T(8,128)(2,1)S(1)} %bitcast.41, f32[768,768]{1,0:T(8,128)S(1)} %place.1.bias_ref, ...), custom_call_target="tpu_custom_call" | custom-call | tf_op jit(solution)/shard_map/attend/pallas_call | solution.py:172
  141.6 0.4 copy.22
  142.0 30.1 %all_to_all.15 = bf16[64,36,128]{2,1,0:T(8,128)(2,1)S(1)} all-to-all(bf16[64,36,128]{2,1,0:T(8,128)(2,1)S(1)} %copy.22), channel_id=1, replica_groups=mesh['xl'=2,'y'=4,'z'=8,'c'=2,'h'=2] {'xl','y','z'}, dimensions={0} | all-to-all | bytes 1179648 | tf_op jit(solution)/shard_map/all_to_all | solution.py:227
  172.1 0.1 copy.23
  172.2 0.4 copy.24
  172.6 1.0 reshape.80
  (9 shorter events, 0.1 us)
Async XLA Ops:
  0.0 1.3 copy-start
  1.3 0.7 copy-start.1
  1.9 0.7 copy-start.2
  9.4 13.4 %copy-start.6 = (bf16[128,2]{0,1:T(2,128)(2,1)S(1)}, bf16[128,2]{0,1:T(2,128)(2,1)}, u32[]{:S(2)}) copy-start(bf16[128,2]{0,1:T(2,128)(2,1)} %param.10) | copy-start | bytes 1540
  9.4 45.6 %all-to-all-start = ((bf16[64,72,128]{2,1,0:T(8,128)(2,1)}), bf16[64,72,128]{2,1,0:T(8,128)(2,1)S(1)}, u32[]{:S(2)}, u32[]{:S(2)}) async-start(bf16[64,72,128]{2,1,0:T(8,128)(2,1)} %copy.16), calls=%async_computation | async-start | bytes 2359296 | tf_op jit(solution)/shard_map/all_to_all | solution.py:215
  22.7 5.3 %collective-permute-start.1 = (bf16[16,128]{1,0:T(8,128)(2,1)S(1)}, bf16[16,128]{1,0:T(8,128)(2,1)S(1)}, u32[]{:S(2)}, u32[]{:S(2)}) collective-permute-start(bf16[16,128]{1,0:T(8,128)(2,1)S(1)} %pad.4.own_ref), channel_id=1, source_target_pairs={{0,1},{1,0},{2,3},{3,2},{4,5},{5,4},{6,7},{7,6},{8,9},{9,8},{10,11... | collective-permute-start | bytes 12296 | tf_op jit(solution)/shard_map/ppermute | solution.py:203
  55.0 1.2 copy-start.3
  56.2 24.2 %all-to-all-start.1 = ((f32[32,40,128]{2,1,0:T(8,128)}), f32[32,40,128]{2,1,0:T(8,128)S(1)}, u32[]{:S(2)}, u32[]{:S(2)}) async-start(f32[32,40,128]{2,1,0:T(8,128)} %bitcast.12), calls=%async_computation.1 | async-start | bytes 1310720 | tf_op jit(solution)/shard_map/all_to_all | solution.py:210
  62.2 0.8 copy-start.4
  62.2 0.8 copy-start.5
  62.3 51.7 %collective-permute-start = (bf16[12,384,128]{2,1,0:T(8,128)(2,1)S(1)}, bf16[12,384,128]{2,1,0:T(8,128)(2,1)S(1)}, u32[]{:S(2)}, u32[]{:S(2)}) collective-permute-start(bf16[12,384,128]{2,1,0:T(8,128)(2,1)S(1)} %bitcast.39), channel_id=1, source_target_pairs={{0,2},{2,0},{1,3},{3,1},{4,6},{6,4},{5,7},{7,5},{8,10},{10,8},{9,1... | collective-permute-start | bytes 3538952 | tf_op jit(solution)/shard_map/ppermute | solution.py:217
  63.0 21.3 %collective-permute-start.5 = (bf16[128,320]{0,1:T(8,128)(2,1)S(1)}, bf16[128,320]{0,1:T(8,128)(2,1)S(1)}, u32[]{:S(2)}, u32[]{:S(2)}) collective-permute-start(bf16[128,320]{0,1:T(8,128)(2,1)S(1)} %pad_maximum_fusion), channel_id=1, source_target_pairs={{0,1},{1,0},{2,3},{3,2},{4,5},{5,4},{6,7},{7,6},{8,9},{9,8},{10,11... | collective-permute-start | bytes 245768 | tf_op jit(solution)/shard_map/ppermute | solution.py:205
  80.4 19.0 %collective-permute-start.2 = (f32[32,40,128]{2,1,0:T(8,128)S(1)}, f32[32,40,128]{2,1,0:T(8,128)}, u32[]{:S(2)}, u32[]{:S(2)}) collective-permute-start(f32[32,40,128]{2,1,0:T(8,128)S(1)} %all-to-all-done.1), channel_id=1, source_target_pairs={{0,32},{32,64},{64,96},{96,0},{1,33},{33,65},{65,97},{97,1},{2,34}... | collective-permute-start | bytes 1966088 | tf_op jit(solution)/shard_map/ppermute | solution.py:211
  81.0 29.6 %collective-permute-start.3 = (f32[32,40,128]{2,1,0:T(8,128)S(1)}, f32[32,40,128]{2,1,0:T(8,128)}, u32[]{:S(2)}, u32[]{:S(2)}) collective-permute-start(f32[32,40,128]{2,1,0:T(8,128)S(1)} %all-to-all-done.1), channel_id=1, source_target_pairs={{0,64},{32,96},{64,0},{96,32},{1,65},{33,97},{65,1},{97,33},{2,66}... | collective-permute-start | bytes 1966088 | tf_op jit(solution)/shard_map/ppermute | solution.py:211
  83.7 27.6 %collective-permute-start.4 = (f32[32,40,128]{2,1,0:T(8,128)S(1)}, f32[32,40,128]{2,1,0:T(8,128)}, u32[]{:S(2)}, u32[]{:S(2)}) collective-permute-start(f32[32,40,128]{2,1,0:T(8,128)S(1)} %all-to-all-done.1), channel_id=1, source_target_pairs={{0,96},{32,0},{64,32},{96,64},{1,97},{33,1},{65,33},{97,65},{2,98}... | collective-permute-start | bytes 1966088 | tf_op jit(solution)/shard_map/ppermute | solution.py:211

commit v2 on v1

v2 whole, which is shorter than its diff:
```python
import functools
import math

import jax
import jax.numpy as jnp
from jax import lax
from jax.experimental import pallas as pl
from jax.experimental.pallas import tpu as pltpu
from jax.sharding import Mesh
from jax.sharding import PartitionSpec as P

F32 = jnp.float32
BF16 = jnp.bfloat16
CHIP = ("xl", "y", "z")
DAP = ("xl", "y", "z", "c")
N, C, H, DH = 768, 128, 4, 32
CHIPS, COLS, ROWS = 64, 12, 6
QR = 3 * CHIPS
KH = ROWS * CHIPS
LEVELS = 240
GROUP = 6
PIECE = 36
ROOT = math.sqrt(DH)
NT = (((1,), (1,)), ((), ()))


def params(mb):
    return pltpu.CompilerParams(vmem_limit_bytes=mb * 2**20)


def layer_norm(x, gain, shift):
    average = jnp.mean(x, axis=-1, keepdims=True)
    centred = x - average
    variance = jnp.mean(centred * centred, axis=-1, keepdims=True)
    return centred * lax.rsqrt(variance + 1e-05) * gain + shift


def norm_kernel(pair_ref, gain_ref, shift_ref, out_ref):
    out_ref[0] = layer_norm(pair_ref[0].astype(F32), gain_ref[...], shift_ref[...]).astype(BF16)


def normalize(pair, gain, shift):
    return pl.pallas_call(
        norm_kernel,
        grid=(ROWS,),
        in_specs=[
            pl.BlockSpec((1, N, C), lambda a: (a, 0, 0)),
            pl.BlockSpec((1, C), lambda a: (0, 0)),
            pl.BlockSpec((1, C), lambda a: (0, 0)),
        ],
        out_specs=pl.BlockSpec((1, N, C), lambda a: (a, 0, 0)),
        out_shape=jax.ShapeDtypeStruct((ROWS, N, C), BF16),
        compiler_params=params(24),
        cost_estimate=pl.CostEstimate(flops=10 * ROWS * N * C, bytes_accessed=4 * ROWS * N * C, transcendentals=0),
        name="norm",
    )(pair, gain, shift)


def bias_range(w, gain, shift):
    w = w.astype(F32)
    middle = jnp.sum(w * shift, axis=1, keepdims=True)
    reach = jnp.sqrt(C * jnp.sum(w * w * gain * gain, axis=1, keepdims=True))
    rounded = jnp.sum(jnp.abs(w * shift), axis=1, keepdims=True)
    return middle, reach * (1 + 1 / 256) + rounded / 256 + 1e-20


def encode(x):
    size = jnp.minimum(jnp.abs(x) * LEVELS, LEVELS - 0.01)
    whole = jnp.floor(size)
    code = jnp.exp2(whole - LEVELS / 2) * (1 + (size - whole))
    return jnp.where(x < 0, -code, code).astype(BF16)


def decode(code):
    code = code.astype(F32)
    size = jnp.abs(code)
    whole = jnp.floor(jnp.log2(size))
    x = (whole + (LEVELS / 2 - 1) + size * jnp.exp2(-whole)) / LEVELS
    return jnp.where(code < 0, -x, x)


def bias_kernel(
    where_ref, own_ref, other_ref, gain_ref, shift_ref, w_own_ref, w_other_ref, out_ref, held, coded
):
    first = 6 * where_ref[1] + 3 * where_ref[0]
    weights = [w_ref[...] for w_ref in (w_own_ref, w_other_ref)]
    ranges = [bias_range(w, gain_ref[...], shift_ref[...]) for w in weights]
    for o, rows_ref in enumerate((own_ref, other_ref)):
        for a in range(ROWS):
            held[...] = rows_ref[a].astype(F32)
            entries = jnp.concatenate(
                [held[pl.ds(first + r, CHIPS, stride=COLS), :] for r in range(3)], axis=0
            )
            entries = layer_norm(entries, gain_ref[...], shift_ref[...]).astype(BF16)
            parts = [
                (lax.dot_general(w, entries, NT, preferred_element_type=F32) - middle) / reach
                for w, (middle, reach) in zip(weights, ranges)
            ]
            row = jnp.concatenate([part[g : g + 1] for part in parts for g in range(2)], axis=1)
            for s in range(6):
                at = (o * ROWS + a) * 6 + s
                coded[at : at + 1, :] = row[:, s * C : (s + 1) * C]
    out_ref[...] = encode(coded[...])


def bias_piece(where, own, other, gain, shift, w_own, w_other):
    return pl.pallas_call(
        bias_kernel,
        grid_spec=pltpu.PrefetchScalarGridSpec(
            num_scalar_prefetch=1,
            grid=(1,),
            in_specs=[pl.BlockSpec((ROWS, N, C), lambda g, w: (0, 0, 0))] * 2
            + [pl.BlockSpec((1, C), lambda g, w: (0, 0))] * 2
            + [pl.BlockSpec((16, C), lambda g, w: (0, 0))] * 2,
            out_specs=pl.BlockSpec((2 * PIECE, C), lambda g, w: (0, 0)),
            scratch_shapes=[pltpu.VMEM((N, C), F32), pltpu.VMEM((2 * PIECE, C), F32)],
        ),
        out_shape=jax.ShapeDtypeStruct((2 * PIECE, C), BF16),
        compiler_params=params(24),
        cost_estimate=pl.CostEstimate(flops=40 * N * ROWS * C, bytes_accessed=4 * ROWS * N * C, transcendentals=0),
        name="bias",
    )(where, own, other, gain, shift, w_own, w_other)


def place_kernel(where_ref, gain_ref, shift_ref, w_own_ref, w_other_ref, *refs):
    parts, out_ref, held = refs[:4], refs[4], refs[5]
    y, xl, z = where_ref[2], where_ref[3], where_ref[4]
    turn = lax.rem(z + 4, 8)
    reaches = [bias_range(w_ref[...], gain_ref[...], shift_ref[...])[1] for w_ref in (w_own_ref, w_other_ref)]
    scale = [jnp.broadcast_to(reach[g : g + 1] * ROOT, (8, QR)) for reach in reaches for g in range(2)]
    scale = jnp.concatenate(scale, axis=1)
    for step, part in enumerate(parts):
        source = lax.rem(y - step + 4, 4)
        held[...] = decode(part[...])
        for step_x in range(2):
            from_x = lax.rem(xl + step_x, 2)
            for other in range(2):
                for a in range(ROWS):
                    to = (other * ROWS + a) * CHIPS + from_x * 32 + source * 8
                    to = pl.multiple_of(to, 8)
                    for s in range(6):
                        at = step_x * 16 * PIECE + other * PIECE + a * 6 + s
                        lanes = slice(s * C, (s + 1) * C)
                        ring = held[pl.ds(at, 8, stride=2 * PIECE), :]
                        out_ref[pl.ds(to, 8), lanes] = pltpu.roll(ring, turn, 0) * scale[:, lanes]


def place_bias(where, gain, shift, w_own, w_other, parts):
    return pl.pallas_call(
        place_kernel,
        grid_spec=pltpu.PrefetchScalarGridSpec(
            num_scalar_prefetch=1,
            grid=(1,),
            in_specs=[pl.BlockSpec((1, C), lambda g, w: (0, 0))] * 2
            + [pl.BlockSpec((16, C), lambda g, w: (0, 0))] * 2
            + [pl.BlockSpec((32 * PIECE, C), lambda g, w: (0, 0))] * 4,
            out_specs=pl.BlockSpec((N, 4 * QR), lambda g, w: (0, 0)),
            scratch_shapes=[pltpu.VMEM((32 * PIECE, C), F32)],
        ),
        out_shape=jax.ShapeDtypeStruct((N, 4 * QR), F32),
        compiler_params=params(32),
        cost_estimate=pl.CostEstimate(flops=20 * N * N, bytes_accessed=8 * N * N, transcendentals=0),
        name="place",
    )(where, gain, shift, w_own, w_other, *parts)


def gather_z(x):
    def shift(value, by):
        return lax.ppermute(value, "z", [(i, (i + by) % 8) for i in range(8)])

    low, high = shift(x, 1), shift(x, -1)
    far_low = shift(jnp.stack([low, x, high]), 3)
    far_high = shift(jnp.stack([low, x]), -3)
    return jnp.concatenate([far_low, low[None], x[None], high[None], far_high], axis=0)


def attend_kernel(
    where_ref, own_ref, other_ref, query_ref, bias_ref, wk_ref, wv_ref, wq_ref, wg_ref, wo_ref, out_ref
):
    head_of_channel = lax.broadcasted_iota(jnp.int32, (C, 2 * QR), 0) // DH
    second = (lax.broadcasted_iota(jnp.int32, (C, 2 * QR), 1) >= QR).astype(jnp.int32)
    first = lax.broadcasted_iota(jnp.int32, (DH, 2 * QR), 1) < QR
    factor = 1.0 / (ROOT * math.log(2.0))

    def project(m):
        entries = jnp.concatenate([own_ref[m], other_ref[m]], axis=0)
        asked = jnp.concatenate([query_ref[m], query_ref[m]], axis=0)
        keys = jnp.dot(entries, wk_ref[...], preferred_element_type=F32).astype(BF16)
        values = lax.dot_general(wv_ref[...], entries, NT, preferred_element_type=F32).astype(BF16)
        queries = lax.dot_general(wq_ref[...], asked, NT, preferred_element_type=F32)
        gates = jax.nn.sigmoid(lax.dot_general(wg_ref[...], asked, NT, preferred_element_type=F32))
        masked = [jnp.where(head_of_channel == 2 * g + second, queries, 0.0).astype(BF16) for g in range(2)]
        return keys, values, jnp.concatenate(masked, axis=1), gates.astype(BF16).astype(F32)

    projected = [project(m) for m in range(GROUP)]

    def score(m):
        keys, _, masked, _ = projected[m]
        return jnp.dot(keys, masked, preferred_element_type=F32) + bias_ref[...]

    def finish(m, scores):
        _, values, _, gates = projected[m]
        highest = jnp.max(scores, axis=0, keepdims=True)
        exponent = jnp.exp2((scores - highest) * factor)
        totals = jnp.sum(exponent, axis=0, keepdims=True)
        sums = jnp.dot(values, exponent.astype(BF16), preferred_element_type=F32)
        gated = []
        for g in range(2):
            lanes = slice(g * 2 * QR, (g + 1) * 2 * QR)
            low, high = slice(2 * g * DH, (2 * g + 1) * DH), slice((2 * g + 1) * DH, (2 * g + 2) * DH)
            attended = jnp.where(first, sums[low, lanes], sums[high, lanes]) / totals[:, lanes]
            gated.append(attended * jnp.where(first, gates[low], gates[high]))
        turned = jnp.concatenate(gated, axis=0).T.astype(BF16)
        turned = jnp.concatenate([turned[:QR], turned[QR:]], axis=1)
        out_ref[m] = jnp.dot(turned, wo_ref[...], preferred_element_type=F32).astype(BF16)

    scores = score(0)
    for m in range(GROUP):
        following = score(m + 1) if m + 1 < GROUP else None
        finish(m, scores)
        scores = following


def attend(where, own, other, bias, wk, wv, wq, wg, wo):
    weight = pl.BlockSpec((C, C), lambda m, w: (0, 0))
    return pl.pallas_call(
        attend_kernel,
        grid_spec=pltpu.PrefetchScalarGridSpec(
            num_scalar_prefetch=1,
            grid=(COLS // GROUP,),
            in_specs=[
                pl.BlockSpec((GROUP, KH, C), lambda m, w: (m, 0, 0)),
                pl.BlockSpec((GROUP, KH, C), lambda m, w: (m, 0, 0)),
                pl.BlockSpec((GROUP, QR, C), lambda m, w: (m, w[0], 0)),
                pl.BlockSpec((N, 4 * QR), lambda m, w: (0, 0)),
            ]
            + [weight] * 5,
            out_specs=pl.BlockSpec((GROUP, QR, C), lambda m, w: (m, 0, 0)),
        ),
        out_shape=jax.ShapeDtypeStruct((COLS, QR, C), BF16),
        compiler_params=params(48),
        cost_estimate=pl.CostEstimate(
            flops=COLS * 8 * N * N * C, bytes_accessed=12 * N * N, transcendentals=COLS * N * N
        ),
        name="attend",
    )(where, own, other, own, bias, wk, wv, wq, wg, wo)


def local(pair, ln_gain, ln_shift, w_project, w_bias, w_out):
    swap_heads = functools.partial(lax.ppermute, axis_name="h", perm=[(0, 1), (1, 0)])
    swap_cores = functools.partial(lax.ppermute, axis_name="c", perm=[(0, 1), (1, 0)])
    where = [lax.axis_index(name) for name in ("h", "c", "y", "xl", "z")]
    where = jnp.stack(where).astype(jnp.int32)
    gain, shift = ln_gain.reshape(1, C), ln_shift.reshape(1, C)

    rows = normalize(pair, gain, shift)
    blocks = rows.reshape(ROWS, CHIPS, COLS, C).transpose(1, 0, 2, 3).reshape(CHIPS, ROWS * COLS, C)
    arrived = lax.all_to_all(blocks, CHIP, 0, 0, tiled=True)
    own = arrived.reshape(CHIPS, ROWS, COLS, C).transpose(2, 1, 0, 3).reshape(COLS, KH, C)
    other = swap_cores(own)

    weights = jnp.concatenate([w_project.reshape(C, 4 * 64), w_out.T], axis=1)
    weights_other = swap_heads(weights)
    full = [
        jnp.concatenate([weights[:, t * 64 : (t + 1) * 64], weights_other[:, t * 64 : (t + 1) * 64]], axis=1)
        for t in range(5)
    ]
    wo = full[4].T.reshape(2, 2, DH, C).transpose(1, 0, 2, 3).reshape(C, C)
    full = (full[1], full[2].T, full[0].T, full[3].T, wo)

    w_own = jnp.pad(w_bias.T, ((0, 14), (0, 0)))
    w_other = swap_heads(w_own)
    piece = bias_piece(where, pair, swap_cores(pair), gain, shift, w_own, w_other)
    ring = gather_z(piece)
    near = jnp.concatenate([ring, lax.ppermute(ring, "xl", [(0, 1), (1, 0)])], axis=0)
    near, *full = lax.optimization_barrier((near, *full))
    parts = [near] + [lax.ppermute(near, "y", [(i, (i + o) % 4) for i in range(4)]) for o in (1, 2, 3)]
    parts = [part.reshape(32 * PIECE, C) for part in parts]
    bias = place_bias(where, gain, shift, w_own, w_other, parts)

    done = attend(where, own, other, bias, *full)

    sent = done.reshape(COLS, 3, CHIPS, C).transpose(2, 1, 0, 3).reshape(CHIPS, 3 * COLS, C)
    returned = lax.all_to_all(sent, CHIP, 0, 0, tiled=True)
    return returned.reshape(CHIPS, 3, COLS, C).transpose(1, 0, 2, 3).reshape(3, N, C)


def solution(mesh):
    fine = Mesh(mesh.devices.reshape(2, 4, 8, 2, 2), DAP + ("h",))
    in_specs = (P(DAP, None, None), P(), P(), P(None, None, "h"), P(None, "h"), P("h", None))
    out_specs = P(DAP + ("h",), None, None)
    return jax.shard_map(local, mesh=fine, in_specs=in_specs, out_specs=out_specs, check_vma=False)
```

time: 174 us -> 135 us (0.78)
  waiting for transfers between devices: 71.4 us -> 37.4 us
  Pallas kernels: 32.8 us -> 24.4 us
  starting transfers between devices: 26.2 us -> 33.4 us
  local copies, waits for them, and re-layouts: 12.9 us -> 8.92 us
    all_to_all x1, waiting for transfers between devices: 26.3 us -> 0.01 us  [local(): arrived = lax.all_to_all(blocks, CHIP, 0, 0, tiled=True)]
    ppermute x1 -> x7, waiting for transfers between devices: 3.12 us -> 20.7 us  [the longest x4 14.8 us: shift(): return lax.ppermute(value, 'z', [(i, (i + by) % 8) for i in range(8)])]
    ppermute x3, waiting for transfers between devices: 26.8 us -> 11.4 us  [local(): lax.ppermute(near, 'y', [(i, (i + o) % 4) for i in range(4)])]
    all_to_all x1 -> x0, waiting for transfers between devices: 15.2 us -> none  [local(): near = lax.all_to_all(spread, ('xl', 'z', 'c'), 0, 0, tiled=True)]
    ppermute x1 -> x7, starting transfers between devices: 2.21 us -> 12.5 us  [the longest x4 9.69 us: shift(): return lax.ppermute(value, 'z', [(i, (i + by) % 8) for i in range(8)])]
    pallas_call x1, Pallas kernels: 27.6 us -> 17.8 us  [attend(): pl.pallas_call(attend_kernel, grid_spec=pltpu.PrefetchScalarGridSpec(num_...]
    ppermute x1, waiting for transfers between devices: 0.01 us -> 5.33 us  [local(): weights_other = swap_heads(weights)]
    all_to_all x1 -> x0, starting transfers between devices: 4.36 us -> none  [local(): near = lax.all_to_all(spread, ('xl', 'z', 'c'), 0, 0, tiled=True)]
  transfers between devices with their start and end apart: 8 -> 13, of which waited for: 6 -> 6; matrix products, arithmetic and copies ran while one was open for 1% -> 1% of each run, Pallas kernels for 2% -> 4%
where the time goes in v2:
time: 135 us
  waiting for transfers between devices  37.4 us (28%)
  starting transfers between devices  33.4 us (25%)
  blocking collectives  30.6 us (23%)
  Pallas kernels  24.4 us (18%)
  local copies, waits for them, and re-layouts  8.92 us (7%)
    all_to_all x1, blocking collectives, local(): returned = lax.all_to_all(sent, CHIP, 0, 0, tiled=True)  30.6 us
    pallas_call x1, Pallas kernels, attend(): pl.pallas_call(attend_kernel, grid_spec=pltpu.PrefetchScalarGridSpec(num_...  17.8 us
    ppermute x4, waiting for transfers between devices, shift(): return lax.ppermute(value, 'z', [(i, (i + by) % 8) for i in range(8)])  14.8 us
    all_to_all x1, starting transfers between devices, local(): arrived = lax.all_to_all(blocks, CHIP, 0, 0, tiled=True)  13.5 us
    ppermute x3, waiting for transfers between devices, local(): lax.ppermute(near, 'y', [(i, (i + o) % 4) for i in range(4)])  11.4 us
    ppermute x4, starting transfers between devices, shift(): return lax.ppermute(value, 'z', [(i, (i + by) % 8) for i in range(8)])  9.69 us
    ppermute x1, waiting for transfers between devices, local(): lax.ppermute(ring, 'xl', [(0, 1), (1, 0)])  5.82 us
    ppermute x3, starting transfers between devices, local(): lax.ppermute(near, 'y', [(i, (i + o) % 4) for i in range(4)])  5.78 us
  transfers between devices with their start and end apart: 13, of which 6 were waited for; matrix products, arithmetic and copies ran while one was open for 1% of the time, Pallas kernels for 4%

profile of v2, /device:TPU:2, one launch (start us, length us, event | category | flops | bytes accessed | tf_op | source)
XLA Modules:
  0.0 135.0 jit_solution(9685548213305651569)
XLA Ops:
  0.0 0.0 copy-start
  0.0 1.3 copy-done
  1.3 0.0 copy-start.2
  1.3 0.7 copy-done.2
  1.9 0.0 copy-start.4
  1.9 0.7 copy-done.4
  2.6 1.8 %norm.1 = bf16[6,768,128]{2,1,0:T(8,128)(2,1)S(1)} custom-call(bf16[6,768,128]{2,1,0:T(8,128)(2,1)S(1)} %copy-done, f32[1,128]{1,0:T(1,128)S(1)} %bitcast.59, f32[1,128]{1,0:T(1,128)S(1)} %bitcast.62), custom_call_target="tpu_custom_call" | custom-call | flops 5898240 | bytes 2359296 | tf_op jit(solution)/shard_map/norm/pallas_call | solution.py:43
  4.4 0.3 reshape.53
  4.7 0.3 copy.15
  5.0 1.8 %copy.16 = bf16[64,72,128]{2,1,0:T(8,128)(2,1)} copy(bf16[64,72,128]{2,0,1:T(8,128)(2,1)S(1)} %bitcast.67) | data formatting | bytes 2359296 | tf_op jit(solution)/shard_map/reshape | solution.py:257
  6.8 0.0 copy-start.1
  6.8 0.0 copy-start.8
  6.8 0.0 copy-start.6
  6.8 0.0 copy-start.7
  6.8 0.0 copy-start.3
  6.8 0.0 copy-start.5
  6.8 13.5 %all-to-all-start = ((bf16[64,72,128]{2,1,0:T(8,128)(2,1)}), bf16[64,72,128]{2,1,0:T(8,128)(2,1)}, u32[]{:S(2)}, u32[]{:S(2)}) async-start(bf16[64,72,128]{2,1,0:T(8,128)(2,1)} %copy.16), calls=%async_computation | async-start | bytes 2359296 | tf_op jit(solution)/shard_map/all_to_all | solution.py:258
  20.4 0.0 copy-done.1
  20.4 0.1 collective-permute-start.2
  20.5 0.0 copy-done.8
  20.5 2.2 %collective-permute-start.1 = (bf16[16,128]{1,0:T(8,128)(2,1)S(1)}, bf16[16,128]{1,0:T(8,128)(2,1)S(1)}, u32[]{:S(2)}, u32[]{:S(2)}) collective-permute-start(bf16[16,128]{1,0:T(8,128)(2,1)S(1)} %pad.4.w_own_ref), channel_id=1, source_target_pairs={{0,1},{1,0},{2,3},{3,2},{4,5},{5,4},{6,7},{7,6},{8,9},{9,8},{10,11... | collective-permute-start | bytes 12296 | tf_op jit(solution)/shard_map/ppermute | solution.py:272
  22.7 0.0 copy-done.6
  22.7 0.0 copy-done.7
  22.7 1.5 %collective-permute-start.8 = (bf16[128,320]{0,1:T(8,128)(2,1)S(1)}, bf16[128,320]{0,1:T(8,128)(2,1)S(1)}, u32[]{:S(2)}, u32[]{:S(2)}) collective-permute-start(bf16[128,320]{0,1:T(8,128)(2,1)S(1)} %pad_maximum_fusion), channel_id=1, source_target_pairs={{0,1},{1,0},{2,3},{3,2},{4,5},{5,4},{6,7},{7,6},{8,9},{9,8},{10,11... | collective-permute-start | bytes 245768 | tf_op jit(solution)/shard_map/ppermute | solution.py:263
  24.2 0.1 stack.40.where_ref
  24.3 5.3 %collective-permute-done.8 = bf16[128,320]{0,1:T(8,128)(2,1)S(1)} collective-permute-done((bf16[128,320]{0,1:T(8,128)(2,1)S(1)}, bf16[128,320]{0,1:T(8,128)(2,1)S(1)}, u32[]{:S(2)}, u32[]{:S(2)}) %collective-permute-start.8) | collective-permute-done | bytes 81952 | tf_op jit(solution)/shard_map/ppermute | solution.py:263
  29.6 0.0 collective-permute-done.1.w_other_ref
  29.6 0.0 collective-permute-done.2.other_ref
  29.7 0.0 copy-done.3
  29.7 0.0 copy-done.5
  29.7 2.1 %bias.1 = bf16[72,128]{1,0:T(8,128)(2,1)S(1)} custom-call(s32[5]{0:T(128)S(1)} %stack.40.where_ref, bf16[6,768,128]{2,1,0:T(8,128)(2,1)S(1)} %copy-done.1, bf16[6,768,128]{2,1,0:T(8,128)(2,1)S(1)} %collective-permute-done.2.other_ref, f32[1,128]{1,0:T(1,128)S(1)} %bitcast.60, f32[1,128]{1,0:T(1,128)S(1)} %bitcast.63, bf16[16,128]{1,0:T(8,128)(2,1)S(1)} %pad.4.w_own_ref, ...), custom_call_target="tpu_custom_call" | custom-call | flops 23592960 | bytes 2359296 | tf_op jit(solution)/shard_map/bias/pallas_call | solution.py:107
  31.8 1.5 %collective-permute-start.3 = (bf16[72,128]{1,0:T(8,128)(2,1)S(1)}, bf16[72,128]{1,0:T(8,128)(2,1)S(1)}, u32[]{:S(2)}, u32[]{:S(2)}) collective-permute-start(bf16[72,128]{1,0:T(8,128)(2,1)S(1)} %bias.1), channel_id=1, source_target_pairs={{0,4},{4,8},{8,12},{12,16},{16,20},{20,24},{24,28},{28,0},{1,5},{5... | collective-permute-start | bytes 55304 | tf_op jit(solution)/shard_map/ppermute | solution.py:169
  33.3 3.0 %collective-permute-start.4 = (bf16[72,128]{1,0:T(8,128)(2,1)S(1)}, bf16[72,128]{1,0:T(8,128)(2,1)S(1)}, u32[]{:S(2)}, u32[]{:S(2)}) collective-permute-start(bf16[72,128]{1,0:T(8,128)(2,1)S(1)} %bias.1), channel_id=1, source_target_pairs={{0,28},{4,0},{8,4},{12,8},{16,12},{20,16},{24,20},{28,24},{1,29},{... | collective-permute-start | bytes 55304 | tf_op jit(solution)/shard_map/ppermute | solution.py:169
  36.3 11.8 %collective-permute-done.3 = bf16[72,128]{1,0:T(8,128)(2,1)S(1)} collective-permute-done((bf16[72,128]{1,0:T(8,128)(2,1)S(1)}, bf16[72,128]{1,0:T(8,128)(2,1)S(1)}, u32[]{:S(2)}, u32[]{:S(2)}) %collective-permute-start.3) | collective-permute-done | bytes 18464 | tf_op jit(solution)/shard_map/ppermute | solution.py:169
  48.2 0.0 collective-permute-done.4
  48.2 3.6 %collective-permute-start.5 = (bf16[3,72,128]{2,1,0:T(8,128)(2,1)S(1)}, bf16[3,72,128]{2,1,0:T(8,128)(2,1)S(1)}, u32[]{:S(2)}, u32[]{:S(2)}) collective-permute-start(bf16[3,72,128]{2,1,0:T(8,128)(2,1)S(1)} %pad_maximum_fusion.1), channel_id=1, source_target_pairs={{0,12},{4,16},{8,20},{12,24},{16,28},{20,0},{24,4},{28,8},{1,13},{... | collective-permute-start | bytes 165896 | tf_op jit(solution)/shard_map/ppermute | solution.py:169
  51.8 1.5 %collective-permute-start.6 = (bf16[2,72,128]{2,1,0:T(8,128)(2,1)S(1)}, bf16[2,72,128]{2,1,0:T(8,128)(2,1)S(1)}, u32[]{:S(2)}, u32[]{:S(2)}) collective-permute-start(bf16[2,72,128]{2,1,0:T(8,128)(2,1)S(1)} %pad_maximum_fusion.2), channel_id=1, source_target_pairs={{0,20},{4,24},{8,28},{12,0},{16,4},{20,8},{24,12},{28,16},{1,21},{... | collective-permute-start | bytes 110600 | tf_op jit(solution)/shard_map/ppermute | solution.py:169
  53.3 3.0 %collective-permute-done.5 = bf16[3,72,128]{2,1,0:T(8,128)(2,1)S(1)} collective-permute-done((bf16[3,72,128]{2,1,0:T(8,128)(2,1)S(1)}, bf16[3,72,128]{2,1,0:T(8,128)(2,1)S(1)}, u32[]{:S(2)}, u32[]{:S(2)}) %collective-permute-start.5) | collective-permute-done | bytes 55328 | tf_op jit(solution)/shard_map/ppermute | solution.py:169
  56.3 0.0 all-to-all-done
  56.3 1.6 %copy.17 = bf16[64,72,128]{2,0,1:T(8,128)(2,1)S(1)} copy(bf16[64,72,128]{2,1,0:T(8,128)(2,1)} %all-to-all-done) | data formatting | bytes 2359296 | tf_op jit(solution)/shard_map/all_to_all | solution.py:258
  57.9 0.1 copy.18
  58.0 0.1 collective-permute-start
  58.2 0.0 collective-permute-done.6
  58.2 0.5 collective-permute-start.7
  58.7 5.8 %collective-permute-done.7 = bf16[8,72,128]{2,1,0:T(8,128)(2,1)S(1)} collective-permute-done((bf16[8,72,128]{2,1,0:T(8,128)(2,1)S(1)}, bf16[8,72,128]{2,1,0:T(8,128)(2,1)S(1)}, u32[]{:S(2)}, u32[]{:S(2)}) %collective-permute-start.7) | collective-permute-done | bytes 147488 | tf_op jit(solution)/shard_map/ppermute | solution.py:275
  64.6 1.6 %collective-permute-start.9 = (bf16[16,72,128]{2,1,0:T(8,128)(2,1)S(1)}, bf16[16,72,128]{2,1,0:T(8,128)(2,1)S(1)}, u32[]{:S(2)}, u32[]{:S(2)}) collective-permute-start(bf16[16,72,128]{2,1,0:T(8,128)(2,1)S(1)} %constant_dynamic-update-slice_fusion.5), channel_id=1, source_target_pairs={{0,32},{32,64},{64,96},{96,0},{1,33},{33,65},{65,97},{97,1},{2,34}... | collective-permute-start | bytes 884744 | tf_op jit(solution)/shard_map/ppermute | solution.py:277
  66.2 2.8 %collective-permute-start.10 = (bf16[16,72,128]{2,1,0:T(8,128)(2,1)S(1)}, bf16[16,72,128]{2,1,0:T(8,128)(2,1)S(1)}, u32[]{:S(2)}, u32[]{:S(2)}) collective-permute-start(bf16[16,72,128]{2,1,0:T(8,128)(2,1)S(1)} %constant_dynamic-update-slice_fusion.5), channel_id=1, source_target_pairs={{0,64},{32,96},{64,0},{96,32},{1,65},{33,97},{65,1},{97,33},{2,66}... | collective-permute-start | bytes 884744 | tf_op jit(solution)/shard_map/ppermute | solution.py:277
  68.9 1.4 %collective-permute-start.11 = (bf16[16,72,128]{2,1,0:T(8,128)(2,1)S(1)}, bf16[16,72,128]{2,1,0:T(8,128)(2,1)S(1)}, u32[]{:S(2)}, u32[]{:S(2)}) collective-permute-start(bf16[16,72,128]{2,1,0:T(8,128)(2,1)S(1)} %constant_dynamic-update-slice_fusion.5), channel_id=1, source_target_pairs={{0,96},{32,0},{64,32},{96,64},{1,97},{33,1},{65,33},{97,65},{2,98}... | collective-permute-start | bytes 884744 | tf_op jit(solution)/shard_map/ppermute | solution.py:277
  70.3 0.1 copy.20.wk_ref
  70.5 4.2 %collective-permute-done.9 = bf16[16,72,128]{2,1,0:T(8,128)(2,1)S(1)} collective-permute-done((bf16[16,72,128]{2,1,0:T(8,128)(2,1)S(1)}, bf16[16,72,128]{2,1,0:T(8,128)(2,1)S(1)}, u32[]{:S(2)}, u32[]{:S(2)}) %collective-permute-start.9) | collective-permute-done | bytes 294944 | tf_op jit(solution)/shard_map/ppermute | solution.py:277
  74.7 7.2 %collective-permute-done.10 = bf16[16,72,128]{2,1,0:T(8,128)(2,1)S(1)} collective-permute-done((bf16[16,72,128]{2,1,0:T(8,128)(2,1)S(1)}, bf16[16,72,128]{2,1,0:T(8,128)(2,1)S(1)}, u32[]{:S(2)}, u32[]{:S(2)}) %collective-permute-start.10) | collective-permute-done | bytes 294944 | tf_op jit(solution)/shard_map/ppermute | solution.py:277
  81.8 0.0 collective-permute-done.11
  81.9 2.7 %place.1.bias_ref = f32[768,768]{1,0:T(8,128)S(1)} custom-call(s32[5]{0:T(128)S(1)} %stack.40.where_ref, f32[1,128]{1,0:T(1,128)S(1)} %bitcast.61, f32[1,128]{1,0:T(1,128)S(1)} %bitcast.64, bf16[16,128]{1,0:T(8,128)(2,1)S(1)} %pad.4.w_own_ref, bf16[16,128]{1,0:T(8,128)(2,1)S(1)} %collective-permute-done.1.w_other_ref, bf16[1152,128]{1,0:T(8,128)(2,1)S(1)} %bitcast.52, ...), custom_call_target="tpu_custom_call" | custom-call | flops 11796480 | bytes 4718592 | tf_op jit(solution)/shard_map/place/pallas_call | solution.py:149
  84.6 0.0 collective-permute-done.other_ref
  84.6 17.8 %attend.1 = bf16[12,192,128]{2,1,0:T(8,128)(2,1)S(1)} custom-call(s32[5]{0:T(128)S(1)} %stack.40.where_ref, bf16[12,384,128]{2,1,0:T(8,128)(2,1)S(1)} %bitcast.49, bf16[12,384,128]{2,1,0:T(8,128)(2,1)} %collective-permute-done.other_ref, bf16[12,384,128]{2,1,0:T(8,128)(2,1)S(1)} %bitcast.50, f32[768,768]{1,0:T(8,128)S(1)} %place.1.bias_ref, ...), custom_call_target="tpu_custom_call" | custom-call | flops 7247757312 | bytes 7077888 | tf_op jit(solution)/shard_map/attend/pallas_call | solution.py:226
  102.5 0.4 copy.22
  102.9 30.6 %all_to_all.10 = bf16[64,36,128]{2,1,0:T(8,128)(2,1)S(1)} all-to-all(bf16[64,36,128]{2,1,0:T(8,128)(2,1)S(1)} %copy.22), channel_id=1, replica_groups=mesh['xl'=2,'y'=4,'z'=8,'c'=2,'h'=2] {'xl','y','z'}, dimensions={0} | all-to-all | bytes 1179648 | tf_op jit(solution)/shard_map/all_to_all | solution.py:284
  133.5 0.1 copy.23
  133.6 0.4 copy.24
  134.1 1.0 reshape.67
  (17 shorter events, 0.2 us)
Async XLA Ops:
  0.0 1.3 copy-start
  1.3 0.7 copy-start.2
  1.9 0.7 copy-start.4
  6.8 13.6 %copy-start.1 = (bf16[6,768,128]{2,1,0:T(8,128)(2,1)S(1)}, bf16[6,768,128]{2,1,0:T(8,128)(2,1)}, u32[]{:S(2)}) copy-start(bf16[6,768,128]{2,1,0:T(8,128)(2,1)} %own_ref.1) | copy-start | bytes 3538948
  6.8 13.7 %copy-start.8 = (bf16[128,2]{0,1:T(2,128)(2,1)S(1)}, bf16[128,2]{0,1:T(2,128)(2,1)}, u32[]{:S(2)}) copy-start(bf16[128,2]{0,1:T(2,128)(2,1)} %param.10) | copy-start | bytes 1540
  6.8 15.9 %copy-start.6 = (bf16[128,4,64]{0,2,1:T(8,128)(2,1)S(1)}, bf16[128,4,64]{0,2,1:T(8,128)(2,1)}, u32[]{:S(2)}) copy-start(bf16[128,4,64]{0,2,1:T(8,128)(2,1)} %param.9) | copy-start | bytes 196612
  6.8 15.9 %copy-start.7 = (bf16[64,128]{1,0:T(8,128)(2,1)S(1)}, bf16[64,128]{1,0:T(8,128)(2,1)}, u32[]{:S(2)}) copy-start(bf16[64,128]{1,0:T(8,128)(2,1)} %param.11) | copy-start | bytes 49156
  6.8 22.9 %copy-start.3 = (f32[128]{0:T(128)S(1)}, f32[128]{0:T(128)}, u32[]{:S(2)}) copy-start(f32[128]{0:T(128)} %param.7) | copy-start | bytes 1540
  6.8 22.8 %copy-start.5 = (f32[128]{0:T(128)S(1)}, f32[128]{0:T(128)}, u32[]{:S(2)}) copy-start(f32[128]{0:T(128)} %param.8) | copy-start | bytes 1540
  6.8 49.5 %all-to-all-start = ((bf16[64,72,128]{2,1,0:T(8,128)(2,1)}), bf16[64,72,128]{2,1,0:T(8,128)(2,1)}, u32[]{:S(2)}, u32[]{:S(2)}) async-start(bf16[64,72,128]{2,1,0:T(8,128)(2,1)} %copy.16), calls=%async_computation | async-start | bytes 2359296 | tf_op jit(solution)/shard_map/all_to_all | solution.py:258
  20.4 9.3 %collective-permute-start.2 = (bf16[6,768,128]{2,1,0:T(8,128)(2,1)S(1)}, bf16[6,768,128]{2,1,0:T(8,128)(2,1)S(1)}, u32[]{:S(2)}, u32[]{:S(2)}) collective-permute-start(bf16[6,768,128]{2,1,0:T(8,128)(2,1)S(1)} %copy-done.1), channel_id=1, source_target_pairs={{0,2},{2,0},{1,3},{3,1},{4,6},{6,4},{5,7},{7,5},{8,10},{10,8},{9,1... | collective-permute-start | bytes 3538952 | tf_op jit(solution)/shard_map/ppermute | solution.py:273
  20.5 9.1 %collective-permute-start.1 = (bf16[16,128]{1,0:T(8,128)(2,1)S(1)}, bf16[16,128]{1,0:T(8,128)(2,1)S(1)}, u32[]{:S(2)}, u32[]{:S(2)}) collective-permute-start(bf16[16,128]{1,0:T(8,128)(2,1)S(1)} %pad.4.w_own_ref), channel_id=1, source_target_pairs={{0,1},{1,0},{2,3},{3,2},{4,5},{5,4},{6,7},{7,6},{8,9},{9,8},{10,11... | collective-permute-start | bytes 12296 | tf_op jit(solution)/shard_map/ppermute | solution.py:272
  22.7 6.9 %collective-permute-start.8 = (bf16[128,320]{0,1:T(8,128)(2,1)S(1)}, bf16[128,320]{0,1:T(8,128)(2,1)S(1)}, u32[]{:S(2)}, u32[]{:S(2)}) collective-permute-start(bf16[128,320]{0,1:T(8,128)(2,1)S(1)} %pad_maximum_fusion), channel_id=1, source_target_pairs={{0,1},{1,0},{2,3},{3,2},{4,5},{5,4},{6,7},{7,6},{8,9},{9,8},{10,11... | collective-permute-start | bytes 245768 | tf_op jit(solution)/shard_map/ppermute | solution.py:263
  31.8 16.4 %collective-permute-start.3 = (bf16[72,128]{1,0:T(8,128)(2,1)S(1)}, bf16[72,128]{1,0:T(8,128)(2,1)S(1)}, u32[]{:S(2)}, u32[]{:S(2)}) collective-permute-start(bf16[72,128]{1,0:T(8,128)(2,1)S(1)} %bias.1), channel_id=1, source_target_pairs={{0,4},{4,8},{8,12},{12,16},{16,20},{20,24},{24,28},{28,0},{1,5},{5... | collective-permute-start | bytes 55304 | tf_op jit(solution)/shard_map/ppermute | solution.py:169
  33.3 14.9 %collective-permute-start.4 = (bf16[72,128]{1,0:T(8,128)(2,1)S(1)}, bf16[72,128]{1,0:T(8,128)(2,1)S(1)}, u32[]{:S(2)}, u32[]{:S(2)}) collective-permute-start(bf16[72,128]{1,0:T(8,128)(2,1)S(1)} %bias.1), channel_id=1, source_target_pairs={{0,28},{4,0},{8,4},{12,8},{16,12},{20,16},{24,20},{28,24},{1,29},{... | collective-permute-start | bytes 55304 | tf_op jit(solution)/shard_map/ppermute | solution.py:169
  48.2 8.1 %collective-permute-start.5 = (bf16[3,72,128]{2,1,0:T(8,128)(2,1)S(1)}, bf16[3,72,128]{2,1,0:T(8,128)(2,1)S(1)}, u32[]{:S(2)}, u32[]{:S(2)}) collective-permute-start(bf16[3,72,128]{2,1,0:T(8,128)(2,1)S(1)} %pad_maximum_fusion.1), channel_id=1, source_target_pairs={{0,12},{4,16},{8,20},{12,24},{16,28},{20,0},{24,4},{28,8},{1,13},{... | collective-permute-start | bytes 165896 | tf_op jit(solution)/shard_map/ppermute | solution.py:169
  51.8 6.4 %collective-permute-start.6 = (bf16[2,72,128]{2,1,0:T(8,128)(2,1)S(1)}, bf16[2,72,128]{2,1,0:T(8,128)(2,1)S(1)}, u32[]{:S(2)}, u32[]{:S(2)}) collective-permute-start(bf16[2,72,128]{2,1,0:T(8,128)(2,1)S(1)} %pad_maximum_fusion.2), channel_id=1, source_target_pairs={{0,20},{4,24},{8,28},{12,0},{16,4},{20,8},{24,12},{28,16},{1,21},{... | collective-permute-start | bytes 110600 | tf_op jit(solution)/shard_map/ppermute | solution.py:169
  58.0 26.6 %collective-permute-start = (bf16[12,384,128]{2,1,0:T(8,128)(2,1)S(1)}, bf16[12,384,128]{2,1,0:T(8,128)(2,1)}, u32[]{:S(2)}, u32[]{:S(2)}) collective-permute-start(bf16[12,384,128]{2,1,0:T(8,128)(2,1)S(1)} %bitcast.48), channel_id=1, source_target_pairs={{0,2},{2,0},{1,3},{3,1},{4,6},{6,4},{5,7},{7,5},{8,10},{10,8},{9,1... | collective-permute-start | bytes 3538952 | tf_op jit(solution)/shard_map/ppermute | solution.py:260
  58.2 6.3 %collective-permute-start.7 = (bf16[8,72,128]{2,1,0:T(8,128)(2,1)S(1)}, bf16[8,72,128]{2,1,0:T(8,128)(2,1)S(1)}, u32[]{:S(2)}, u32[]{:S(2)}) collective-permute-start(bf16[8,72,128]{2,1,0:T(8,128)(2,1)S(1)} %get-tuple-element.28), channel_id=1, source_target_pairs={{0,128},{128,0},{1,129},{129,1},{2,130},{130,2},{3,131},{131,3},{4... | collective-permute-start | bytes 442376 | tf_op jit(solution)/shard_map/ppermute | solution.py:275
  64.6 10.1 %collective-permute-start.9 = (bf16[16,72,128]{2,1,0:T(8,128)(2,1)S(1)}, bf16[16,72,128]{2,1,0:T(8,128)(2,1)S(1)}, u32[]{:S(2)}, u32[]{:S(2)}) collective-permute-start(bf16[16,72,128]{2,1,0:T(8,128)(2,1)S(1)} %constant_dynamic-update-slice_fusion.5), channel_id=1, source_target_pairs={{0,32},{32,64},{64,96},{96,0},{1,33},{33,65},{65,97},{97,1},{2,34}... | collective-permute-start | bytes 884744 | tf_op jit(solution)/shard_map/ppermute | solution.py:277
  66.2 15.7 %collective-permute-start.10 = (bf16[16,72,128]{2,1,0:T(8,128)(2,1)S(1)}, bf16[16,72,128]{2,1,0:T(8,128)(2,1)S(1)}, u32[]{:S(2)}, u32[]{:S(2)}) collective-permute-start(bf16[16,72,128]{2,1,0:T(8,128)(2,1)S(1)} %constant_dynamic-update-slice_fusion.5), channel_id=1, source_target_pairs={{0,64},{32,96},{64,0},{96,32},{1,65},{33,97},{65,1},{97,33},{2,66}... | collective-permute-start | bytes 884744 | tf_op jit(solution)/shard_map/ppermute | solution.py:277
  68.9 12.9 %collective-permute-start.11 = (bf16[16,72,128]{2,1,0:T(8,128)(2,1)S(1)}, bf16[16,72,128]{2,1,0:T(8,128)(2,1)S(1)}, u32[]{:S(2)}, u32[]{:S(2)}) collective-permute-start(bf16[16,72,128]{2,1,0:T(8,128)(2,1)S(1)} %constant_dynamic-update-slice_fusion.5), channel_id=1, source_target_pairs={{0,96},{32,0},{64,32},{96,64},{1,97},{33,1},{65,33},{97,65},{2,98}... | collective-permute-start | bytes 884744 | tf_op jit(solution)/shard_map/ppermute | solution.py:277

commit v3 on v2

v3 whole, which is shorter than its diff:
```python
import functools
import math

import jax
import jax.numpy as jnp
from jax import lax
from jax.experimental import pallas as pl
from jax.experimental.pallas import tpu as pltpu
from jax.sharding import Mesh
from jax.sharding import PartitionSpec as P

F32 = jnp.float32
BF16 = jnp.bfloat16
CHIP = ("xl", "y", "z")
DAP = ("xl", "y", "z", "c")
N, C, H, DH = 768, 128, 4, 32
CHIPS, COLS, ROWS = 64, 12, 6
QR = 3 * CHIPS
KH = ROWS * CHIPS
LEVELS = 240
GROUP = 6
SHARE = 18
LAID = 3 * COLS
MESSAGE = 56
ROOT = math.sqrt(DH)
NT = (((1,), (1,)), ((), ()))


def params(mb):
    return pltpu.CompilerParams(vmem_limit_bytes=mb * 2**20)


def layer_norm(x, gain, shift):
    average = jnp.mean(x, axis=-1, keepdims=True)
    centred = x - average
    variance = jnp.mean(centred * centred, axis=-1, keepdims=True)
    return centred * lax.rsqrt(variance + 1e-05) * gain + shift


def bias_range(w, gain, shift):
    w = w.astype(F32)
    middle = jnp.sum(w * shift, axis=1, keepdims=True)
    reach = jnp.sqrt(C * jnp.sum(w * w * gain * gain, axis=1, keepdims=True))
    rounded = jnp.sum(jnp.abs(w * shift), axis=1, keepdims=True)
    return middle, reach * (1 + 1 / 256) + rounded / 256 + 1e-20


def encode(x):
    size = jnp.minimum(jnp.abs(x) * LEVELS, LEVELS - 0.01)
    whole = jnp.floor(size)
    code = jnp.exp2(whole - LEVELS / 2) * (1 + (size - whole))
    return jnp.where(x < 0, -code, code)


def decode(code):
    code = code.astype(F32)
    size = jnp.abs(code)
    whole = jnp.floor(jnp.log2(size))
    x = (whole + (LEVELS / 2 - 1) + size * jnp.exp2(-whole)) / LEVELS
    return jnp.where(code < 0, -x, x)


def lay_kernel(where_ref, own_ref, norm_ref, out_ref, picked_ref, normed, held):
    h = where_ref[0]
    first = 6 * where_ref[1] + 3 * h
    gain, shift = norm_ref[0:1], norm_ref[1:2]
    for r in range(3):
        rows = layer_norm(own_ref[3 * h + r].astype(F32), gain, shift)
        normed[r * N : (r + 1) * N, :] = rows.astype(BF16).astype(F32)
        for q in range(3):
            got = normed[pl.ds(r * N + first + q, CHIPS, stride=COLS), :]
            picked_ref[r, q * CHIPS : (q + 1) * CHIPS, :] = got.astype(BF16)
    for r in range(3):
        held[...] = own_ref[3 * (1 - h) + r].astype(F32)
        got = [held[pl.ds(first + q, CHIPS, stride=COLS), :] for q in range(3)]
        picked_ref[3 + r] = layer_norm(jnp.concatenate(got, axis=0), gain, shift).astype(BF16)
    for p in range(CHIPS):
        for r in range(3):
            to = (p * 3 + r) * COLS
            out_ref[to : to + COLS, :] = normed[r * N + p * COLS : r * N + (p + 1) * COLS, :]


def lay_out(where, pair, norm):
    return pl.pallas_call(
        lay_kernel,
        grid_spec=pltpu.PrefetchScalarGridSpec(
            num_scalar_prefetch=1,
            grid=(1,),
            in_specs=[
                pl.BlockSpec((ROWS, N, C), lambda g, w: (0, 0, 0)),
                pl.BlockSpec((2, C), lambda g, w: (0, 0)),
            ],
            out_specs=[
                pl.BlockSpec((3 * N, C), lambda g, w: (0, 0)),
                pl.BlockSpec((ROWS, QR, C), lambda g, w: (0, 0, 0)),
            ],
            scratch_shapes=[pltpu.VMEM((3 * N, C), F32), pltpu.VMEM((N, C), F32)],
        ),
        out_shape=[
            jax.ShapeDtypeStruct((3 * N, C), F32),
            jax.ShapeDtypeStruct((ROWS, QR, C), BF16),
        ],
        compiler_params=params(24),
        cost_estimate=pl.CostEstimate(flops=20 * N * ROWS * C, bytes_accessed=6 * ROWS * N * C, transcendentals=0),
        name="lay",
    )(where, pair, norm)


def pack_kernel(
    where_ref, laid_ref, picked_ref, other_ref, norm_ref, w_own_ref, w_other_ref, out_ref, held, coded, tail
):
    h = where_ref[0]
    first = 6 * where_ref[1] + 3 * h
    gain, shift = norm_ref[0:1], norm_ref[1:2]
    weights = [w_ref[...] for w_ref in (w_own_ref, w_other_ref)]
    ranges = [bias_range(w, gain, shift) for w in weights]

    def code_row(at, entries):
        parts = [
            (lax.dot_general(w, entries, NT, preferred_element_type=F32) - middle) / reach
            for w, (middle, reach) in zip(weights, ranges)
        ]
        row = jnp.concatenate([part[g : g + 1] for part in parts for g in range(2)], axis=1)
        for s in range(6):
            coded[at * 6 + s : at * 6 + s + 1, :] = row[:, s * C : (s + 1) * C]

    for half in range(2):
        for r in range(3):
            code_row(half * 6 + r, picked_ref[half * 3 + r])
            held[...] = other_ref[3 * (h if half == 0 else 1 - h) + r].astype(F32)
            got = [held[pl.ds(first + q, CHIPS, stride=COLS), :] for q in range(3)]
            entries = layer_norm(jnp.concatenate(got, axis=0), gain, shift).astype(BF16)
            code_row(half * 6 + 3 + r, entries)
    coded[...] = encode(coded[...])
    for p in range(CHIPS):
        y = p // 8 % 4
        tail[p * 24 : p * 24 + 4, :] = laid_ref[p * LAID + 32 : (p + 1) * LAID, :]
        tail[p * 24 + 4 : p * 24 + 4 + SHARE, :] = coded[y * SHARE : (y + 1) * SHARE, :]
        tail[p * 24 + 4 + SHARE : (p + 1) * 24, :] = jnp.zeros((20 - SHARE, C), F32)
    for p in range(CHIPS):
        out_ref[p, :32, :] = laid_ref[p * LAID : p * LAID + 32, :].astype(BF16)
        out_ref[p, 32:, :] = tail[p * 24 : (p + 1) * 24, :].astype(BF16)


def pack(where, laid, picked, other, norm, w_own, w_other):
    return pl.pallas_call(
        pack_kernel,
        grid_spec=pltpu.PrefetchScalarGridSpec(
            num_scalar_prefetch=1,
            grid=(1,),
            in_specs=[
                pl.BlockSpec((3 * N, C), lambda g, w: (0, 0)),
                pl.BlockSpec((ROWS, QR, C), lambda g, w: (0, 0, 0)),
                pl.BlockSpec((ROWS, N, C), lambda g, w: (0, 0, 0)),
                pl.BlockSpec((2, C), lambda g, w: (0, 0)),
                pl.BlockSpec((16, C), lambda g, w: (0, 0)),
                pl.BlockSpec((16, C), lambda g, w: (0, 0)),
            ],
            out_specs=pl.BlockSpec((CHIPS, MESSAGE, C), lambda g, w: (0, 0, 0)),
            scratch_shapes=[
                pltpu.VMEM((N, C), F32),
                pltpu.VMEM((4 * SHARE, C), F32),
                pltpu.VMEM((CHIPS * 24, C), F32),
            ],
        ),
        out_shape=jax.ShapeDtypeStruct((CHIPS, MESSAGE, C), BF16),
        compiler_params=params(24),
        cost_estimate=pl.CostEstimate(flops=60 * N * ROWS * C, bytes_accessed=6 * ROWS * N * C, transcendentals=0),
        name="pack",
    )(where, laid, picked, other, norm, w_own, w_other)


def unpack_kernel(arrived_ref, share_ref, column_ref, held):
    held[...] = arrived_ref[...].astype(F32).reshape(CHIPS * MESSAGE, C)
    for j in range(SHARE):
        got = held[pl.ds(LAID + j, CHIPS, stride=MESSAGE), :]
        share_ref[j * CHIPS : (j + 1) * CHIPS, :] = got.astype(BF16)
    for m in range(COLS):
        for r in range(3):
            got = held[pl.ds(r * COLS + m, CHIPS, stride=MESSAGE), :]
            column_ref[m, r * CHIPS : (r + 1) * CHIPS, :] = got.astype(BF16)


def unpack(arrived):
    return pl.pallas_call(
        unpack_kernel,
        out_shape=[
            jax.ShapeDtypeStruct((SHARE * CHIPS, C), BF16),
            jax.ShapeDtypeStruct((COLS, QR, C), BF16),
        ],
        scratch_shapes=[pltpu.VMEM((CHIPS * MESSAGE, C), F32)],
        compiler_params=params(24),
        cost_estimate=pl.CostEstimate(flops=CHIPS * MESSAGE * C, bytes_accessed=8 * CHIPS * MESSAGE * C, transcendentals=0),
        name="unpack",
    )(arrived)


def place_kernel(where_ref, norm_ref, w_own_ref, w_other_ref, part_ref, *refs):
    out_ref = refs[-1]
    reaches = [bias_range(w_ref[...], norm_ref[0:1], norm_ref[1:2])[1] for w_ref in (w_own_ref, w_other_ref)]
    scale = [jnp.broadcast_to(reach[g : g + 1] * ROOT, (8, QR)) for reach in reaches for g in range(2)]
    scale = jnp.concatenate(scale, axis=1)[:1]
    for a in range(3):
        for s in range(6):
            lanes = slice(s * C, (s + 1) * C)
            at = (a * 6 + s) * CHIPS
            out_ref[a * CHIPS : (a + 1) * CHIPS, lanes] = decode(part_ref[at : at + CHIPS, :]) * scale[:, lanes]


def place_bias(where, norm, w_own, w_other, part, step, bias):
    small = lambda g, w: (0, 0)
    in_specs = [
        pl.BlockSpec((2, C), small),
        pl.BlockSpec((16, C), small),
        pl.BlockSpec((16, C), small),
        pl.BlockSpec((SHARE * CHIPS, C), small),
    ]
    operands = [where, norm, w_own, w_other, part]
    aliases = {}
    if bias is not None:
        in_specs.append(pl.BlockSpec(memory_space=pl.ANY))
        operands.append(bias)
        aliases = {5: 0}
    return pl.pallas_call(
        place_kernel,
        grid_spec=pltpu.PrefetchScalarGridSpec(
            num_scalar_prefetch=1,
            grid=(1,),
            in_specs=in_specs,
            out_specs=pl.BlockSpec((QR, 4 * QR), lambda g, w: (lax.rem(w[2] - step + 4, 4), 0)),
        ),
        out_shape=jax.ShapeDtypeStruct((N, 4 * QR), F32),
        input_output_aliases=aliases,
        compiler_params=params(16),
        cost_estimate=pl.CostEstimate(flops=5 * N * N, bytes_accessed=2 * N * N, transcendentals=0),
        name="place",
    )(*operands)


def project_kernel(own_ref, other_ref, wk_ref, wv_ref, keys_ref, values_ref):
    for m in range(GROUP):
        entries = jnp.concatenate([own_ref[m], other_ref[m]], axis=0)
        keys_ref[m] = jnp.dot(entries, wk_ref[...], preferred_element_type=F32).astype(BF16)
        values_ref[m] = lax.dot_general(wv_ref[...], entries, NT, preferred_element_type=F32).astype(BF16)


def project(own, other, wk, wv):
    block = pl.BlockSpec((GROUP, QR, C), lambda m: (m, 0, 0))
    weight = pl.BlockSpec((C, C), lambda m: (0, 0))
    shapes = [(2 * QR, C), (C, 2 * QR)]
    return pl.pallas_call(
        project_kernel,
        grid=(COLS // GROUP,),
        in_specs=[block, block, weight, weight],
        out_specs=[pl.BlockSpec((GROUP,) + shape, lambda m: (m, 0, 0)) for shape in shapes],
        out_shape=[jax.ShapeDtypeStruct((COLS,) + shape, BF16) for shape in shapes],
        compiler_params=params(16),
        cost_estimate=pl.CostEstimate(flops=COLS * 2 * N * C * C, bytes_accessed=10 * N * N, transcendentals=0),
        name="project",
    )(own, other, wk, wv)


def ask_kernel(own_ref, wq_ref, wg_ref, masked_ref, gates_ref):
    head_of_channel = lax.broadcasted_iota(jnp.int32, (C, 2 * QR), 0) // DH
    second = (lax.broadcasted_iota(jnp.int32, (C, 2 * QR), 1) >= QR).astype(jnp.int32)
    first = lax.broadcasted_iota(jnp.int32, (DH, 2 * QR), 1) < QR
    for m in range(GROUP):
        asked = jnp.concatenate([own_ref[m], own_ref[m]], axis=0)
        queries = lax.dot_general(wq_ref[...], asked, NT, preferred_element_type=F32)
        gates = jax.nn.sigmoid(lax.dot_general(wg_ref[...], asked, NT, preferred_element_type=F32))
        for g in range(2):
            lanes = slice(g * 2 * QR, (g + 1) * 2 * QR)
            low, high = slice(2 * g * DH, (2 * g + 1) * DH), slice((2 * g + 1) * DH, (2 * g + 2) * DH)
            masked_ref[m, :, lanes] = jnp.where(head_of_channel == 2 * g + second, queries, 0.0).astype(BF16)
            gates_ref[m, g * DH : (g + 1) * DH, :] = jnp.where(first, gates[low], gates[high]).astype(BF16)


def ask(own, wq, wg):
    weight = pl.BlockSpec((C, C), lambda m: (0, 0))
    shapes = [(C, 4 * QR), (2 * DH, 2 * QR)]
    return pl.pallas_call(
        ask_kernel,
        grid=(COLS // GROUP,),
        in_specs=[pl.BlockSpec((GROUP, QR, C), lambda m: (m, 0, 0)), weight, weight],
        out_specs=[pl.BlockSpec((GROUP,) + shape, lambda m: (m, 0, 0)) for shape in shapes],
        out_shape=[jax.ShapeDtypeStruct((COLS,) + shape, BF16) for shape in shapes],
        compiler_params=params(16),
        cost_estimate=pl.CostEstimate(flops=COLS * 2 * N * C * C, bytes_accessed=10 * N * N, transcendentals=0),
        name="ask",
    )(own, wq, wg)


def attend_kernel(k0_ref, v0_ref, k1_ref, v1_ref, masked_ref, gates_ref, bias_ref, wo_ref, out_ref):
    first = lax.broadcasted_iota(jnp.int32, (DH, 2 * QR), 1) < QR
    factor = 1.0 / (ROOT * math.log(2.0))

    def score(m):
        keys = jnp.concatenate([k0_ref[m], k1_ref[m]], axis=0)
        return jnp.dot(keys, masked_ref[m], preferred_element_type=F32) + bias_ref[...]

    def soften(m, scores):
        highest = jnp.max(scores, axis=0, keepdims=True)
        exponent = jnp.exp2((scores - highest) * factor)
        totals = jnp.sum(exponent, axis=0, keepdims=True)
        values = jnp.concatenate([v0_ref[m], v1_ref[m]], axis=1)
        return jnp.dot(values, exponent.astype(BF16), preferred_element_type=F32), totals

    def finish(m, sums, totals):
        gated = []
        for g in range(2):
            lanes = slice(g * 2 * QR, (g + 1) * 2 * QR)
            low, high = slice(2 * g * DH, (2 * g + 1) * DH), slice((2 * g + 1) * DH, (2 * g + 2) * DH)
            attended = jnp.where(first, sums[low, lanes], sums[high, lanes]) / totals[:, lanes]
            gated.append(attended * gates_ref[m, g * DH : (g + 1) * DH, :].astype(F32))
        turned = jnp.concatenate(gated, axis=0).T.astype(BF16)
        turned = jnp.concatenate([turned[:QR], turned[QR:]], axis=1)
        out_ref[m] = jnp.dot(turned, wo_ref[...], preferred_element_type=F32).astype(BF16)

    attended = []
    scores = score(0)
    for m in range(GROUP):
        following = score(m + 1) if m + 1 < GROUP else None
        attended.append(soften(m, scores))
        scores = following
    for m in range(GROUP):
        finish(m, *attended[m])


def attend(k0, v0, k1, v1, masked, gates, bias, wo):
    shapes = [(2 * QR, C), (C, 2 * QR)] * 2 + [(C, 4 * QR), (2 * DH, 2 * QR)]
    return pl.pallas_call(
        attend_kernel,
        grid=(COLS // GROUP,),
        in_specs=[pl.BlockSpec((GROUP,) + shape, lambda m: (m, 0, 0)) for shape in shapes]
        + [pl.BlockSpec((N, 4 * QR), lambda m: (0, 0)), pl.BlockSpec((C, C), lambda m: (0, 0))],
        out_specs=pl.BlockSpec((GROUP, QR, C), lambda m: (m, 0, 0)),
        out_shape=jax.ShapeDtypeStruct((COLS, QR, C), BF16),
        compiler_params=params(40),
        cost_estimate=pl.CostEstimate(
            flops=COLS * 8 * N * N * C, bytes_accessed=12 * N * N, transcendentals=COLS * N * N
        ),
        name="attend",
    )(k0, v0, k1, v1, masked, gates, bias, wo)


def local(pair, ln_gain, ln_shift, w_project, w_bias, w_out):
    swap_heads = functools.partial(lax.ppermute, axis_name="h", perm=[(0, 1), (1, 0)])
    swap_cores = functools.partial(lax.ppermute, axis_name="c", perm=[(0, 1), (1, 0)])
    where = [lax.axis_index(name) for name in ("h", "c", "y", "xl", "z")]
    where = jnp.stack(where).astype(jnp.int32)
    norm = jnp.stack([ln_gain, ln_shift])

    w_own = jnp.pad(w_bias.T, ((0, 14), (0, 0)))
    w_other = swap_heads(w_own)
    laid, picked = lay_out(where, pair, norm)
    blocks = pack(where, laid, picked, swap_cores(pair), norm, w_own, w_other)
    arrived = lax.all_to_all(blocks, CHIP, 0, 0, tiled=True)
    weights = jnp.concatenate([w_project.reshape(C, 4 * 64), w_out.T], axis=1)
    weights_other = swap_heads(weights)
    full = [
        jnp.concatenate([weights[:, t * 64 : (t + 1) * 64], weights_other[:, t * 64 : (t + 1) * 64]], axis=1)
        for t in range(5)
    ]
    wo = full[4].T.reshape(2, 2, DH, C).transpose(1, 0, 2, 3).reshape(C, C)
    full = (full[1], full[2].T, full[0].T, full[3].T, wo)
    arrived, *full = lax.optimization_barrier((arrived, *full))

    wk, wv, wq, wg, wo = full
    share, own = unpack(arrived)
    far = swap_heads(own)
    parts = [share] + [lax.ppermute(share, "y", [(i, (i + o) % 4) for i in range(4)]) for o in (1, 2, 3)]
    masked, gates = ask(own, wq, wg)
    k0, v0 = project(own, swap_cores(own), wk, wv)
    bias = place_bias(where, norm, w_own, w_other, share, 0, None)
    waited = (far, *parts, masked, gates, k0, v0, bias)
    far, *parts, masked, gates, k0, v0, bias = lax.optimization_barrier(waited)
    k1, v1 = project(far, swap_cores(far), wk, wv)
    for step in (3, 2, 1):
        bias = place_bias(where, norm, w_own, w_other, parts[step], step, bias)
    done = attend(k0, v0, k1, v1, masked, gates, bias, wo)

    sent = done.reshape(COLS, 3, CHIPS, C).transpose(2, 1, 0, 3).reshape(CHIPS, 3 * COLS, C)
    returned = lax.all_to_all(sent, CHIP, 0, 0, tiled=True)
    return returned.reshape(CHIPS, 3, COLS, C).transpose(1, 0, 2, 3).reshape(3, N, C)


def solution(mesh):
    fine = Mesh(mesh.devices.reshape(2, 4, 8, 2, 2), DAP + ("h",))
    in_specs = (P(DAP, None, None), P(), P(), P(None, None, "h"), P(None, "h"), P("h", None))
    out_specs = P(DAP + ("h",), None, None)
    return jax.shard_map(local, mesh=fine, in_specs=in_specs, out_specs=out_specs, check_vma=False)
```

time: 135 us -> 115 us (0.85)
  starting transfers between devices: 33.4 us -> 21.9 us
  local copies, waits for them, and re-layouts: 8.92 us -> 4.07 us
  Pallas kernels: 24.4 us -> 22.6 us
  blocking collectives: 30.6 us -> 28.9 us
    ppermute x10 -> x7, waiting for transfers between devices: 32 us -> 10.6 us  [the longest x3 10.6 us: local(): lax.ppermute(share, 'y', [(i, (i + o) % 4) for i in range(4)])]
    all_to_all x1, waiting for transfers between devices: 0.01 us -> 20.4 us  [local(): arrived = lax.all_to_all(blocks, CHIP, 0, 0, tiled=True)]
    ppermute x10 -> x7, starting transfers between devices: 16.1 us -> 4.89 us  [the longest x3 3.29 us: local(): lax.ppermute(share, 'y', [(i, (i + o) % 4) for i in range(4)])]
    pallas_call x3 -> x7, Pallas kernels: 21.7 us -> 19.3 us  [the longest x1 10.9 us: attend(): pl.pallas_call(attend_kernel, grid=(COLS // GROUP,), in_specs=[pl.BlockSp...]
    reshape x2 -> x0, local copies, waits for them, and re-layouts: 2.1 us -> none  [local(): rows.reshape(ROWS, CHIPS, COLS, C).transpose(1, 0, 2, 3)]
    all_to_all x1, blocking collectives: 30.6 us -> 28.9 us  [local(): returned = lax.all_to_all(sent, CHIP, 0, 0, tiled=True)]
    all_to_all x1 -> x0, local copies, waits for them, and re-layouts: 1.56 us -> none  [local(): arrived = lax.all_to_all(blocks, CHIP, 0, 0, tiled=True)]
    unnamed x22 -> x6, local copies, waits for them, and re-layouts: 2.66 us -> 1.28 us
  transfers between devices with their start and end apart: 13 -> 10, of which waited for: 6 -> 4; matrix products, arithmetic and copies ran while one was open for 1% -> 1% of each run, Pallas kernels for 4% -> 6%
where the time goes in v3:
time: 115 us
  waiting for transfers between devices  36.2 us (31%)
  blocking collectives  28.9 us (25%)
  Pallas kernels  22.6 us (20%)
  starting transfers between devices  21.9 us (19%)
  local copies, waits for them, and re-layouts  4.07 us (4%)
    all_to_all x1, blocking collectives, local(): returned = lax.all_to_all(sent, CHIP, 0, 0, tiled=True)  28.9 us
    all_to_all x1, waiting for transfers between devices, local(): arrived = lax.all_to_all(blocks, CHIP, 0, 0, tiled=True)  20.4 us
    all_to_all x1, starting transfers between devices, local(): arrived = lax.all_to_all(blocks, CHIP, 0, 0, tiled=True)  13.3 us
    pallas_call x1, Pallas kernels, attend(): pl.pallas_call(attend_kernel, grid=(COLS // GROUP,), in_specs=[pl.BlockSp...  10.9 us
    ppermute x3, waiting for transfers between devices, local(): lax.ppermute(share, 'y', [(i, (i + o) % 4) for i in range(4)])  10.6 us
    ppermute x1, waiting for transfers between devices, local(): weights_other = swap_heads(weights)  5.21 us
    pallas_call x4, Pallas kernels, place_bias(): pl.pallas_call(place_kernel, grid_spec=pltpu.PrefetchScalarGridSpec(num_s...  3.37 us
    ppermute x3, starting transfers between devices, local(): lax.ppermute(share, 'y', [(i, (i + o) % 4) for i in range(4)])  3.29 us
  transfers between devices with their start and end apart: 10, of which 4 were waited for; matrix products, arithmetic and copies ran while one was open for 1% of the time, Pallas kernels for 6%

profile of v3, /device:TPU:2, one launch (start us, length us, event | category | flops | bytes accessed | tf_op | source)
XLA Modules:
  0.0 114.6 jit_solution(13507578009607963986)
XLA Ops:
  0.0 0.0 collective-permute-start
  0.0 0.7 pad.4.w_own_ref
  0.7 2.1 %collective-permute-start.1 = (bf16[16,128]{1,0:T(8,128)(2,1)S(1)}, bf16[16,128]{1,0:T(8,128)(2,1)S(1)}, u32[]{:S(2)}, u32[]{:S(2)}) collective-permute-start(bf16[16,128]{1,0:T(8,128)(2,1)S(1)} %pad.4.w_own_ref), channel_id=1, source_target_pairs={{0,1},{1,0},{2,3},{3,2},{4,5},{5,4},{6,7},{7,6},{8,9},{9,8},{10,11... | collective-permute-start | bytes 12296 | tf_op jit(solution)/shard_map/ppermute | solution.py:354
  2.8 0.7 pad_maximum_fusion.3.norm_ref
  3.5 0.1 stack.32.where_ref
  3.6 0.0 copy-start
  3.6 1.3 %copy-done = bf16[6,768,128]{2,1,0:T(8,128)(2,1)S(1)} copy-done((bf16[6,768,128]{2,1,0:T(8,128)(2,1)S(1)}, bf16[6,768,128]{2,1,0:T(8,128)(2,1)}, u32[]{:S(2)}) %copy-start) | copy-done | bytes 1179672
  4.8 1.6 %lay.1 = (f32[2304,128]{1,0:T(8,128)S(1)}, bf16[6,192,128]{2,1,0:T(8,128)(2,1)S(1)}) custom-call(s32[5]{0:T(128)S(1)} %stack.32.where_ref, bf16[6,768,128]{2,1,0:T(8,128)(2,1)S(1)} %copy-done, f32[2,128]{1,0:T(2,128)S(1)} %pad_maximum_fusion.3.norm_ref), custom_call_target="tpu_custom_call" | custom-call | flops 11796480 | bytes 3538944 | tf_op jit(solution)/shard_map/lay/pallas_call | solution.py:84
  6.5 0.0 collective-permute-done.1.w_other_ref
  6.5 0.0 collective-permute-done.other_ref
  6.5 2.9 %pack.1 = bf16[64,56,128]{2,1,0:T(8,128)(2,1)} custom-call(s32[5]{0:T(128)S(1)} %stack.32.where_ref, f32[2304,128]{1,0:T(8,128)S(1)} %get-tuple-element.30.laid_ref, bf16[6,192,128]{2,1,0:T(8,128)(2,1)S(1)} %get-tuple-element.31.picked_ref, bf16[6,768,128]{2,1,0:T(8,128)(2,1)S(1)} %collective-permute-done.other_ref, ...), custom_call_target="tpu_custom_call" | custom-call | flops 35389440 | bytes 3538944 | tf_op jit(solution)/shard_map/pack/pallas_call | solution.py:146
  9.4 0.0 copy-start.1
  9.4 0.0 copy-start.2
  9.4 13.3 %all-to-all-start = ((bf16[64,56,128]{2,1,0:T(8,128)(2,1)}), bf16[64,56,128]{2,1,0:T(8,128)(2,1)S(1)}, u32[]{:S(2)}, u32[]{:S(2)}) async-start(bf16[64,56,128]{2,1,0:T(8,128)(2,1)} %pack.1), calls=%async_computation | async-start | bytes 1835008 | tf_op jit(solution)/shard_map/all_to_all | solution.py:357
  22.7 0.0 copy-done.1
  22.7 0.0 copy-done.2
  22.8 1.5 %collective-permute-start.2 = (bf16[128,320]{0,1:T(8,128)(2,1)S(1)}, bf16[128,320]{0,1:T(8,128)(2,1)S(1)}, u32[]{:S(2)}, u32[]{:S(2)}) collective-permute-start(bf16[128,320]{0,1:T(8,128)(2,1)S(1)} %pad_maximum_fusion), channel_id=1, source_target_pairs={{0,1},{1,0},{2,3},{3,2},{4,5},{5,4},{6,7},{7,6},{8,9},{9,8},{10,11... | collective-permute-start | bytes 245768 | tf_op jit(solution)/shard_map/ppermute | solution.py:359
  24.3 5.2 %collective-permute-done.2 = bf16[128,320]{0,1:T(8,128)(2,1)S(1)} collective-permute-done((bf16[128,320]{0,1:T(8,128)(2,1)S(1)}, bf16[128,320]{0,1:T(8,128)(2,1)S(1)}, u32[]{:S(2)}, u32[]{:S(2)}) %collective-permute-start.2) | collective-permute-done | bytes 81952 | tf_op jit(solution)/shard_map/ppermute | solution.py:359
  29.5 20.4 %all-to-all-done.arrived_ref = bf16[64,56,128]{2,1,0:T(8,128)(2,1)S(1)} async-done(((bf16[64,56,128]{2,1,0:T(8,128)(2,1)}), bf16[64,56,128]{2,1,0:T(8,128)(2,1)S(1)}, u32[]{:S(2)}, u32[]{:S(2)}) %all-to-all-start) | async-done | bytes 917536 | tf_op jit(solution)/shard_map/all_to_all | solution.py:357
  49.9 0.4 unpack.1
  50.3 0.1 collective-permute-start.7
  50.4 1.5 %collective-permute-start.3 = (bf16[12,192,128]{2,1,0:T(8,128)(2,1)S(1)}, bf16[12,192,128]{2,1,0:T(8,128)(2,1)S(1)}, u32[]{:S(2)}, u32[]{:S(2)}) collective-permute-start(bf16[12,192,128]{2,1,0:T(8,128)(2,1)S(1)} %get-tuple-element.33.own_ref), channel_id=1, source_target_pairs={{0,1},{1,0},{2,3},{3,2},{4,5},{5,4},{6,7},{7,6},{8,9},{9,8},{10,11... | collective-permute-start | bytes 1769480 | tf_op jit(solution)/shard_map/ppermute | solution.py:370
  51.9 0.6 collective-permute-start.4
  52.5 1.6 %collective-permute-start.5 = (bf16[1152,128]{1,0:T(8,128)(2,1)S(1)}, bf16[1152,128]{1,0:T(8,128)(2,1)S(1)}, u32[]{:S(2)}, u32[]{:S(2)}) collective-permute-start(bf16[1152,128]{1,0:T(8,128)(2,1)S(1)} %get-tuple-element.34.part_ref), channel_id=1, source_target_pairs={{0,64},{32,96},{64,0},{96,32},{1,65},{33,97},{65,1},{97,33},{2,66}... | collective-permute-start | bytes 884744 | tf_op jit(solution)/shard_map/ppermute | solution.py:371
  54.2 1.0 collective-permute-start.6
  55.2 0.1 copy.19.wk_ref
  55.3 0.8 place.4.refs_0_
  56.2 1.3 %ask.1 = (bf16[12,128,768]{2,1,0:T(8,128)(2,1)S(1)}, bf16[12,64,384]{2,1,0:T(8,128)(2,1)S(1)}) custom-call(bf16[12,192,128]{2,1,0:T(8,128)(2,1)S(1)} %get-tuple-element.33.own_ref, bf16[128,128]{1,0:T(8,128)(2,1)S(1)} %get-tuple-element.35.wq_ref, bf16[128,128]{1,0:T(8,128)(2,1)S(1)} %get-tuple-element.36.wg_ref), custom_call_target="tpu_custom_call" | custom-call | flops 301989888 | bytes 5898240 | tf_op jit(solution)/shard_map/ask/pallas_call | solution.py:281
  57.5 0.0 collective-permute-done.7.other_ref
  57.5 1.1 project.2
  58.5 10.0 %collective-permute-done.4.part_ref = bf16[1152,128]{1,0:T(8,128)(2,1)S(1)} collective-permute-done((bf16[1152,128]{1,0:T(8,128)(2,1)S(1)}, bf16[1152,128]{1,0:T(8,128)(2,1)S(1)}, u32[]{:S(2)}, u32[]{:S(2)}) %collective-permute-start.4) | collective-permute-done | bytes 294944 | tf_op jit(solution)/shard_map/ppermute | solution.py:371
  68.5 0.0 collective-permute-done.5.part_ref
  68.5 0.6 collective-permute-done.6.part_ref
  69.1 0.0 collective-permute-done.3.own_ref
  69.1 0.0 collective-permute-start.8
  69.1 0.8 place.5.refs_0_
  70.0 0.8 place.6.refs_0_
  70.8 0.8 place.7.bias_ref
  71.7 0.0 collective-permute-done.8.other_ref
  71.7 1.1 project.3
  72.8 10.9 %attend.1 = bf16[12,192,128]{2,1,0:T(8,128)(2,1)S(1)} custom-call(bf16[12,384,128]{2,1,0:T(8,128)(2,1)S(1)} %get-tuple-element.43.k0_ref, bf16[12,128,384]{2,1,0:T(8,128)(2,1)S(1)} %get-tuple-element.44.v0_ref, bf16[12,384,128]{2,1,0:T(8,128)(2,1)S(1)} %get-tuple-element.46.k1_ref, bf16[12,128,384]{2,1,0:T(8,128)(2,1)S(1)} %get-tuple-element.47.v1_ref, ...), custom_call_target="tpu_custom_call" | custom-call | flops 7247757312 | bytes 7077888 | tf_op jit(solution)/shard_map/attend/pallas_call | solution.py:331
  83.7 0.4 copy.22
  84.1 28.9 %all_to_all.10 = bf16[64,36,128]{2,1,0:T(8,128)(2,1)S(1)} all-to-all(bf16[64,36,128]{2,1,0:T(8,128)(2,1)S(1)} %copy.22), channel_id=1, replica_groups=mesh['xl'=2,'y'=4,'z'=8,'c'=2,'h'=2] {'xl','y','z'}, dimensions={0} | all-to-all | bytes 1179648 | tf_op jit(solution)/shard_map/all_to_all | solution.py:383
  113.1 0.1 copy.23
  113.2 0.4 copy.24
  113.6 1.0 reshape.27
  (8 shorter events, 0.1 us)
Async XLA Ops:
  0.0 6.5 %collective-permute-start = (bf16[6,768,128]{2,1,0:T(8,128)(2,1)}, bf16[6,768,128]{2,1,0:T(8,128)(2,1)S(1)}, u32[]{:S(2)}, u32[]{:S(2)}) collective-permute-start(bf16[6,768,128]{2,1,0:T(8,128)(2,1)} %own_ref.1), channel_id=1, source_target_pairs={{0,2},{2,0},{1,3},{3,1},{4,6},{6,4},{5,7},{7,5},{8,10},{10,8},{9,1... | collective-permute-start | bytes 3538952 | tf_op jit(solution)/shard_map/ppermute | solution.py:356
  0.7 5.8 %collective-permute-start.1 = (bf16[16,128]{1,0:T(8,128)(2,1)S(1)}, bf16[16,128]{1,0:T(8,128)(2,1)S(1)}, u32[]{:S(2)}, u32[]{:S(2)}) collective-permute-start(bf16[16,128]{1,0:T(8,128)(2,1)S(1)} %pad.4.w_own_ref), channel_id=1, source_target_pairs={{0,1},{1,0},{2,3},{3,2},{4,5},{5,4},{6,7},{7,6},{8,9},{9,8},{10,11... | collective-permute-start | bytes 12296 | tf_op jit(solution)/shard_map/ppermute | solution.py:354
  3.6 1.3 %copy-start = (bf16[6,768,128]{2,1,0:T(8,128)(2,1)S(1)}, bf16[6,768,128]{2,1,0:T(8,128)(2,1)}, u32[]{:S(2)}) copy-start(bf16[6,768,128]{2,1,0:T(8,128)(2,1)} %own_ref.1) | copy-start | bytes 3538948
  9.4 13.4 %copy-start.1 = (bf16[128,4,64]{0,2,1:T(8,128)(2,1)S(1)}, bf16[128,4,64]{0,2,1:T(8,128)(2,1)}, u32[]{:S(2)}) copy-start(bf16[128,4,64]{0,2,1:T(8,128)(2,1)} %param.9) | copy-start | bytes 196612
  9.4 13.4 %copy-start.2 = (bf16[64,128]{1,0:T(8,128)(2,1)S(1)}, bf16[64,128]{1,0:T(8,128)(2,1)}, u32[]{:S(2)}) copy-start(bf16[64,128]{1,0:T(8,128)(2,1)} %param.11) | copy-start | bytes 49156
  9.4 40.5 %all-to-all-start = ((bf16[64,56,128]{2,1,0:T(8,128)(2,1)}), bf16[64,56,128]{2,1,0:T(8,128)(2,1)S(1)}, u32[]{:S(2)}, u32[]{:S(2)}) async-start(bf16[64,56,128]{2,1,0:T(8,128)(2,1)} %pack.1), calls=%async_computation | async-start | bytes 1835008 | tf_op jit(solution)/shard_map/all_to_all | solution.py:357
  22.8 6.7 %collective-permute-start.2 = (bf16[128,320]{0,1:T(8,128)(2,1)S(1)}, bf16[128,320]{0,1:T(8,128)(2,1)S(1)}, u32[]{:S(2)}, u32[]{:S(2)}) collective-permute-start(bf16[128,320]{0,1:T(8,128)(2,1)S(1)} %pad_maximum_fusion), channel_id=1, source_target_pairs={{0,1},{1,0},{2,3},{3,2},{4,5},{5,4},{6,7},{7,6},{8,9},{9,8},{10,11... | collective-permute-start | bytes 245768 | tf_op jit(solution)/shard_map/ppermute | solution.py:359
  50.3 7.2 %collective-permute-start.7 = (bf16[12,192,128]{2,1,0:T(8,128)(2,1)S(1)}, bf16[12,192,128]{2,1,0:T(8,128)(2,1)S(1)}, u32[]{:S(2)}, u32[]{:S(2)}) collective-permute-start(bf16[12,192,128]{2,1,0:T(8,128)(2,1)S(1)} %get-tuple-element.33.own_ref), channel_id=1, source_target_pairs={{0,2},{2,0},{1,3},{3,1},{4,6},{6,4},{5,7},{7,5},{8,10},{10,8},{9,1... | collective-permute-start | bytes 1769480 | tf_op jit(solution)/shard_map/ppermute | solution.py:373
  50.4 18.7 %collective-permute-start.3 = (bf16[12,192,128]{2,1,0:T(8,128)(2,1)S(1)}, bf16[12,192,128]{2,1,0:T(8,128)(2,1)S(1)}, u32[]{:S(2)}, u32[]{:S(2)}) collective-permute-start(bf16[12,192,128]{2,1,0:T(8,128)(2,1)S(1)} %get-tuple-element.33.own_ref), channel_id=1, source_target_pairs={{0,1},{1,0},{2,3},{3,2},{4,5},{5,4},{6,7},{7,6},{8,9},{9,8},{10,11... | collective-permute-start | bytes 1769480 | tf_op jit(solution)/shard_map/ppermute | solution.py:370
  51.9 16.6 %collective-permute-start.4 = (bf16[1152,128]{1,0:T(8,128)(2,1)S(1)}, bf16[1152,128]{1,0:T(8,128)(2,1)S(1)}, u32[]{:S(2)}, u32[]{:S(2)}) collective-permute-start(bf16[1152,128]{1,0:T(8,128)(2,1)S(1)} %get-tuple-element.34.part_ref), channel_id=1, source_target_pairs={{0,32},{32,64},{64,96},{96,0},{1,33},{33,65},{65,97},{97,1},{2,34}... | collective-permute-start | bytes 884744 | tf_op jit(solution)/shard_map/ppermute | solution.py:371
  52.5 16.0 %collective-permute-start.5 = (bf16[1152,128]{1,0:T(8,128)(2,1)S(1)}, bf16[1152,128]{1,0:T(8,128)(2,1)S(1)}, u32[]{:S(2)}, u32[]{:S(2)}) collective-permute-start(bf16[1152,128]{1,0:T(8,128)(2,1)S(1)} %get-tuple-element.34.part_ref), channel_id=1, source_target_pairs={{0,64},{32,96},{64,0},{96,32},{1,65},{33,97},{65,1},{97,33},{2,66}... | collective-permute-start | bytes 884744 | tf_op jit(solution)/shard_map/ppermute | solution.py:371
  54.2 14.9 %collective-permute-start.6 = (bf16[1152,128]{1,0:T(8,128)(2,1)S(1)}, bf16[1152,128]{1,0:T(8,128)(2,1)S(1)}, u32[]{:S(2)}, u32[]{:S(2)}) collective-permute-start(bf16[1152,128]{1,0:T(8,128)(2,1)S(1)} %get-tuple-element.34.part_ref), channel_id=1, source_target_pairs={{0,96},{32,0},{64,32},{96,64},{1,97},{33,1},{65,33},{97,65},{2,98}... | collective-permute-start | bytes 884744 | tf_op jit(solution)/shard_map/ppermute | solution.py:371
  69.1 2.6 %collective-permute-start.8 = (bf16[12,192,128]{2,1,0:T(8,128)(2,1)S(1)}, bf16[12,192,128]{2,1,0:T(8,128)(2,1)S(1)}, u32[]{:S(2)}, u32[]{:S(2)}) collective-permute-start(bf16[12,192,128]{2,1,0:T(8,128)(2,1)S(1)} %collective-permute-done.3.own_ref), channel_id=1, source_target_pairs={{0,2},{2,0},{1,3},{3,1},{4,6},{6,4},{5,7},{7,5},{8,10},{10,8},{9,1... | collective-permute-start | bytes 1769480 | tf_op jit(solution)/shard_map/ppermute | solution.py:377

commit v4 on v3

--- a/solution.py
+++ b/solution.py
@@ -24,6 +24,8 @@
 MESSAGE = 56
 ROOT = math.sqrt(DH)
 NT = (((1,), (1,)), ((), ()))
+VMEM = pl.BlockSpec(memory_space=pltpu.VMEM)
+SMEM = pl.BlockSpec(memory_space=pltpu.SMEM)
 
 
 def params(mb):
@@ -43,6 +45,11 @@
     reach = jnp.sqrt(C * jnp.sum(w * w * gain * gain, axis=1, keepdims=True))
     rounded = jnp.sum(jnp.abs(w * shift), axis=1, keepdims=True)
     return middle, reach * (1 + 1 / 256) + rounded / 256 + 1e-20
+
+
+def head_weights(own_ref, other_ref):
+    own, other = own_ref[...].astype(F32), other_ref[...].astype(F32)
+    return jnp.concatenate([own[:2], other[:2], own[4:16]], axis=0)
 
 
 def encode(x):
@@ -69,11 +76,13 @@
         normed[r * N : (r + 1) * N, :] = rows.astype(BF16).astype(F32)
         for q in range(3):
             got = normed[pl.ds(r * N + first + q, CHIPS, stride=COLS), :]
-            picked_ref[r, q * CHIPS : (q + 1) * CHIPS, :] = got.astype(BF16)
+            at = r * QR + q * CHIPS
+            picked_ref[at : at + CHIPS, :] = got.astype(BF16)
     for r in range(3):
         held[...] = own_ref[3 * (1 - h) + r].astype(F32)
         got = [held[pl.ds(first + q, CHIPS, stride=COLS), :] for q in range(3)]
-        picked_ref[3 + r] = layer_norm(jnp.concatenate(got, axis=0), gain, shift).astype(BF16)
+        at = (3 + r) * QR
+        picked_ref[at : at + QR, :] = layer_norm(jnp.concatenate(got, axis=0), gain, shift).astype(BF16)
     for p in range(CHIPS):
         for r in range(3):
             to = (p * 3 + r) * COLS
@@ -83,22 +92,12 @@
 def lay_out(where, pair, norm):
     return pl.pallas_call(
         lay_kernel,
-        grid_spec=pltpu.PrefetchScalarGridSpec(
-            num_scalar_prefetch=1,
-            grid=(1,),
-            in_specs=[
-                pl.BlockSpec((ROWS, N, C), lambda g, w: (0, 0, 0)),
-                pl.BlockSpec((2, C), lambda g, w: (0, 0)),
-            ],
-            out_specs=[
-                pl.BlockSpec((3 * N, C), lambda g, w: (0, 0)),
-                pl.BlockSpec((ROWS, QR, C), lambda g, w: (0, 0, 0)),
-            ],
-            scratch_shapes=[pltpu.VMEM((3 * N, C), F32), pltpu.VMEM((N, C), F32)],
-        ),
+        in_specs=[SMEM, VMEM, VMEM],
+        out_specs=[VMEM, VMEM],
+        scratch_shapes=[pltpu.VMEM((3 * N, C), F32), pltpu.VMEM((N, C), F32)],
         out_shape=[
             jax.ShapeDtypeStruct((3 * N, C), F32),
-            jax.ShapeDtypeStruct((ROWS, QR, C), BF16),
+            jax.ShapeDtypeStruct((ROWS * QR, C), BF16),
         ],
         compiler_params=params(24),
         cost_estimate=pl.CostEstimate(flops=20 * N * ROWS * C, bytes_accessed=6 * ROWS * N * C, transcendentals=0),
@@ -112,26 +111,23 @@
     h = where_ref[0]
     first = 6 * where_ref[1] + 3 * h
     gain, shift = norm_ref[0:1], norm_ref[1:2]
-    weights = [w_ref[...] for w_ref in (w_own_ref, w_other_ref)]
-    ranges = [bias_range(w, gain, shift) for w in weights]
-
-    def code_row(at, entries):
-        parts = [
-            (lax.dot_general(w, entries, NT, preferred_element_type=F32) - middle) / reach
-            for w, (middle, reach) in zip(weights, ranges)
-        ]
-        row = jnp.concatenate([part[g : g + 1] for part in parts for g in range(2)], axis=1)
+    weights = head_weights(w_own_ref, w_other_ref)
+    middle, reach = bias_range(weights, gain, shift)
+    entries = []
+    for half in range(2):
+        entries.append(picked_ref[half * 3 * QR : (half + 1) * 3 * QR, :])
+        for r in range(3):
+            held[...] = other_ref[3 * (h if half == 0 else 1 - h) + r].astype(F32)
+            got = [held[pl.ds(first + q, CHIPS, stride=COLS), :] for q in range(3)]
+            entries.append(layer_norm(jnp.concatenate(got, axis=0), gain, shift).astype(BF16))
+    entries = jnp.concatenate(entries, axis=0)
+    bias = lax.dot_general(weights.astype(BF16), entries, NT, preferred_element_type=F32)
+    codes = encode((bias - middle) / reach)
+    for at in range(2 * ROWS):
+        row = [codes[g : g + 1, at * QR : (at + 1) * QR] for g in range(H)]
+        row = jnp.concatenate(row, axis=1)
         for s in range(6):
             coded[at * 6 + s : at * 6 + s + 1, :] = row[:, s * C : (s + 1) * C]
-
-    for half in range(2):
-        for r in range(3):
-            code_row(half * 6 + r, picked_ref[half * 3 + r])
-            held[...] = other_ref[3 * (h if half == 0 else 1 - h) + r].astype(F32)
-            got = [held[pl.ds(first + q, CHIPS, stride=COLS), :] for q in range(3)]
-            entries = layer_norm(jnp.concatenate(got, axis=0), gain, shift).astype(BF16)
-            code_row(half * 6 + 3 + r, entries)
-    coded[...] = encode(coded[...])
     for p in range(CHIPS):
         y = p // 8 % 4
         tail[p * 24 : p * 24 + 4, :] = laid_ref[p * LAID + 32 : (p + 1) * LAID, :]
@@ -145,24 +141,13 @@
 def pack(where, laid, picked, other, norm, w_own, w_other):
     return pl.pallas_call(
         pack_kernel,
-        grid_spec=pltpu.PrefetchScalarGridSpec(
-            num_scalar_prefetch=1,
-            grid=(1,),
-            in_specs=[
-                pl.BlockSpec((3 * N, C), lambda g, w: (0, 0)),
-                pl.BlockSpec((ROWS, QR, C), lambda g, w: (0, 0, 0)),
-                pl.BlockSpec((ROWS, N, C), lambda g, w: (0, 0, 0)),
-                pl.BlockSpec((2, C), lambda g, w: (0, 0)),
-                pl.BlockSpec((16, C), lambda g, w: (0, 0)),
-                pl.BlockSpec((16, C), lambda g, w: (0, 0)),
-            ],
-            out_specs=pl.BlockSpec((CHIPS, MESSAGE, C), lambda g, w: (0, 0, 0)),
-            scratch_shapes=[
-                pltpu.VMEM((N, C), F32),
-                pltpu.VMEM((4 * SHARE, C), F32),
-                pltpu.VMEM((CHIPS * 24, C), F32),
-            ],
-        ),
+        in_specs=[SMEM] + [VMEM] * 6,
+        out_specs=VMEM,
+        scratch_shapes=[
+            pltpu.VMEM((N, C), F32),
+            pltpu.VMEM((4 * SHARE, C), F32),
+            pltpu.VMEM((CHIPS * 24, C), F32),
+        ],
         out_shape=jax.ShapeDtypeStruct((CHIPS, MESSAGE, C), BF16),
         compiler_params=params(24),
         cost_estimate=pl.CostEstimate(flops=60 * N * ROWS * C, bytes_accessed=6 * ROWS * N * C, transcendentals=0),
@@ -302,15 +287,20 @@
         highest = jnp.max(scores, axis=0, keepdims=True)
         exponent = jnp.exp2((scores - highest) * factor)
         totals = jnp.sum(exponent, axis=0, keepdims=True)
+        weights = exponent.astype(BF16)
         values = jnp.concatenate([v0_ref[m], v1_ref[m]], axis=1)
-        return jnp.dot(values, exponent.astype(BF16), preferred_element_type=F32), totals
+        low = jnp.dot(values[: 2 * DH], weights[:, :256], preferred_element_type=F32)
+        both = jnp.dot(values, weights[:, 256:512], preferred_element_type=F32)
+        high = jnp.dot(values[2 * DH :], weights[:, 512:], preferred_element_type=F32)
+        low = jnp.concatenate([low, both[: 2 * DH, :128]], axis=1)
+        high = jnp.concatenate([both[2 * DH :, 128:], high], axis=1)
+        return (low, high), totals
 
     def finish(m, sums, totals):
         gated = []
         for g in range(2):
             lanes = slice(g * 2 * QR, (g + 1) * 2 * QR)
-            low, high = slice(2 * g * DH, (2 * g + 1) * DH), slice((2 * g + 1) * DH, (2 * g + 2) * DH)
-            attended = jnp.where(first, sums[low, lanes], sums[high, lanes]) / totals[:, lanes]
+            attended = jnp.where(first, sums[g][:DH], sums[g][DH:]) / totals[:, lanes]
             gated.append(attended * gates_ref[m, g * DH : (g + 1) * DH, :].astype(F32))
         turned = jnp.concatenate(gated, axis=0).T.astype(BF16)
         turned = jnp.concatenate([turned[:QR], turned[QR:]], axis=1)
@@ -318,22 +308,19 @@
 
     attended = []
     scores = score(0)
-    for m in range(GROUP):
-        following = score(m + 1) if m + 1 < GROUP else None
+    for m in range(COLS):
+        following = score(m + 1) if m + 1 < COLS else None
         attended.append(soften(m, scores))
         scores = following
-    for m in range(GROUP):
+    for m in range(COLS):
         finish(m, *attended[m])
 
 
 def attend(k0, v0, k1, v1, masked, gates, bias, wo):
-    shapes = [(2 * QR, C), (C, 2 * QR)] * 2 + [(C, 4 * QR), (2 * DH, 2 * QR)]
     return pl.pallas_call(
         attend_kernel,
-        grid=(COLS // GROUP,),
-        in_specs=[pl.BlockSpec((GROUP,) + shape, lambda m: (m, 0, 0)) for shape in shapes]
-        + [pl.BlockSpec((N, 4 * QR), lambda m: (0, 0)), pl.BlockSpec((C, C), lambda m: (0, 0))],
-        out_specs=pl.BlockSpec((GROUP, QR, C), lambda m: (m, 0, 0)),
+        in_specs=[VMEM] * 8,
+        out_specs=VMEM,
         out_shape=jax.ShapeDtypeStruct((COLS, QR, C), BF16),
         compiler_params=params(40),
         cost_estimate=pl.CostEstimate(
@@ -372,14 +359,16 @@
     masked, gates = ask(own, wq, wg)
     k0, v0 = project(own, swap_cores(own), wk, wv)
     bias = place_bias(where, norm, w_own, w_other, share, 0, None)
-    waited = (far, *parts, masked, gates, k0, v0, bias)
-    far, *parts, masked, gates, k0, v0, bias = lax.optimization_barrier(waited)
+    waited = (parts[3], masked, gates, k0, v0, bias)
+    parts[3], masked, gates, k0, v0, bias = lax.optimization_barrier(waited)
+    for step in (3, 2):
+        bias = place_bias(where, norm, w_own, w_other, parts[step], step, bias)
+    far, parts[1], bias = lax.optimization_barrier((far, parts[1], bias))
     k1, v1 = project(far, swap_cores(far), wk, wv)
-    for step in (3, 2, 1):
-        bias = place_bias(where, norm, w_own, w_other, parts[step], step, bias)
+    bias = place_bias(where, norm, w_own, w_other, parts[1], 1, bias)
     done = attend(k0, v0, k1, v1, masked, gates, bias, wo)
 
-    sent = done.reshape(COLS, 3, CHIPS, C).transpose(2, 1, 0, 3).reshape(CHIPS, 3 * COLS, C)
+    sent = done.reshape(COLS, 3, CHIPS, C).transpose(2, 1, 0, 3).reshape(CHIPS, 9, 4, C)
     returned = lax.all_to_all(sent, CHIP, 0, 0, tiled=True)
     return returned.reshape(CHIPS, 3, COLS, C).transpose(1, 0, 2, 3).reshape(3, N, C)
 

time: 115 us -> 111 us (0.965)
  Pallas kernels: 22.6 us -> 21 us
  blocking collectives: 28.9 us -> 27.3 us
    all_to_all x1, blocking collectives: 28.9 us -> 27.3 us  [local(): returned = lax.all_to_all(sent, CHIP, 0, 0, tiled=True)]
    pallas_call x3, Pallas kernels: 15.4 us -> 13.8 us  [the longest x1 9.95 us: attend(): pl.pallas_call(attend_kernel, in_specs=[VMEM] * 8, out_specs=VMEM, out_sh...]
  transfers between devices with their start and end apart: 10 -> 10, of which waited for: 4 -> 6; matrix products, arithmetic and copies ran while one was open for 1% -> 1% of each run, Pallas kernels for 6% -> 7%
where the time goes in v4:
time: 111 us
  waiting for transfers between devices  36.4 us (33%)
  blocking collectives  27.3 us (25%)
  starting transfers between devices  21.3 us (19%)
  Pallas kernels  21 us (19%)
  local copies, waits for them, and re-layouts  4.14 us (4%)
    all_to_all x1, blocking collectives, local(): returned = lax.all_to_all(sent, CHIP, 0, 0, tiled=True)  27.3 us
    all_to_all x1, waiting for transfers between devices, local(): arrived = lax.all_to_all(blocks, CHIP, 0, 0, tiled=True)  20.4 us
    all_to_all x1, starting transfers between devices, local(): arrived = lax.all_to_all(blocks, CHIP, 0, 0, tiled=True)  13.3 us
    pallas_call x1, Pallas kernels, attend(): pl.pallas_call(attend_kernel, in_specs=[VMEM] * 8, out_specs=VMEM, out_sh...  9.95 us
    ppermute x3, waiting for transfers between devices, local(): lax.ppermute(share, 'y', [(i, (i + o) % 4) for i in range(4)])  9.68 us
    ppermute x1, waiting for transfers between devices, local(): weights_other = swap_heads(weights)  5.21 us
    pallas_call x4, Pallas kernels, place_bias(): pl.pallas_call(place_kernel, grid_spec=pltpu.PrefetchScalarGridSpec(num_s...  3.37 us
    ppermute x3, starting transfers between devices, local(): lax.ppermute(share, 'y', [(i, (i + o) % 4) for i in range(4)])  2.69 us
  transfers between devices with their start and end apart: 10, of which 6 were waited for; matrix products, arithmetic and copies ran while one was open for 1% of the time, Pallas kernels for 7%

profile of v4, /device:TPU:2, one launch (start us, length us, event | category | flops | bytes accessed | tf_op | source)
XLA Modules:
  0.0 111.0 jit_solution(17366104127112039027)
XLA Ops:
  0.0 0.0 collective-permute-start
  0.0 0.7 pad.4.w_own_ref
  0.7 2.1 %collective-permute-start.1 = (bf16[16,128]{1,0:T(8,128)(2,1)S(1)}, bf16[16,128]{1,0:T(8,128)(2,1)S(1)}, u32[]{:S(2)}, u32[]{:S(2)}) collective-permute-start(bf16[16,128]{1,0:T(8,128)(2,1)S(1)} %pad.4.w_own_ref), channel_id=1, source_target_pairs={{0,1},{1,0},{2,3},{3,2},{4,5},{5,4},{6,7},{7,6},{8,9},{9,8},{10,11... | collective-permute-start | bytes 12296 | tf_op jit(solution)/shard_map/ppermute | solution.py:341
  2.8 0.7 pad_maximum_fusion.3.norm_ref
  3.5 0.1 stack.32.where_ref
  3.6 0.0 copy-start
  3.6 1.3 %copy-done = bf16[6,768,128]{2,1,0:T(8,128)(2,1)S(1)} copy-done((bf16[6,768,128]{2,1,0:T(8,128)(2,1)S(1)}, bf16[6,768,128]{2,1,0:T(8,128)(2,1)}, u32[]{:S(2)}) %copy-start) | copy-done | bytes 1179672
  4.8 1.6 %lay.1 = (f32[2304,128]{1,0:T(8,128)S(1)}, bf16[1152,128]{1,0:T(8,128)(2,1)S(1)}) custom-call(s32[5]{0:T(128)S(1)} %stack.32.where_ref, bf16[6,768,128]{2,1,0:T(8,128)(2,1)S(1)} %copy-done, f32[2,128]{1,0:T(2,128)S(1)} %pad_maximum_fusion.3.norm_ref), custom_call_target="tpu_custom_call" | custom-call | flops 11796480 | bytes 3538944 | tf_op jit(solution)/shard_map/lay/pallas_call | solution.py:93
  6.5 0.0 collective-permute-done.1.w_other_ref
  6.5 0.0 collective-permute-done.other_ref
  6.5 2.3 %pack.1 = bf16[64,56,128]{2,1,0:T(8,128)(2,1)} custom-call(s32[5]{0:T(128)S(1)} %stack.32.where_ref, f32[2304,128]{1,0:T(8,128)S(1)} %get-tuple-element.30.laid_ref, bf16[1152,128]{1,0:T(8,128)(2,1)S(1)} %get-tuple-element.31.picked_ref, bf16[6,768,128]{2,1,0:T(8,128)(2,1)S(1)} %collective-permute-done.other_ref, f32[2,128]{1,0:T(2,128)S(1)} %pad_maximum_fusion.3.norm_ref, ...), custom_call_target="tpu_custom_call" | custom-call | flops 35389440 | bytes 3538944 | tf_op jit(solution)/shard_map/pack/pallas_call | solution.py:142
  8.8 0.0 copy-start.1
  8.8 0.0 copy-start.2
  8.8 13.3 %all-to-all-start = ((bf16[64,56,128]{2,1,0:T(8,128)(2,1)}), bf16[64,56,128]{2,1,0:T(8,128)(2,1)S(1)}, u32[]{:S(2)}, u32[]{:S(2)}) async-start(bf16[64,56,128]{2,1,0:T(8,128)(2,1)} %pack.1), calls=%async_computation | async-start | bytes 1835008 | tf_op jit(solution)/shard_map/all_to_all | solution.py:344
  22.1 0.0 copy-done.1
  22.1 0.0 copy-done.2
  22.1 1.5 %collective-permute-start.2 = (bf16[128,320]{0,1:T(8,128)(2,1)S(1)}, bf16[128,320]{0,1:T(8,128)(2,1)S(1)}, u32[]{:S(2)}, u32[]{:S(2)}) collective-permute-start(bf16[128,320]{0,1:T(8,128)(2,1)S(1)} %pad_maximum_fusion), channel_id=1, source_target_pairs={{0,1},{1,0},{2,3},{3,2},{4,5},{5,4},{6,7},{7,6},{8,9},{9,8},{10,11... | collective-permute-start | bytes 245768 | tf_op jit(solution)/shard_map/ppermute | solution.py:346
  23.7 5.2 %collective-permute-done.2 = bf16[128,320]{0,1:T(8,128)(2,1)S(1)} collective-permute-done((bf16[128,320]{0,1:T(8,128)(2,1)S(1)}, bf16[128,320]{0,1:T(8,128)(2,1)S(1)}, u32[]{:S(2)}, u32[]{:S(2)}) %collective-permute-start.2) | collective-permute-done | bytes 81952 | tf_op jit(solution)/shard_map/ppermute | solution.py:346
  28.9 20.4 %all-to-all-done.arrived_ref = bf16[64,56,128]{2,1,0:T(8,128)(2,1)S(1)} async-done(((bf16[64,56,128]{2,1,0:T(8,128)(2,1)}), bf16[64,56,128]{2,1,0:T(8,128)(2,1)S(1)}, u32[]{:S(2)}, u32[]{:S(2)}) %all-to-all-start) | async-done | bytes 917536 | tf_op jit(solution)/shard_map/all_to_all | solution.py:344
  49.3 0.4 unpack.1
  49.7 0.1 collective-permute-start.4
  49.8 1.5 %collective-permute-start.5 = (bf16[12,192,128]{2,1,0:T(8,128)(2,1)S(1)}, bf16[12,192,128]{2,1,0:T(8,128)(2,1)S(1)}, u32[]{:S(2)}, u32[]{:S(2)}) collective-permute-start(bf16[12,192,128]{2,1,0:T(8,128)(2,1)S(1)} %get-tuple-element.34.own_ref), channel_id=1, source_target_pairs={{0,1},{1,0},{2,3},{3,2},{4,5},{5,4},{6,7},{7,6},{8,9},{9,8},{10,11... | collective-permute-start | bytes 1769480 | tf_op jit(solution)/shard_map/ppermute | solution.py:357
  51.3 0.8 collective-permute-start.3
  52.1 1.9 %collective-permute-start.7 = (bf16[1152,128]{1,0:T(8,128)(2,1)S(1)}, bf16[1152,128]{1,0:T(8,128)(2,1)S(1)}, u32[]{:S(2)}, u32[]{:S(2)}) collective-permute-start(bf16[1152,128]{1,0:T(8,128)(2,1)S(1)} %get-tuple-element.33.part_ref), channel_id=1, source_target_pairs={{0,64},{32,96},{64,0},{96,32},{1,65},{33,97},{65,1},{97,33},{2,66}... | collective-permute-start | bytes 884744 | tf_op jit(solution)/shard_map/ppermute | solution.py:358
  54.0 0.0 collective-permute-start.6
  54.0 0.1 copy.19.wk_ref
  54.1 0.8 place.4.refs_0_
  54.9 1.3 %ask.1 = (bf16[12,128,768]{2,1,0:T(8,128)(2,1)S(1)}, bf16[12,64,384]{2,1,0:T(8,128)(2,1)S(1)}) custom-call(bf16[12,192,128]{2,1,0:T(8,128)(2,1)S(1)} %get-tuple-element.34.own_ref, bf16[128,128]{1,0:T(8,128)(2,1)S(1)} %get-tuple-element.35.wq_ref, bf16[128,128]{1,0:T(8,128)(2,1)S(1)} %get-tuple-element.36.wg_ref), custom_call_target="tpu_custom_call" | custom-call | flops 301989888 | bytes 5898240 | tf_op jit(solution)/shard_map/ask/pallas_call | solution.py:266
  56.2 0.0 collective-permute-done.4.other_ref
  56.2 1.1 project.2
  57.3 3.8 %collective-permute-done.3.part_ref = bf16[1152,128]{1,0:T(8,128)(2,1)S(1)} collective-permute-done((bf16[1152,128]{1,0:T(8,128)(2,1)S(1)}, bf16[1152,128]{1,0:T(8,128)(2,1)S(1)}, u32[]{:S(2)}, u32[]{:S(2)}) %collective-permute-start.3) | collective-permute-done | bytes 294944 | tf_op jit(solution)/shard_map/ppermute | solution.py:358
  61.1 0.8 place.5.refs_0_
  62.0 1.5 %collective-permute-done.7.part_ref = bf16[1152,128]{1,0:T(8,128)(2,1)S(1)} collective-permute-done((bf16[1152,128]{1,0:T(8,128)(2,1)S(1)}, bf16[1152,128]{1,0:T(8,128)(2,1)S(1)}, u32[]{:S(2)}, u32[]{:S(2)}) %collective-permute-start.7) | collective-permute-done | bytes 294944 | tf_op jit(solution)/shard_map/ppermute | solution.py:358
  63.5 0.8 place.6.refs_0_
  64.4 4.3 %collective-permute-done.6.part_ref = bf16[1152,128]{1,0:T(8,128)(2,1)S(1)} collective-permute-done((bf16[1152,128]{1,0:T(8,128)(2,1)S(1)}, bf16[1152,128]{1,0:T(8,128)(2,1)S(1)}, u32[]{:S(2)}, u32[]{:S(2)}) %collective-permute-start.6) | collective-permute-done | bytes 294944 | tf_op jit(solution)/shard_map/ppermute | solution.py:358
  68.7 0.0 collective-permute-done.5.own_ref
  68.7 0.0 collective-permute-start.8
  68.7 0.8 place.7.bias_ref
  69.6 1.1 %collective-permute-done.8.other_ref = bf16[12,192,128]{2,1,0:T(8,128)(2,1)S(1)} collective-permute-done((bf16[12,192,128]{2,1,0:T(8,128)(2,1)S(1)}, bf16[12,192,128]{2,1,0:T(8,128)(2,1)S(1)}, u32[]{:S(2)}, u32[]{:S(2)}) %collective-permute-start.8) | collective-permute-done | bytes 589856 | tf_op jit(solution)/shard_map/ppermute | solution.py:367
  70.7 1.1 project.3
  71.8 10.0 %attend.1 = bf16[12,192,128]{2,1,0:T(8,128)(2,1)S(1)} custom-call(bf16[12,384,128]{2,1,0:T(8,128)(2,1)S(1)} %get-tuple-element.43.k0_ref, bf16[12,128,384]{2,1,0:T(8,128)(2,1)S(1)} %get-tuple-element.44.v0_ref, bf16[12,384,128]{2,1,0:T(8,128)(2,1)S(1)} %get-tuple-element.48.k1_ref, bf16[12,128,384]{2,1,0:T(8,128)(2,1)S(1)} %get-tuple-element.49.v1_ref, ...), custom_call_target="tpu_custom_call" | custom-call | flops 7247757312 | bytes 7077888 | tf_op jit(solution)/shard_map/attend/pallas_call | solution.py:320
  81.8 0.5 copy.22
  82.2 27.3 %all_to_all.10 = bf16[64,9,4,128]{3,2,1,0:T(4,128)(2,1)S(1)} all-to-all(bf16[64,9,4,128]{3,2,1,0:T(4,128)(2,1)S(1)} %copy.22), channel_id=1, replica_groups=mesh['xl'=2,'y'=4,'z'=8,'c'=2,'h'=2] {'xl','y','z'}, dimensions={0} | all-to-all | bytes 1179648 | tf_op jit(solution)/shard_map/all_to_all | solution.py:372
  109.5 0.1 copy.23
  109.6 0.4 copy.24
  110.1 1.0 reshape.27
  (8 shorter events, 0.1 us)
Async XLA Ops:
  0.0 6.5 %collective-permute-start = (bf16[6,768,128]{2,1,0:T(8,128)(2,1)}, bf16[6,768,128]{2,1,0:T(8,128)(2,1)S(1)}, u32[]{:S(2)}, u32[]{:S(2)}) collective-permute-start(bf16[6,768,128]{2,1,0:T(8,128)(2,1)} %own_ref.1), channel_id=1, source_target_pairs={{0,2},{2,0},{1,3},{3,1},{4,6},{6,4},{5,7},{7,5},{8,10},{10,8},{9,1... | collective-permute-start | bytes 3538952 | tf_op jit(solution)/shard_map/ppermute | solution.py:343
  0.7 5.8 %collective-permute-start.1 = (bf16[16,128]{1,0:T(8,128)(2,1)S(1)}, bf16[16,128]{1,0:T(8,128)(2,1)S(1)}, u32[]{:S(2)}, u32[]{:S(2)}) collective-permute-start(bf16[16,128]{1,0:T(8,128)(2,1)S(1)} %pad.4.w_own_ref), channel_id=1, source_target_pairs={{0,1},{1,0},{2,3},{3,2},{4,5},{5,4},{6,7},{7,6},{8,9},{9,8},{10,11... | collective-permute-start | bytes 12296 | tf_op jit(solution)/shard_map/ppermute | solution.py:341
  3.6 1.3 %copy-start = (bf16[6,768,128]{2,1,0:T(8,128)(2,1)S(1)}, bf16[6,768,128]{2,1,0:T(8,128)(2,1)}, u32[]{:S(2)}) copy-start(bf16[6,768,128]{2,1,0:T(8,128)(2,1)} %own_ref.1) | copy-start | bytes 3538948
  8.8 13.4 %copy-start.1 = (bf16[128,4,64]{0,2,1:T(8,128)(2,1)S(1)}, bf16[128,4,64]{0,2,1:T(8,128)(2,1)}, u32[]{:S(2)}) copy-start(bf16[128,4,64]{0,2,1:T(8,128)(2,1)} %param.9) | copy-start | bytes 196612
  8.8 13.4 %copy-start.2 = (bf16[64,128]{1,0:T(8,128)(2,1)S(1)}, bf16[64,128]{1,0:T(8,128)(2,1)}, u32[]{:S(2)}) copy-start(bf16[64,128]{1,0:T(8,128)(2,1)} %param.11) | copy-start | bytes 49156
  8.8 40.5 %all-to-all-start = ((bf16[64,56,128]{2,1,0:T(8,128)(2,1)}), bf16[64,56,128]{2,1,0:T(8,128)(2,1)S(1)}, u32[]{:S(2)}, u32[]{:S(2)}) async-start(bf16[64,56,128]{2,1,0:T(8,128)(2,1)} %pack.1), calls=%async_computation | async-start | bytes 1835008 | tf_op jit(solution)/shard_map/all_to_all | solution.py:344
  22.1 6.7 %collective-permute-start.2 = (bf16[128,320]{0,1:T(8,128)(2,1)S(1)}, bf16[128,320]{0,1:T(8,128)(2,1)S(1)}, u32[]{:S(2)}, u32[]{:S(2)}) collective-permute-start(bf16[128,320]{0,1:T(8,128)(2,1)S(1)} %pad_maximum_fusion), channel_id=1, source_target_pairs={{0,1},{1,0},{2,3},{3,2},{4,5},{5,4},{6,7},{7,6},{8,9},{9,8},{10,11... | collective-permute-start | bytes 245768 | tf_op jit(solution)/shard_map/ppermute | solution.py:346
  49.7 6.5 %collective-permute-start.4 = (bf16[12,192,128]{2,1,0:T(8,128)(2,1)S(1)}, bf16[12,192,128]{2,1,0:T(8,128)(2,1)S(1)}, u32[]{:S(2)}, u32[]{:S(2)}) collective-permute-start(bf16[12,192,128]{2,1,0:T(8,128)(2,1)S(1)} %get-tuple-element.34.own_ref), channel_id=1, source_target_pairs={{0,2},{2,0},{1,3},{3,1},{4,6},{6,4},{5,7},{7,5},{8,10},{10,8},{9,1... | collective-permute-start | bytes 1769480 | tf_op jit(solution)/shard_map/ppermute | solution.py:360
  49.8 18.9 %collective-permute-start.5 = (bf16[12,192,128]{2,1,0:T(8,128)(2,1)S(1)}, bf16[12,192,128]{2,1,0:T(8,128)(2,1)S(1)}, u32[]{:S(2)}, u32[]{:S(2)}) collective-permute-start(bf16[12,192,128]{2,1,0:T(8,128)(2,1)S(1)} %get-tuple-element.34.own_ref), channel_id=1, source_target_pairs={{0,1},{1,0},{2,3},{3,2},{4,5},{5,4},{6,7},{7,6},{8,9},{9,8},{10,11... | collective-permute-start | bytes 1769480 | tf_op jit(solution)/shard_map/ppermute | solution.py:357
  51.3 9.9 %collective-permute-start.3 = (bf16[1152,128]{1,0:T(8,128)(2,1)S(1)}, bf16[1152,128]{1,0:T(8,128)(2,1)S(1)}, u32[]{:S(2)}, u32[]{:S(2)}) collective-permute-start(bf16[1152,128]{1,0:T(8,128)(2,1)S(1)} %get-tuple-element.33.part_ref), channel_id=1, source_target_pairs={{0,96},{32,0},{64,32},{96,64},{1,97},{33,1},{65,33},{97,65},{2,98}... | collective-permute-start | bytes 884744 | tf_op jit(solution)/shard_map/ppermute | solution.py:358
  52.1 11.4 %collective-permute-start.7 = (bf16[1152,128]{1,0:T(8,128)(2,1)S(1)}, bf16[1152,128]{1,0:T(8,128)(2,1)S(1)}, u32[]{:S(2)}, u32[]{:S(2)}) collective-permute-start(bf16[1152,128]{1,0:T(8,128)(2,1)S(1)} %get-tuple-element.33.part_ref), channel_id=1, source_target_pairs={{0,64},{32,96},{64,0},{96,32},{1,65},{33,97},{65,1},{97,33},{2,66}... | collective-permute-start | bytes 884744 | tf_op jit(solution)/shard_map/ppermute | solution.py:358
  54.0 14.7 %collective-permute-start.6 = (bf16[1152,128]{1,0:T(8,128)(2,1)S(1)}, bf16[1152,128]{1,0:T(8,128)(2,1)S(1)}, u32[]{:S(2)}, u32[]{:S(2)}) collective-permute-start(bf16[1152,128]{1,0:T(8,128)(2,1)S(1)} %get-tuple-element.33.part_ref), channel_id=1, source_target_pairs={{0,32},{32,64},{64,96},{96,0},{1,33},{33,65},{65,97},{97,1},{2,34}... | collective-permute-start | bytes 884744 | tf_op jit(solution)/shard_map/ppermute | solution.py:358
  68.7 2.0 %collective-permute-start.8 = (bf16[12,192,128]{2,1,0:T(8,128)(2,1)S(1)}, bf16[12,192,128]{2,1,0:T(8,128)(2,1)S(1)}, u32[]{:S(2)}, u32[]{:S(2)}) collective-permute-start(bf16[12,192,128]{2,1,0:T(8,128)(2,1)S(1)} %collective-permute-done.5.own_ref), channel_id=1, source_target_pairs={{0,2},{2,0},{1,3},{3,1},{4,6},{6,4},{5,7},{7,5},{8,10},{10,8},{9,1... | collective-permute-start | bytes 1769480 | tf_op jit(solution)/shard_map/ppermute | solution.py:367

commit v5 on v4

--- a/solution.py
+++ b/solution.py
@@ -275,20 +275,24 @@
     )(own, wq, wg)
 
 
-def attend_kernel(k0_ref, v0_ref, k1_ref, v1_ref, masked_ref, gates_ref, bias_ref, wo_ref, out_ref):
+def attend_kernel(
+    k0_ref, v0_ref, far_ref, other_ref, wk_ref, wv_ref, masked_ref, gates_ref, bias_ref, wo_ref, out_ref
+):
     first = lax.broadcasted_iota(jnp.int32, (DH, 2 * QR), 1) < QR
     factor = 1.0 / (ROOT * math.log(2.0))
 
-    def score(m):
-        keys = jnp.concatenate([k0_ref[m], k1_ref[m]], axis=0)
+    def project(m):
+        entries = jnp.concatenate([far_ref[m], other_ref[m]], axis=0)
+        keys = jnp.dot(entries, wk_ref[...], preferred_element_type=F32).astype(BF16)
+        values = lax.dot_general(wv_ref[...], entries, NT, preferred_element_type=F32).astype(BF16)
+        return jnp.concatenate([k0_ref[m], keys], axis=0), jnp.concatenate([v0_ref[m], values], axis=1)
+
+    def score(m, keys):
         return jnp.dot(keys, masked_ref[m], preferred_element_type=F32) + bias_ref[...]
 
-    def soften(m, scores):
-        highest = jnp.max(scores, axis=0, keepdims=True)
-        exponent = jnp.exp2((scores - highest) * factor)
+    def gather(exponent, values):
         totals = jnp.sum(exponent, axis=0, keepdims=True)
         weights = exponent.astype(BF16)
-        values = jnp.concatenate([v0_ref[m], v1_ref[m]], axis=1)
         low = jnp.dot(values[: 2 * DH], weights[:, :256], preferred_element_type=F32)
         both = jnp.dot(values, weights[:, 256:512], preferred_element_type=F32)
         high = jnp.dot(values[2 * DH :], weights[:, 512:], preferred_element_type=F32)
@@ -307,19 +311,26 @@
         out_ref[m] = jnp.dot(turned, wo_ref[...], preferred_element_type=F32).astype(BF16)
 
     attended = []
-    scores = score(0)
+    keys, values = project(0)
+    scores, held = score(0, keys), values
+    keys, values = project(1)
     for m in range(COLS):
-        following = score(m + 1) if m + 1 < COLS else None
-        attended.append(soften(m, scores))
-        scores = following
+        if m + 1 < COLS:
+            following, after = score(m + 1, keys), values
+        if m + 2 < COLS:
+            keys, values = project(m + 2)
+        highest = jnp.max(scores, axis=0, keepdims=True)
+        attended.append(gather(jnp.exp2((scores - highest) * factor), held))
+        if m + 1 < COLS:
+            scores, held = following, after
     for m in range(COLS):
         finish(m, *attended[m])
 
 
-def attend(k0, v0, k1, v1, masked, gates, bias, wo):
+def attend(k0, v0, far, other, wk, wv, masked, gates, bias, wo):
     return pl.pallas_call(
         attend_kernel,
-        in_specs=[VMEM] * 8,
+        in_specs=[VMEM] * 10,
         out_specs=VMEM,
         out_shape=jax.ShapeDtypeStruct((COLS, QR, C), BF16),
         compiler_params=params(40),
@@ -327,7 +338,7 @@
             flops=COLS * 8 * N * N * C, bytes_accessed=12 * N * N, transcendentals=COLS * N * N
         ),
         name="attend",
-    )(k0, v0, k1, v1, masked, gates, bias, wo)
+    )(k0, v0, far, other, wk, wv, masked, gates, bias, wo)
 
 
 def local(pair, ln_gain, ln_shift, w_project, w_bias, w_out):
@@ -364,9 +375,9 @@
     for step in (3, 2):
         bias = place_bias(where, norm, w_own, w_other, parts[step], step, bias)
     far, parts[1], bias = lax.optimization_barrier((far, parts[1], bias))
-    k1, v1 = project(far, swap_cores(far), wk, wv)
+    far_other = swap_cores(far)
     bias = place_bias(where, norm, w_own, w_other, parts[1], 1, bias)
-    done = attend(k0, v0, k1, v1, masked, gates, bias, wo)
+    done = attend(k0, v0, far, far_other, wk, wv, masked, gates, bias, wo)
 
     sent = done.reshape(COLS, 3, CHIPS, C).transpose(2, 1, 0, 3).reshape(CHIPS, 9, 4, C)
     returned = lax.all_to_all(sent, CHIP, 0, 0, tiled=True)

time: 111 us -> 111 us (level)
  no operation moved by 1% of the time
where the time goes in v5:
time: 111 us; the launch traced here: 110 us
  waiting for transfers between devices  36.4 us (33%)
  blocking collectives  27.3 us (25%)
  starting transfers between devices  21.1 us (19%)
  Pallas kernels  20.4 us (18%)
  local copies, waits for them, and re-layouts  4.15 us (4%)
    all_to_all x1, blocking collectives, local(): returned = lax.all_to_all(sent, CHIP, 0, 0, tiled=True)  27.3 us
    all_to_all x1, waiting for transfers between devices, local(): arrived = lax.all_to_all(blocks, CHIP, 0, 0, tiled=True)  20.4 us
    all_to_all x1, starting transfers between devices, local(): arrived = lax.all_to_all(blocks, CHIP, 0, 0, tiled=True)  13.2 us
    pallas_call x1, Pallas kernels, attend(): pl.pallas_call(attend_kernel, in_specs=[VMEM] * 10, out_specs=VMEM, out_s...  10.4 us
    ppermute x3, waiting for transfers between devices, local(): lax.ppermute(share, 'y', [(i, (i + o) % 4) for i in range(4)])  9.67 us
    ppermute x1, waiting for transfers between devices, local(): weights_other = swap_heads(weights)  5.23 us
    pallas_call x4, Pallas kernels, place_bias(): pl.pallas_call(place_kernel, grid_spec=pltpu.PrefetchScalarGridSpec(num_s...  3.37 us
    ppermute x3, starting transfers between devices, local(): lax.ppermute(share, 'y', [(i, (i + o) % 4) for i in range(4)])  2.69 us
  transfers between devices with their start and end apart: 10, of which 6 were waited for; matrix products, arithmetic and copies ran while one was open for 1% of the time, Pallas kernels for 7%

profile of v5, /device:TPU:2, one launch (start us, length us, event | category | flops | bytes accessed | tf_op | source)
XLA Modules:
  0.0 110.3 jit_solution(13003692491005714157)
XLA Ops:
  0.0 0.0 collective-permute-start
  0.0 0.7 pad.4.w_own_ref
  0.7 2.1 %collective-permute-start.1 = (bf16[16,128]{1,0:T(8,128)(2,1)S(1)}, bf16[16,128]{1,0:T(8,128)(2,1)S(1)}, u32[]{:S(2)}, u32[]{:S(2)}) collective-permute-start(bf16[16,128]{1,0:T(8,128)(2,1)S(1)} %pad.4.w_own_ref), channel_id=1, source_target_pairs={{0,1},{1,0},{2,3},{3,2},{4,5},{5,4},{6,7},{7,6},{8,9},{9,8},{10,11... | collective-permute-start | bytes 12296 | tf_op jit(solution)/shard_map/ppermute | solution.py:352
  2.8 0.7 pad_maximum_fusion.3.norm_ref
  3.5 0.1 stack.32.where_ref
  3.6 0.0 copy-start
  3.6 1.3 %copy-done = bf16[6,768,128]{2,1,0:T(8,128)(2,1)S(1)} copy-done((bf16[6,768,128]{2,1,0:T(8,128)(2,1)S(1)}, bf16[6,768,128]{2,1,0:T(8,128)(2,1)}, u32[]{:S(2)}) %copy-start) | copy-done | bytes 1179672
  4.8 1.6 %lay.1 = (f32[2304,128]{1,0:T(8,128)S(1)}, bf16[1152,128]{1,0:T(8,128)(2,1)S(1)}) custom-call(s32[5]{0:T(128)S(1)} %stack.32.where_ref, bf16[6,768,128]{2,1,0:T(8,128)(2,1)S(1)} %copy-done, f32[2,128]{1,0:T(2,128)S(1)} %pad_maximum_fusion.3.norm_ref), custom_call_target="tpu_custom_call" | custom-call | flops 11796480 | bytes 3538944 | tf_op jit(solution)/shard_map/lay/pallas_call | solution.py:93
  6.5 0.0 collective-permute-done.1.w_other_ref
  6.5 0.0 collective-permute-done.other_ref
  6.5 0.0 copy-start.1
  6.5 0.0 copy-start.2
  6.5 2.3 %pack.1 = bf16[64,56,128]{2,1,0:T(8,128)(2,1)} custom-call(s32[5]{0:T(128)S(1)} %stack.32.where_ref, f32[2304,128]{1,0:T(8,128)S(1)} %get-tuple-element.28.laid_ref, bf16[1152,128]{1,0:T(8,128)(2,1)S(1)} %get-tuple-element.29.picked_ref, bf16[6,768,128]{2,1,0:T(8,128)(2,1)S(1)} %collective-permute-done.other_ref, f32[2,128]{1,0:T(2,128)S(1)} %pad_maximum_fusion.3.norm_ref, ...), custom_call_target="tpu_custom_call" | custom-call | flops 35389440 | bytes 3538944 | tf_op jit(solution)/shard_map/pack/pallas_call | solution.py:142
  8.8 13.2 %all-to-all-start = ((bf16[64,56,128]{2,1,0:T(8,128)(2,1)}), bf16[64,56,128]{2,1,0:T(8,128)(2,1)S(1)}, u32[]{:S(2)}, u32[]{:S(2)}) async-start(bf16[64,56,128]{2,1,0:T(8,128)(2,1)} %pack.1), calls=%async_computation | async-start | bytes 1835008 | tf_op jit(solution)/shard_map/all_to_all | solution.py:355
  22.0 0.0 copy-done.1
  22.0 0.0 copy-done.2
  22.0 1.5 %collective-permute-start.2 = (bf16[128,320]{0,1:T(8,128)(2,1)S(1)}, bf16[128,320]{0,1:T(8,128)(2,1)S(1)}, u32[]{:S(2)}, u32[]{:S(2)}) collective-permute-start(bf16[128,320]{0,1:T(8,128)(2,1)S(1)} %pad_maximum_fusion), channel_id=1, source_target_pairs={{0,1},{1,0},{2,3},{3,2},{4,5},{5,4},{6,7},{7,6},{8,9},{9,8},{10,11... | collective-permute-start | bytes 245768 | tf_op jit(solution)/shard_map/ppermute | solution.py:357
  23.5 5.2 %collective-permute-done.2 = bf16[128,320]{0,1:T(8,128)(2,1)S(1)} collective-permute-done((bf16[128,320]{0,1:T(8,128)(2,1)S(1)}, bf16[128,320]{0,1:T(8,128)(2,1)S(1)}, u32[]{:S(2)}, u32[]{:S(2)}) %collective-permute-start.2) | collective-permute-done | bytes 81952 | tf_op jit(solution)/shard_map/ppermute | solution.py:357
  28.8 20.4 %all-to-all-done.arrived_ref = bf16[64,56,128]{2,1,0:T(8,128)(2,1)S(1)} async-done(((bf16[64,56,128]{2,1,0:T(8,128)(2,1)}), bf16[64,56,128]{2,1,0:T(8,128)(2,1)S(1)}, u32[]{:S(2)}, u32[]{:S(2)}) %all-to-all-start) | async-done | bytes 917536 | tf_op jit(solution)/shard_map/all_to_all | solution.py:355
  49.2 0.4 unpack.1
  49.6 0.1 collective-permute-start.4
  49.7 1.5 %collective-permute-start.5 = (bf16[12,192,128]{2,1,0:T(8,128)(2,1)S(1)}, bf16[12,192,128]{2,1,0:T(8,128)(2,1)S(1)}, u32[]{:S(2)}, u32[]{:S(2)}) collective-permute-start(bf16[12,192,128]{2,1,0:T(8,128)(2,1)S(1)} %get-tuple-element.32.own_ref), channel_id=1, source_target_pairs={{0,1},{1,0},{2,3},{3,2},{4,5},{5,4},{6,7},{7,6},{8,9},{9,8},{10,11... | collective-permute-start | bytes 1769480 | tf_op jit(solution)/shard_map/ppermute | solution.py:368
  51.2 0.8 collective-permute-start.3
  52.0 1.9 %collective-permute-start.7 = (bf16[1152,128]{1,0:T(8,128)(2,1)S(1)}, bf16[1152,128]{1,0:T(8,128)(2,1)S(1)}, u32[]{:S(2)}, u32[]{:S(2)}) collective-permute-start(bf16[1152,128]{1,0:T(8,128)(2,1)S(1)} %get-tuple-element.31.part_ref), channel_id=1, source_target_pairs={{0,64},{32,96},{64,0},{96,32},{1,65},{33,97},{65,1},{97,33},{2,66}... | collective-permute-start | bytes 884744 | tf_op jit(solution)/shard_map/ppermute | solution.py:369
  53.8 0.0 collective-permute-start.6
  53.8 0.1 copy.19.wk_ref
  54.0 0.8 place.4.refs_0_
  54.8 1.3 %ask.1 = (bf16[12,128,768]{2,1,0:T(8,128)(2,1)S(1)}, bf16[12,64,384]{2,1,0:T(8,128)(2,1)S(1)}) custom-call(bf16[12,192,128]{2,1,0:T(8,128)(2,1)S(1)} %get-tuple-element.32.own_ref, bf16[128,128]{1,0:T(8,128)(2,1)S(1)} %get-tuple-element.33.wq_ref, bf16[128,128]{1,0:T(8,128)(2,1)S(1)} %get-tuple-element.34.wg_ref), custom_call_target="tpu_custom_call" | custom-call | flops 301989888 | bytes 5898240 | tf_op jit(solution)/shard_map/ask/pallas_call | solution.py:266
  56.1 0.0 collective-permute-done.4.other_ref
  56.1 1.1 project.1
  57.2 3.8 %collective-permute-done.3.part_ref = bf16[1152,128]{1,0:T(8,128)(2,1)S(1)} collective-permute-done((bf16[1152,128]{1,0:T(8,128)(2,1)S(1)}, bf16[1152,128]{1,0:T(8,128)(2,1)S(1)}, u32[]{:S(2)}, u32[]{:S(2)}) %collective-permute-start.3) | collective-permute-done | bytes 294944 | tf_op jit(solution)/shard_map/ppermute | solution.py:369
  61.0 0.8 place.5.refs_0_
  61.9 1.5 %collective-permute-done.7.part_ref = bf16[1152,128]{1,0:T(8,128)(2,1)S(1)} collective-permute-done((bf16[1152,128]{1,0:T(8,128)(2,1)S(1)}, bf16[1152,128]{1,0:T(8,128)(2,1)S(1)}, u32[]{:S(2)}, u32[]{:S(2)}) %collective-permute-start.7) | collective-permute-done | bytes 294944 | tf_op jit(solution)/shard_map/ppermute | solution.py:369
  63.4 0.8 place.6.refs_0_
  64.2 4.3 %collective-permute-done.6.part_ref = bf16[1152,128]{1,0:T(8,128)(2,1)S(1)} collective-permute-done((bf16[1152,128]{1,0:T(8,128)(2,1)S(1)}, bf16[1152,128]{1,0:T(8,128)(2,1)S(1)}, u32[]{:S(2)}, u32[]{:S(2)}) %collective-permute-start.6) | collective-permute-done | bytes 294944 | tf_op jit(solution)/shard_map/ppermute | solution.py:369
  68.6 0.0 collective-permute-done.5.far_ref
  68.6 0.0 collective-permute-start.8
  68.6 0.8 place.7.bias_ref
  69.4 1.1 %collective-permute-done.8.other_ref = bf16[12,192,128]{2,1,0:T(8,128)(2,1)S(1)} collective-permute-done((bf16[12,192,128]{2,1,0:T(8,128)(2,1)S(1)}, bf16[12,192,128]{2,1,0:T(8,128)(2,1)S(1)}, u32[]{:S(2)}, u32[]{:S(2)}) %collective-permute-start.8) | collective-permute-done | bytes 589856 | tf_op jit(solution)/shard_map/ppermute | solution.py:378
  70.6 10.4 %attend.1 = bf16[12,192,128]{2,1,0:T(8,128)(2,1)S(1)} custom-call(bf16[12,384,128]{2,1,0:T(8,128)(2,1)S(1)} %get-tuple-element.41.k0_ref, bf16[12,128,384]{2,1,0:T(8,128)(2,1)S(1)} %get-tuple-element.42.v0_ref, bf16[12,192,128]{2,1,0:T(8,128)(2,1)S(1)} %collective-permute-done.5.far_ref, bf16[12,192,128]{2,1,0:T(8,128)(2,1)S(1)} %collective-permute-done.8.other_ref, ...), custom_call_target="tpu_custom_call" | custom-call | flops 7247757312 | bytes 7077888 | tf_op jit(solution)/shard_map/attend/pallas_call | solution.py:331
  81.1 0.5 copy.22
  81.5 27.3 %all_to_all.10 = bf16[64,9,4,128]{3,2,1,0:T(4,128)(2,1)S(1)} all-to-all(bf16[64,9,4,128]{3,2,1,0:T(4,128)(2,1)S(1)} %copy.22), channel_id=1, replica_groups=mesh['xl'=2,'y'=4,'z'=8,'c'=2,'h'=2] {'xl','y','z'}, dimensions={0} | all-to-all | bytes 1179648 | tf_op jit(solution)/shard_map/all_to_all | solution.py:383
  108.8 0.1 copy.23
  108.9 0.4 copy.24
  109.4 1.0 reshape.27
  (8 shorter events, 0.1 us)
Async XLA Ops:
  0.0 6.5 %collective-permute-start = (bf16[6,768,128]{2,1,0:T(8,128)(2,1)}, bf16[6,768,128]{2,1,0:T(8,128)(2,1)S(1)}, u32[]{:S(2)}, u32[]{:S(2)}) collective-permute-start(bf16[6,768,128]{2,1,0:T(8,128)(2,1)} %own_ref.1), channel_id=1, source_target_pairs={{0,2},{2,0},{1,3},{3,1},{4,6},{6,4},{5,7},{7,5},{8,10},{10,8},{9,1... | collective-permute-start | bytes 3538952 | tf_op jit(solution)/shard_map/ppermute | solution.py:354
  0.7 5.8 %collective-permute-start.1 = (bf16[16,128]{1,0:T(8,128)(2,1)S(1)}, bf16[16,128]{1,0:T(8,128)(2,1)S(1)}, u32[]{:S(2)}, u32[]{:S(2)}) collective-permute-start(bf16[16,128]{1,0:T(8,128)(2,1)S(1)} %pad.4.w_own_ref), channel_id=1, source_target_pairs={{0,1},{1,0},{2,3},{3,2},{4,5},{5,4},{6,7},{7,6},{8,9},{9,8},{10,11... | collective-permute-start | bytes 12296 | tf_op jit(solution)/shard_map/ppermute | solution.py:352
  3.6 1.3 %copy-start = (bf16[6,768,128]{2,1,0:T(8,128)(2,1)S(1)}, bf16[6,768,128]{2,1,0:T(8,128)(2,1)}, u32[]{:S(2)}) copy-start(bf16[6,768,128]{2,1,0:T(8,128)(2,1)} %own_ref.1) | copy-start | bytes 3538948
  6.5 15.5 %copy-start.1 = (bf16[128,4,64]{0,2,1:T(8,128)(2,1)S(1)}, bf16[128,4,64]{0,2,1:T(8,128)(2,1)}, u32[]{:S(2)}) copy-start(bf16[128,4,64]{0,2,1:T(8,128)(2,1)} %param.9) | copy-start | bytes 196612
  6.5 15.5 %copy-start.2 = (bf16[64,128]{1,0:T(8,128)(2,1)S(1)}, bf16[64,128]{1,0:T(8,128)(2,1)}, u32[]{:S(2)}) copy-start(bf16[64,128]{1,0:T(8,128)(2,1)} %param.11) | copy-start | bytes 49156
  8.8 40.4 %all-to-all-start = ((bf16[64,56,128]{2,1,0:T(8,128)(2,1)}), bf16[64,56,128]{2,1,0:T(8,128)(2,1)S(1)}, u32[]{:S(2)}, u32[]{:S(2)}) async-start(bf16[64,56,128]{2,1,0:T(8,128)(2,1)} %pack.1), calls=%async_computation | async-start | bytes 1835008 | tf_op jit(solution)/shard_map/all_to_all | solution.py:355
  22.0 6.7 %collective-permute-start.2 = (bf16[128,320]{0,1:T(8,128)(2,1)S(1)}, bf16[128,320]{0,1:T(8,128)(2,1)S(1)}, u32[]{:S(2)}, u32[]{:S(2)}) collective-permute-start(bf16[128,320]{0,1:T(8,128)(2,1)S(1)} %pad_maximum_fusion), channel_id=1, source_target_pairs={{0,1},{1,0},{2,3},{3,2},{4,5},{5,4},{6,7},{7,6},{8,9},{9,8},{10,11... | collective-permute-start | bytes 245768 | tf_op jit(solution)/shard_map/ppermute | solution.py:357
  49.6 6.5 %collective-permute-start.4 = (bf16[12,192,128]{2,1,0:T(8,128)(2,1)S(1)}, bf16[12,192,128]{2,1,0:T(8,128)(2,1)S(1)}, u32[]{:S(2)}, u32[]{:S(2)}) collective-permute-start(bf16[12,192,128]{2,1,0:T(8,128)(2,1)S(1)} %get-tuple-element.32.own_ref), channel_id=1, source_target_pairs={{0,2},{2,0},{1,3},{3,1},{4,6},{6,4},{5,7},{7,5},{8,10},{10,8},{9,1... | collective-permute-start | bytes 1769480 | tf_op jit(solution)/shard_map/ppermute | solution.py:371
  49.7 18.9 %collective-permute-start.5 = (bf16[12,192,128]{2,1,0:T(8,128)(2,1)S(1)}, bf16[12,192,128]{2,1,0:T(8,128)(2,1)S(1)}, u32[]{:S(2)}, u32[]{:S(2)}) collective-permute-start(bf16[12,192,128]{2,1,0:T(8,128)(2,1)S(1)} %get-tuple-element.32.own_ref), channel_id=1, source_target_pairs={{0,1},{1,0},{2,3},{3,2},{4,5},{5,4},{6,7},{7,6},{8,9},{9,8},{10,11... | collective-permute-start | bytes 1769480 | tf_op jit(solution)/shard_map/ppermute | solution.py:368
  51.2 9.9 %collective-permute-start.3 = (bf16[1152,128]{1,0:T(8,128)(2,1)S(1)}, bf16[1152,128]{1,0:T(8,128)(2,1)S(1)}, u32[]{:S(2)}, u32[]{:S(2)}) collective-permute-start(bf16[1152,128]{1,0:T(8,128)(2,1)S(1)} %get-tuple-element.31.part_ref), channel_id=1, source_target_pairs={{0,96},{32,0},{64,32},{96,64},{1,97},{33,1},{65,33},{97,65},{2,98}... | collective-permute-start | bytes 884744 | tf_op jit(solution)/shard_map/ppermute | solution.py:369
  52.0 11.4 %collective-permute-start.7 = (bf16[1152,128]{1,0:T(8,128)(2,1)S(1)}, bf16[1152,128]{1,0:T(8,128)(2,1)S(1)}, u32[]{:S(2)}, u32[]{:S(2)}) collective-permute-start(bf16[1152,128]{1,0:T(8,128)(2,1)S(1)} %get-tuple-element.31.part_ref), channel_id=1, source_target_pairs={{0,64},{32,96},{64,0},{96,32},{1,65},{33,97},{65,1},{97,33},{2,66}... | collective-permute-start | bytes 884744 | tf_op jit(solution)/shard_map/ppermute | solution.py:369
  53.8 14.7 %collective-permute-start.6 = (bf16[1152,128]{1,0:T(8,128)(2,1)S(1)}, bf16[1152,128]{1,0:T(8,128)(2,1)S(1)}, u32[]{:S(2)}, u32[]{:S(2)}) collective-permute-start(bf16[1152,128]{1,0:T(8,128)(2,1)S(1)} %get-tuple-element.31.part_ref), channel_id=1, source_target_pairs={{0,32},{32,64},{64,96},{96,0},{1,33},{33,65},{65,97},{97,1},{2,34}... | collective-permute-start | bytes 884744 | tf_op jit(solution)/shard_map/ppermute | solution.py:369
  68.6 2.0 %collective-permute-start.8 = (bf16[12,192,128]{2,1,0:T(8,128)(2,1)S(1)}, bf16[12,192,128]{2,1,0:T(8,128)(2,1)S(1)}, u32[]{:S(2)}, u32[]{:S(2)}) collective-permute-start(bf16[12,192,128]{2,1,0:T(8,128)(2,1)S(1)} %collective-permute-done.5.far_ref), channel_id=1, source_target_pairs={{0,2},{2,0},{1,3},{3,1},{4,6},{6,4},{5,7},{7,5},{8,10},{10,8},{9,1... | collective-permute-start | bytes 1769480 | tf_op jit(solution)/shard_map/ppermute | solution.py:378

commit v6 on v5

--- a/solution.py
+++ b/solution.py
@@ -379,9 +379,9 @@
     bias = place_bias(where, norm, w_own, w_other, parts[1], 1, bias)
     done = attend(k0, v0, far, far_other, wk, wv, masked, gates, bias, wo)
 
-    sent = done.reshape(COLS, 3, CHIPS, C).transpose(2, 1, 0, 3).reshape(CHIPS, 9, 4, C)
+    sent = done.reshape(COLS, 3, CHIPS, C).transpose(2, 0, 1, 3).reshape(CHIPS, 9, 4, C)
     returned = lax.all_to_all(sent, CHIP, 0, 0, tiled=True)
-    return returned.reshape(CHIPS, 3, COLS, C).transpose(1, 0, 2, 3).reshape(3, N, C)
+    return returned.reshape(N, 3, C).transpose(1, 0, 2)
 
 
 def solution(mesh):

time: 111 us -> 110 us (level)
  no operation moved by 1% of the time
where the time goes in v6:
time: 110 us
  waiting for transfers between devices  36.4 us (33%)
  blocking collectives  27.3 us (25%)
  starting transfers between devices  21.1 us (19%)
  Pallas kernels  20.4 us (19%)
  local copies, waits for them, and re-layouts  3.81 us (3%)
    all_to_all x1, blocking collectives, local(): returned = lax.all_to_all(sent, CHIP, 0, 0, tiled=True)  27.3 us
    all_to_all x1, waiting for transfers between devices, local(): arrived = lax.all_to_all(blocks, CHIP, 0, 0, tiled=True)  20.4 us
    all_to_all x1, starting transfers between devices, local(): arrived = lax.all_to_all(blocks, CHIP, 0, 0, tiled=True)  13.2 us
    pallas_call x1, Pallas kernels, attend(): pl.pallas_call(attend_kernel, in_specs=[VMEM] * 10, out_specs=VMEM, out_s...  10.4 us
    ppermute x3, waiting for transfers between devices, local(): lax.ppermute(share, 'y', [(i, (i + o) % 4) for i in range(4)])  9.67 us
    ppermute x1, waiting for transfers between devices, local(): weights_other = swap_heads(weights)  5.23 us
    pallas_call x4, Pallas kernels, place_bias(): pl.pallas_call(place_kernel, grid_spec=pltpu.PrefetchScalarGridSpec(num_s...  3.37 us
    ppermute x3, starting transfers between devices, local(): lax.ppermute(share, 'y', [(i, (i + o) % 4) for i in range(4)])  2.69 us
  transfers between devices with their start and end apart: 10, of which 6 were waited for; matrix products, arithmetic and copies ran while one was open for 1% of the time, Pallas kernels for 7%

profile of v6, /device:TPU:2, one launch (start us, length us, event | category | flops | bytes accessed | tf_op | source)
XLA Modules:
  0.0 110.0 jit_solution(16327503440082000942)
XLA Ops:
  0.0 0.0 collective-permute-start
  0.0 0.7 pad.4.w_own_ref
  0.7 2.1 %collective-permute-start.1 = (bf16[16,128]{1,0:T(8,128)(2,1)S(1)}, bf16[16,128]{1,0:T(8,128)(2,1)S(1)}, u32[]{:S(2)}, u32[]{:S(2)}) collective-permute-start(bf16[16,128]{1,0:T(8,128)(2,1)S(1)} %pad.4.w_own_ref), channel_id=1, source_target_pairs={{0,1},{1,0},{2,3},{3,2},{4,5},{5,4},{6,7},{7,6},{8,9},{9,8},{10,11... | collective-permute-start | bytes 12296 | tf_op jit(solution)/shard_map/ppermute | solution.py:352
  2.8 0.7 pad_maximum_fusion.3.norm_ref
  3.5 0.1 stack.32.where_ref
  3.6 0.0 copy-start
  3.6 1.3 %copy-done = bf16[6,768,128]{2,1,0:T(8,128)(2,1)S(1)} copy-done((bf16[6,768,128]{2,1,0:T(8,128)(2,1)S(1)}, bf16[6,768,128]{2,1,0:T(8,128)(2,1)}, u32[]{:S(2)}) %copy-start) | copy-done | bytes 1179672
  4.8 1.6 %lay.1 = (f32[2304,128]{1,0:T(8,128)S(1)}, bf16[1152,128]{1,0:T(8,128)(2,1)S(1)}) custom-call(s32[5]{0:T(128)S(1)} %stack.32.where_ref, bf16[6,768,128]{2,1,0:T(8,128)(2,1)S(1)} %copy-done, f32[2,128]{1,0:T(2,128)S(1)} %pad_maximum_fusion.3.norm_ref), custom_call_target="tpu_custom_call" | custom-call | flops 11796480 | bytes 3538944 | tf_op jit(solution)/shard_map/lay/pallas_call | solution.py:93
  6.5 0.0 collective-permute-done.1.w_other_ref
  6.5 0.0 collective-permute-done.other_ref
  6.5 0.0 copy-start.1
  6.5 0.0 copy-start.2
  6.5 2.3 %pack.1 = bf16[64,56,128]{2,1,0:T(8,128)(2,1)} custom-call(s32[5]{0:T(128)S(1)} %stack.32.where_ref, f32[2304,128]{1,0:T(8,128)S(1)} %get-tuple-element.28.laid_ref, bf16[1152,128]{1,0:T(8,128)(2,1)S(1)} %get-tuple-element.29.picked_ref, bf16[6,768,128]{2,1,0:T(8,128)(2,1)S(1)} %collective-permute-done.other_ref, f32[2,128]{1,0:T(2,128)S(1)} %pad_maximum_fusion.3.norm_ref, ...), custom_call_target="tpu_custom_call" | custom-call | flops 35389440 | bytes 3538944 | tf_op jit(solution)/shard_map/pack/pallas_call | solution.py:142
  8.8 13.2 %all-to-all-start = ((bf16[64,56,128]{2,1,0:T(8,128)(2,1)}), bf16[64,56,128]{2,1,0:T(8,128)(2,1)S(1)}, u32[]{:S(2)}, u32[]{:S(2)}) async-start(bf16[64,56,128]{2,1,0:T(8,128)(2,1)} %pack.1), calls=%async_computation | async-start | bytes 1835008 | tf_op jit(solution)/shard_map/all_to_all | solution.py:355
  22.0 0.0 copy-done.1
  22.0 0.0 copy-done.2
  22.0 1.5 %collective-permute-start.2 = (bf16[128,320]{0,1:T(8,128)(2,1)S(1)}, bf16[128,320]{0,1:T(8,128)(2,1)S(1)}, u32[]{:S(2)}, u32[]{:S(2)}) collective-permute-start(bf16[128,320]{0,1:T(8,128)(2,1)S(1)} %pad_maximum_fusion), channel_id=1, source_target_pairs={{0,1},{1,0},{2,3},{3,2},{4,5},{5,4},{6,7},{7,6},{8,9},{9,8},{10,11... | collective-permute-start | bytes 245768 | tf_op jit(solution)/shard_map/ppermute | solution.py:357
  23.5 5.2 %collective-permute-done.2 = bf16[128,320]{0,1:T(8,128)(2,1)S(1)} collective-permute-done((bf16[128,320]{0,1:T(8,128)(2,1)S(1)}, bf16[128,320]{0,1:T(8,128)(2,1)S(1)}, u32[]{:S(2)}, u32[]{:S(2)}) %collective-permute-start.2) | collective-permute-done | bytes 81952 | tf_op jit(solution)/shard_map/ppermute | solution.py:357
  28.8 20.4 %all-to-all-done.arrived_ref = bf16[64,56,128]{2,1,0:T(8,128)(2,1)S(1)} async-done(((bf16[64,56,128]{2,1,0:T(8,128)(2,1)}), bf16[64,56,128]{2,1,0:T(8,128)(2,1)S(1)}, u32[]{:S(2)}, u32[]{:S(2)}) %all-to-all-start) | async-done | bytes 917536 | tf_op jit(solution)/shard_map/all_to_all | solution.py:355
  49.2 0.4 unpack.1
  49.6 0.1 collective-permute-start.4
  49.7 1.5 %collective-permute-start.5 = (bf16[12,192,128]{2,1,0:T(8,128)(2,1)S(1)}, bf16[12,192,128]{2,1,0:T(8,128)(2,1)S(1)}, u32[]{:S(2)}, u32[]{:S(2)}) collective-permute-start(bf16[12,192,128]{2,1,0:T(8,128)(2,1)S(1)} %get-tuple-element.32.own_ref), channel_id=1, source_target_pairs={{0,1},{1,0},{2,3},{3,2},{4,5},{5,4},{6,7},{7,6},{8,9},{9,8},{10,11... | collective-permute-start | bytes 1769480 | tf_op jit(solution)/shard_map/ppermute | solution.py:368
  51.2 0.8 collective-permute-start.3
  52.0 1.9 %collective-permute-start.7 = (bf16[1152,128]{1,0:T(8,128)(2,1)S(1)}, bf16[1152,128]{1,0:T(8,128)(2,1)S(1)}, u32[]{:S(2)}, u32[]{:S(2)}) collective-permute-start(bf16[1152,128]{1,0:T(8,128)(2,1)S(1)} %get-tuple-element.31.part_ref), channel_id=1, source_target_pairs={{0,64},{32,96},{64,0},{96,32},{1,65},{33,97},{65,1},{97,33},{2,66}... | collective-permute-start | bytes 884744 | tf_op jit(solution)/shard_map/ppermute | solution.py:369
  53.8 0.0 collective-permute-start.6
  53.8 0.1 copy.24.wk_ref
  54.0 0.8 place.4.refs_0_
  54.8 1.3 %ask.1 = (bf16[12,128,768]{2,1,0:T(8,128)(2,1)S(1)}, bf16[12,64,384]{2,1,0:T(8,128)(2,1)S(1)}) custom-call(bf16[12,192,128]{2,1,0:T(8,128)(2,1)S(1)} %get-tuple-element.32.own_ref, bf16[128,128]{1,0:T(8,128)(2,1)S(1)} %get-tuple-element.33.wq_ref, bf16[128,128]{1,0:T(8,128)(2,1)S(1)} %get-tuple-element.34.wg_ref), custom_call_target="tpu_custom_call" | custom-call | flops 301989888 | bytes 5898240 | tf_op jit(solution)/shard_map/ask/pallas_call | solution.py:266
  56.1 0.0 collective-permute-done.4.other_ref
  56.1 1.1 project.1
  57.2 3.8 %collective-permute-done.3.part_ref = bf16[1152,128]{1,0:T(8,128)(2,1)S(1)} collective-permute-done((bf16[1152,128]{1,0:T(8,128)(2,1)S(1)}, bf16[1152,128]{1,0:T(8,128)(2,1)S(1)}, u32[]{:S(2)}, u32[]{:S(2)}) %collective-permute-start.3) | collective-permute-done | bytes 294944 | tf_op jit(solution)/shard_map/ppermute | solution.py:369
  61.0 0.8 place.5.refs_0_
  61.9 1.5 %collective-permute-done.7.part_ref = bf16[1152,128]{1,0:T(8,128)(2,1)S(1)} collective-permute-done((bf16[1152,128]{1,0:T(8,128)(2,1)S(1)}, bf16[1152,128]{1,0:T(8,128)(2,1)S(1)}, u32[]{:S(2)}, u32[]{:S(2)}) %collective-permute-start.7) | collective-permute-done | bytes 294944 | tf_op jit(solution)/shard_map/ppermute | solution.py:369
  63.4 0.8 place.6.refs_0_
  64.2 4.3 %collective-permute-done.6.part_ref = bf16[1152,128]{1,0:T(8,128)(2,1)S(1)} collective-permute-done((bf16[1152,128]{1,0:T(8,128)(2,1)S(1)}, bf16[1152,128]{1,0:T(8,128)(2,1)S(1)}, u32[]{:S(2)}, u32[]{:S(2)}) %collective-permute-start.6) | collective-permute-done | bytes 294944 | tf_op jit(solution)/shard_map/ppermute | solution.py:369
  68.6 0.0 collective-permute-done.5.far_ref
  68.6 0.0 collective-permute-start.8
  68.6 0.8 place.7.bias_ref
  69.4 1.1 %collective-permute-done.8.other_ref = bf16[12,192,128]{2,1,0:T(8,128)(2,1)S(1)} collective-permute-done((bf16[12,192,128]{2,1,0:T(8,128)(2,1)S(1)}, bf16[12,192,128]{2,1,0:T(8,128)(2,1)S(1)}, u32[]{:S(2)}, u32[]{:S(2)}) %collective-permute-start.8) | collective-permute-done | bytes 589856 | tf_op jit(solution)/shard_map/ppermute | solution.py:378
  70.6 10.4 %attend.1 = bf16[12,192,128]{2,1,0:T(8,128)(2,1)S(1)} custom-call(bf16[12,384,128]{2,1,0:T(8,128)(2,1)S(1)} %get-tuple-element.41.k0_ref, bf16[12,128,384]{2,1,0:T(8,128)(2,1)S(1)} %get-tuple-element.42.v0_ref, bf16[12,192,128]{2,1,0:T(8,128)(2,1)S(1)} %collective-permute-done.5.far_ref, bf16[12,192,128]{2,1,0:T(8,128)(2,1)S(1)} %collective-permute-done.8.other_ref, ...), custom_call_target="tpu_custom_call" | custom-call | flops 7247757312 | bytes 7077888 | tf_op jit(solution)/shard_map/attend/pallas_call | solution.py:331
  81.0 0.5 copy.26
  81.5 27.3 %all_to_all.10 = bf16[64,9,4,128]{3,2,1,0:T(4,128)(2,1)S(1)} all-to-all(bf16[64,9,4,128]{3,2,1,0:T(4,128)(2,1)S(1)} %copy.26), channel_id=1, replica_groups=mesh['xl'=2,'y'=4,'z'=8,'c'=2,'h'=2] {'xl','y','z'}, dimensions={0} | all-to-all | bytes 1179648 | tf_op jit(solution)/shard_map/all_to_all | solution.py:383
  108.7 0.3 reshape.23
  109.1 0.9 copy.27
  (7 shorter events, 0.0 us)
Async XLA Ops:
  0.0 6.5 %collective-permute-start = (bf16[6,768,128]{2,1,0:T(8,128)(2,1)}, bf16[6,768,128]{2,1,0:T(8,128)(2,1)S(1)}, u32[]{:S(2)}, u32[]{:S(2)}) collective-permute-start(bf16[6,768,128]{2,1,0:T(8,128)(2,1)} %own_ref.1), channel_id=1, source_target_pairs={{0,2},{2,0},{1,3},{3,1},{4,6},{6,4},{5,7},{7,5},{8,10},{10,8},{9,1... | collective-permute-start | bytes 3538952 | tf_op jit(solution)/shard_map/ppermute | solution.py:354
  0.7 5.8 %collective-permute-start.1 = (bf16[16,128]{1,0:T(8,128)(2,1)S(1)}, bf16[16,128]{1,0:T(8,128)(2,1)S(1)}, u32[]{:S(2)}, u32[]{:S(2)}) collective-permute-start(bf16[16,128]{1,0:T(8,128)(2,1)S(1)} %pad.4.w_own_ref), channel_id=1, source_target_pairs={{0,1},{1,0},{2,3},{3,2},{4,5},{5,4},{6,7},{7,6},{8,9},{9,8},{10,11... | collective-permute-start | bytes 12296 | tf_op jit(solution)/shard_map/ppermute | solution.py:352
  3.6 1.3 %copy-start = (bf16[6,768,128]{2,1,0:T(8,128)(2,1)S(1)}, bf16[6,768,128]{2,1,0:T(8,128)(2,1)}, u32[]{:S(2)}) copy-start(bf16[6,768,128]{2,1,0:T(8,128)(2,1)} %own_ref.1) | copy-start | bytes 3538948
  6.5 15.5 %copy-start.1 = (bf16[128,4,64]{0,2,1:T(8,128)(2,1)S(1)}, bf16[128,4,64]{0,2,1:T(8,128)(2,1)}, u32[]{:S(2)}) copy-start(bf16[128,4,64]{0,2,1:T(8,128)(2,1)} %param.9) | copy-start | bytes 196612
  6.5 15.5 %copy-start.2 = (bf16[64,128]{1,0:T(8,128)(2,1)S(1)}, bf16[64,128]{1,0:T(8,128)(2,1)}, u32[]{:S(2)}) copy-start(bf16[64,128]{1,0:T(8,128)(2,1)} %param.11) | copy-start | bytes 49156
  8.8 40.4 %all-to-all-start = ((bf16[64,56,128]{2,1,0:T(8,128)(2,1)}), bf16[64,56,128]{2,1,0:T(8,128)(2,1)S(1)}, u32[]{:S(2)}, u32[]{:S(2)}) async-start(bf16[64,56,128]{2,1,0:T(8,128)(2,1)} %pack.1), calls=%async_computation | async-start | bytes 1835008 | tf_op jit(solution)/shard_map/all_to_all | solution.py:355
  22.0 6.7 %collective-permute-start.2 = (bf16[128,320]{0,1:T(8,128)(2,1)S(1)}, bf16[128,320]{0,1:T(8,128)(2,1)S(1)}, u32[]{:S(2)}, u32[]{:S(2)}) collective-permute-start(bf16[128,320]{0,1:T(8,128)(2,1)S(1)} %pad_maximum_fusion), channel_id=1, source_target_pairs={{0,1},{1,0},{2,3},{3,2},{4,5},{5,4},{6,7},{7,6},{8,9},{9,8},{10,11... | collective-permute-start | bytes 245768 | tf_op jit(solution)/shard_map/ppermute | solution.py:357
  49.6 6.5 %collective-permute-start.4 = (bf16[12,192,128]{2,1,0:T(8,128)(2,1)S(1)}, bf16[12,192,128]{2,1,0:T(8,128)(2,1)S(1)}, u32[]{:S(2)}, u32[]{:S(2)}) collective-permute-start(bf16[12,192,128]{2,1,0:T(8,128)(2,1)S(1)} %get-tuple-element.32.own_ref), channel_id=1, source_target_pairs={{0,2},{2,0},{1,3},{3,1},{4,6},{6,4},{5,7},{7,5},{8,10},{10,8},{9,1... | collective-permute-start | bytes 1769480 | tf_op jit(solution)/shard_map/ppermute | solution.py:371
  49.7 18.9 %collective-permute-start.5 = (bf16[12,192,128]{2,1,0:T(8,128)(2,1)S(1)}, bf16[12,192,128]{2,1,0:T(8,128)(2,1)S(1)}, u32[]{:S(2)}, u32[]{:S(2)}) collective-permute-start(bf16[12,192,128]{2,1,0:T(8,128)(2,1)S(1)} %get-tuple-element.32.own_ref), channel_id=1, source_target_pairs={{0,1},{1,0},{2,3},{3,2},{4,5},{5,4},{6,7},{7,6},{8,9},{9,8},{10,11... | collective-permute-start | bytes 1769480 | tf_op jit(solution)/shard_map/ppermute | solution.py:368
  51.2 9.9 %collective-permute-start.3 = (bf16[1152,128]{1,0:T(8,128)(2,1)S(1)}, bf16[1152,128]{1,0:T(8,128)(2,1)S(1)}, u32[]{:S(2)}, u32[]{:S(2)}) collective-permute-start(bf16[1152,128]{1,0:T(8,128)(2,1)S(1)} %get-tuple-element.31.part_ref), channel_id=1, source_target_pairs={{0,96},{32,0},{64,32},{96,64},{1,97},{33,1},{65,33},{97,65},{2,98}... | collective-permute-start | bytes 884744 | tf_op jit(solution)/shard_map/ppermute | solution.py:369
  52.0 11.4 %collective-permute-start.7 = (bf16[1152,128]{1,0:T(8,128)(2,1)S(1)}, bf16[1152,128]{1,0:T(8,128)(2,1)S(1)}, u32[]{:S(2)}, u32[]{:S(2)}) collective-permute-start(bf16[1152,128]{1,0:T(8,128)(2,1)S(1)} %get-tuple-element.31.part_ref), channel_id=1, source_target_pairs={{0,64},{32,96},{64,0},{96,32},{1,65},{33,97},{65,1},{97,33},{2,66}... | collective-permute-start | bytes 884744 | tf_op jit(solution)/shard_map/ppermute | solution.py:369
  53.8 14.7 %collective-permute-start.6 = (bf16[1152,128]{1,0:T(8,128)(2,1)S(1)}, bf16[1152,128]{1,0:T(8,128)(2,1)S(1)}, u32[]{:S(2)}, u32[]{:S(2)}) collective-permute-start(bf16[1152,128]{1,0:T(8,128)(2,1)S(1)} %get-tuple-element.31.part_ref), channel_id=1, source_target_pairs={{0,32},{32,64},{64,96},{96,0},{1,33},{33,65},{65,97},{97,1},{2,34}... | collective-permute-start | bytes 884744 | tf_op jit(solution)/shard_map/ppermute | solution.py:369
  68.6 2.0 %collective-permute-start.8 = (bf16[12,192,128]{2,1,0:T(8,128)(2,1)S(1)}, bf16[12,192,128]{2,1,0:T(8,128)(2,1)S(1)}, u32[]{:S(2)}, u32[]{:S(2)}) collective-permute-start(bf16[12,192,128]{2,1,0:T(8,128)(2,1)S(1)} %collective-permute-done.5.far_ref), channel_id=1, source_target_pairs={{0,2},{2,0},{1,3},{3,1},{4,6},{6,4},{5,7},{7,5},{8,10},{10,8},{9,1... | collective-permute-start | bytes 1769480 | tf_op jit(solution)/shard_map/ppermute | solution.py:378

commit v7 on v6

--- a/solution.py
+++ b/solution.py
@@ -79,7 +79,7 @@
             at = r * QR + q * CHIPS
             picked_ref[at : at + CHIPS, :] = got.astype(BF16)
     for r in range(3):
-        held[...] = own_ref[3 * (1 - h) + r].astype(F32)
+        held[:N, :] = own_ref[3 * (1 - h) + r].astype(F32)
         got = [held[pl.ds(first + q, CHIPS, stride=COLS), :] for q in range(3)]
         at = (3 + r) * QR
         picked_ref[at : at + QR, :] = layer_norm(jnp.concatenate(got, axis=0), gain, shift).astype(BF16)
@@ -94,7 +94,7 @@
         lay_kernel,
         in_specs=[SMEM, VMEM, VMEM],
         out_specs=[VMEM, VMEM],
-        scratch_shapes=[pltpu.VMEM((3 * N, C), F32), pltpu.VMEM((N, C), F32)],
+        scratch_shapes=[pltpu.VMEM((3 * N + 16, C), F32), pltpu.VMEM((N + 16, C), F32)],
         out_shape=[
             jax.ShapeDtypeStruct((3 * N, C), F32),
             jax.ShapeDtypeStruct((ROWS * QR, C), BF16),
@@ -117,7 +117,7 @@
     for half in range(2):
         entries.append(picked_ref[half * 3 * QR : (half + 1) * 3 * QR, :])
         for r in range(3):
-            held[...] = other_ref[3 * (h if half == 0 else 1 - h) + r].astype(F32)
+            held[:N, :] = other_ref[3 * (h if half == 0 else 1 - h) + r].astype(F32)
             got = [held[pl.ds(first + q, CHIPS, stride=COLS), :] for q in range(3)]
             entries.append(layer_norm(jnp.concatenate(got, axis=0), gain, shift).astype(BF16))
     entries = jnp.concatenate(entries, axis=0)
@@ -144,7 +144,7 @@
         in_specs=[SMEM] + [VMEM] * 6,
         out_specs=VMEM,
         scratch_shapes=[
-            pltpu.VMEM((N, C), F32),
+            pltpu.VMEM((N + 16, C), F32),
             pltpu.VMEM((4 * SHARE, C), F32),
             pltpu.VMEM((CHIPS * 24, C), F32),
         ],

time: 110 us -> 110 us (level)
  no operation moved by 1% of the time
where the time goes in v7:
time: 110 us
  waiting for transfers between devices  36.4 us (33%)
  blocking collectives  27.3 us (25%)
  starting transfers between devices  21.1 us (19%)
  Pallas kernels  20.4 us (19%)
  local copies, waits for them, and re-layouts  3.81 us (3%)
    all_to_all x1, blocking collectives, local(): returned = lax.all_to_all(sent, CHIP, 0, 0, tiled=True)  27.3 us
    all_to_all x1, waiting for transfers between devices, local(): arrived = lax.all_to_all(blocks, CHIP, 0, 0, tiled=True)  20.4 us
    all_to_all x1, starting transfers between devices, local(): arrived = lax.all_to_all(blocks, CHIP, 0, 0, tiled=True)  13.2 us
    pallas_call x1, Pallas kernels, attend(): pl.pallas_call(attend_kernel, in_specs=[VMEM] * 10, out_specs=VMEM, out_s...  10.4 us
    ppermute x3, waiting for transfers between devices, local(): lax.ppermute(share, 'y', [(i, (i + o) % 4) for i in range(4)])  9.66 us
    ppermute x1, waiting for transfers between devices, local(): weights_other = swap_heads(weights)  5.23 us
    pallas_call x4, Pallas kernels, place_bias(): pl.pallas_call(place_kernel, grid_spec=pltpu.PrefetchScalarGridSpec(num_s...  3.37 us
    ppermute x3, starting transfers between devices, local(): lax.ppermute(share, 'y', [(i, (i + o) % 4) for i in range(4)])  2.69 us
  transfers between devices with their start and end apart: 10, of which 6 were waited for; matrix products, arithmetic and copies ran while one was open for 1% of the time, Pallas kernels for 7%

profile of v7, /device:TPU:2, one launch (start us, length us, event | category | flops | bytes accessed | tf_op | source)
XLA Modules:
  0.0 110.0 jit_solution(1362382997950470441)
XLA Ops:
  0.0 0.0 collective-permute-start
  0.0 0.7 pad.4.w_own_ref
  0.7 2.1 %collective-permute-start.1 = (bf16[16,128]{1,0:T(8,128)(2,1)S(1)}, bf16[16,128]{1,0:T(8,128)(2,1)S(1)}, u32[]{:S(2)}, u32[]{:S(2)}) collective-permute-start(bf16[16,128]{1,0:T(8,128)(2,1)S(1)} %pad.4.w_own_ref), channel_id=1, source_target_pairs={{0,1},{1,0},{2,3},{3,2},{4,5},{5,4},{6,7},{7,6},{8,9},{9,8},{10,11... | collective-permute-start | bytes 12296 | tf_op jit(solution)/shard_map/ppermute | solution.py:352
  2.8 0.7 pad_maximum_fusion.3.norm_ref
  3.5 0.1 stack.32.where_ref
  3.6 0.0 copy-start
  3.6 1.3 %copy-done = bf16[6,768,128]{2,1,0:T(8,128)(2,1)S(1)} copy-done((bf16[6,768,128]{2,1,0:T(8,128)(2,1)S(1)}, bf16[6,768,128]{2,1,0:T(8,128)(2,1)}, u32[]{:S(2)}) %copy-start) | copy-done | bytes 1179672
  4.8 1.6 %lay.1 = (f32[2304,128]{1,0:T(8,128)S(1)}, bf16[1152,128]{1,0:T(8,128)(2,1)S(1)}) custom-call(s32[5]{0:T(128)S(1)} %stack.32.where_ref, bf16[6,768,128]{2,1,0:T(8,128)(2,1)S(1)} %copy-done, f32[2,128]{1,0:T(2,128)S(1)} %pad_maximum_fusion.3.norm_ref), custom_call_target="tpu_custom_call" | custom-call | flops 11796480 | bytes 3538944 | tf_op jit(solution)/shard_map/lay/pallas_call | solution.py:93
  6.5 0.0 collective-permute-done.1.w_other_ref
  6.5 0.0 collective-permute-done.other_ref
  6.5 0.0 copy-start.1
  6.5 0.0 copy-start.2
  6.5 2.3 %pack.1 = bf16[64,56,128]{2,1,0:T(8,128)(2,1)} custom-call(s32[5]{0:T(128)S(1)} %stack.32.where_ref, f32[2304,128]{1,0:T(8,128)S(1)} %get-tuple-element.28.laid_ref, bf16[1152,128]{1,0:T(8,128)(2,1)S(1)} %get-tuple-element.29.picked_ref, bf16[6,768,128]{2,1,0:T(8,128)(2,1)S(1)} %collective-permute-done.other_ref, f32[2,128]{1,0:T(2,128)S(1)} %pad_maximum_fusion.3.norm_ref, ...), custom_call_target="tpu_custom_call" | custom-call | flops 35389440 | bytes 3538944 | tf_op jit(solution)/shard_map/pack/pallas_call | solution.py:142
  8.8 13.2 %all-to-all-start = ((bf16[64,56,128]{2,1,0:T(8,128)(2,1)}), bf16[64,56,128]{2,1,0:T(8,128)(2,1)S(1)}, u32[]{:S(2)}, u32[]{:S(2)}) async-start(bf16[64,56,128]{2,1,0:T(8,128)(2,1)} %pack.1), calls=%async_computation | async-start | bytes 1835008 | tf_op jit(solution)/shard_map/all_to_all | solution.py:355
  22.0 0.0 copy-done.1
  22.0 0.0 copy-done.2
  22.0 1.5 %collective-permute-start.2 = (bf16[128,320]{0,1:T(8,128)(2,1)S(1)}, bf16[128,320]{0,1:T(8,128)(2,1)S(1)}, u32[]{:S(2)}, u32[]{:S(2)}) collective-permute-start(bf16[128,320]{0,1:T(8,128)(2,1)S(1)} %pad_maximum_fusion), channel_id=1, source_target_pairs={{0,1},{1,0},{2,3},{3,2},{4,5},{5,4},{6,7},{7,6},{8,9},{9,8},{10,11... | collective-permute-start | bytes 245768 | tf_op jit(solution)/shard_map/ppermute | solution.py:357
  23.5 5.2 %collective-permute-done.2 = bf16[128,320]{0,1:T(8,128)(2,1)S(1)} collective-permute-done((bf16[128,320]{0,1:T(8,128)(2,1)S(1)}, bf16[128,320]{0,1:T(8,128)(2,1)S(1)}, u32[]{:S(2)}, u32[]{:S(2)}) %collective-permute-start.2) | collective-permute-done | bytes 81952 | tf_op jit(solution)/shard_map/ppermute | solution.py:357
  28.8 20.4 %all-to-all-done.arrived_ref = bf16[64,56,128]{2,1,0:T(8,128)(2,1)S(1)} async-done(((bf16[64,56,128]{2,1,0:T(8,128)(2,1)}), bf16[64,56,128]{2,1,0:T(8,128)(2,1)S(1)}, u32[]{:S(2)}, u32[]{:S(2)}) %all-to-all-start) | async-done | bytes 917536 | tf_op jit(solution)/shard_map/all_to_all | solution.py:355
  49.2 0.4 unpack.1
  49.6 0.1 collective-permute-start.4
  49.7 1.5 %collective-permute-start.5 = (bf16[12,192,128]{2,1,0:T(8,128)(2,1)S(1)}, bf16[12,192,128]{2,1,0:T(8,128)(2,1)S(1)}, u32[]{:S(2)}, u32[]{:S(2)}) collective-permute-start(bf16[12,192,128]{2,1,0:T(8,128)(2,1)S(1)} %get-tuple-element.32.own_ref), channel_id=1, source_target_pairs={{0,1},{1,0},{2,3},{3,2},{4,5},{5,4},{6,7},{7,6},{8,9},{9,8},{10,11... | collective-permute-start | bytes 1769480 | tf_op jit(solution)/shard_map/ppermute | solution.py:368
  51.2 0.8 collective-permute-start.3
  52.0 1.9 %collective-permute-start.7 = (bf16[1152,128]{1,0:T(8,128)(2,1)S(1)}, bf16[1152,128]{1,0:T(8,128)(2,1)S(1)}, u32[]{:S(2)}, u32[]{:S(2)}) collective-permute-start(bf16[1152,128]{1,0:T(8,128)(2,1)S(1)} %get-tuple-element.31.part_ref), channel_id=1, source_target_pairs={{0,64},{32,96},{64,0},{96,32},{1,65},{33,97},{65,1},{97,33},{2,66}... | collective-permute-start | bytes 884744 | tf_op jit(solution)/shard_map/ppermute | solution.py:369
  53.8 0.0 collective-permute-start.6
  53.8 0.1 copy.24.wk_ref
  54.0 0.8 place.4.refs_0_
  54.8 1.3 %ask.1 = (bf16[12,128,768]{2,1,0:T(8,128)(2,1)S(1)}, bf16[12,64,384]{2,1,0:T(8,128)(2,1)S(1)}) custom-call(bf16[12,192,128]{2,1,0:T(8,128)(2,1)S(1)} %get-tuple-element.32.own_ref, bf16[128,128]{1,0:T(8,128)(2,1)S(1)} %get-tuple-element.33.wq_ref, bf16[128,128]{1,0:T(8,128)(2,1)S(1)} %get-tuple-element.34.wg_ref), custom_call_target="tpu_custom_call" | custom-call | flops 301989888 | bytes 5898240 | tf_op jit(solution)/shard_map/ask/pallas_call | solution.py:266
  56.1 0.0 collective-permute-done.4.other_ref
  56.1 1.1 project.1
  57.2 3.8 %collective-permute-done.3.part_ref = bf16[1152,128]{1,0:T(8,128)(2,1)S(1)} collective-permute-done((bf16[1152,128]{1,0:T(8,128)(2,1)S(1)}, bf16[1152,128]{1,0:T(8,128)(2,1)S(1)}, u32[]{:S(2)}, u32[]{:S(2)}) %collective-permute-start.3) | collective-permute-done | bytes 294944 | tf_op jit(solution)/shard_map/ppermute | solution.py:369
  61.0 0.8 place.5.refs_0_
  61.9 1.5 %collective-permute-done.7.part_ref = bf16[1152,128]{1,0:T(8,128)(2,1)S(1)} collective-permute-done((bf16[1152,128]{1,0:T(8,128)(2,1)S(1)}, bf16[1152,128]{1,0:T(8,128)(2,1)S(1)}, u32[]{:S(2)}, u32[]{:S(2)}) %collective-permute-start.7) | collective-permute-done | bytes 294944 | tf_op jit(solution)/shard_map/ppermute | solution.py:369
  63.4 0.8 place.6.refs_0_
  64.2 4.3 %collective-permute-done.6.part_ref = bf16[1152,128]{1,0:T(8,128)(2,1)S(1)} collective-permute-done((bf16[1152,128]{1,0:T(8,128)(2,1)S(1)}, bf16[1152,128]{1,0:T(8,128)(2,1)S(1)}, u32[]{:S(2)}, u32[]{:S(2)}) %collective-permute-start.6) | collective-permute-done | bytes 294944 | tf_op jit(solution)/shard_map/ppermute | solution.py:369
  68.6 0.0 collective-permute-done.5.far_ref
  68.6 0.0 collective-permute-start.8
  68.6 0.8 place.7.bias_ref
  69.4 1.1 %collective-permute-done.8.other_ref = bf16[12,192,128]{2,1,0:T(8,128)(2,1)S(1)} collective-permute-done((bf16[12,192,128]{2,1,0:T(8,128)(2,1)S(1)}, bf16[12,192,128]{2,1,0:T(8,128)(2,1)S(1)}, u32[]{:S(2)}, u32[]{:S(2)}) %collective-permute-start.8) | collective-permute-done | bytes 589856 | tf_op jit(solution)/shard_map/ppermute | solution.py:378
  70.6 10.4 %attend.1 = bf16[12,192,128]{2,1,0:T(8,128)(2,1)S(1)} custom-call(bf16[12,384,128]{2,1,0:T(8,128)(2,1)S(1)} %get-tuple-element.41.k0_ref, bf16[12,128,384]{2,1,0:T(8,128)(2,1)S(1)} %get-tuple-element.42.v0_ref, bf16[12,192,128]{2,1,0:T(8,128)(2,1)S(1)} %collective-permute-done.5.far_ref, bf16[12,192,128]{2,1,0:T(8,128)(2,1)S(1)} %collective-permute-done.8.other_ref, ...), custom_call_target="tpu_custom_call" | custom-call | flops 7247757312 | bytes 7077888 | tf_op jit(solution)/shard_map/attend/pallas_call | solution.py:331
  81.0 0.5 copy.26
  81.5 27.3 %all_to_all.10 = bf16[64,9,4,128]{3,2,1,0:T(4,128)(2,1)S(1)} all-to-all(bf16[64,9,4,128]{3,2,1,0:T(4,128)(2,1)S(1)} %copy.26), channel_id=1, replica_groups=mesh['xl'=2,'y'=4,'z'=8,'c'=2,'h'=2] {'xl','y','z'}, dimensions={0} | all-to-all | bytes 1179648 | tf_op jit(solution)/shard_map/all_to_all | solution.py:383
  108.8 0.3 reshape.23
  109.1 0.9 copy.27
  (7 shorter events, 0.0 us)
Async XLA Ops:
  0.0 6.5 %collective-permute-start = (bf16[6,768,128]{2,1,0:T(8,128)(2,1)}, bf16[6,768,128]{2,1,0:T(8,128)(2,1)S(1)}, u32[]{:S(2)}, u32[]{:S(2)}) collective-permute-start(bf16[6,768,128]{2,1,0:T(8,128)(2,1)} %own_ref.1), channel_id=1, source_target_pairs={{0,2},{2,0},{1,3},{3,1},{4,6},{6,4},{5,7},{7,5},{8,10},{10,8},{9,1... | collective-permute-start | bytes 3538952 | tf_op jit(solution)/shard_map/ppermute | solution.py:354
  0.7 5.8 %collective-permute-start.1 = (bf16[16,128]{1,0:T(8,128)(2,1)S(1)}, bf16[16,128]{1,0:T(8,128)(2,1)S(1)}, u32[]{:S(2)}, u32[]{:S(2)}) collective-permute-start(bf16[16,128]{1,0:T(8,128)(2,1)S(1)} %pad.4.w_own_ref), channel_id=1, source_target_pairs={{0,1},{1,0},{2,3},{3,2},{4,5},{5,4},{6,7},{7,6},{8,9},{9,8},{10,11... | collective-permute-start | bytes 12296 | tf_op jit(solution)/shard_map/ppermute | solution.py:352
  3.6 1.3 %copy-start = (bf16[6,768,128]{2,1,0:T(8,128)(2,1)S(1)}, bf16[6,768,128]{2,1,0:T(8,128)(2,1)}, u32[]{:S(2)}) copy-start(bf16[6,768,128]{2,1,0:T(8,128)(2,1)} %own_ref.1) | copy-start | bytes 3538948
  6.5 15.5 %copy-start.1 = (bf16[128,4,64]{0,2,1:T(8,128)(2,1)S(1)}, bf16[128,4,64]{0,2,1:T(8,128)(2,1)}, u32[]{:S(2)}) copy-start(bf16[128,4,64]{0,2,1:T(8,128)(2,1)} %param.9) | copy-start | bytes 196612
  6.5 15.5 %copy-start.2 = (bf16[64,128]{1,0:T(8,128)(2,1)S(1)}, bf16[64,128]{1,0:T(8,128)(2,1)}, u32[]{:S(2)}) copy-start(bf16[64,128]{1,0:T(8,128)(2,1)} %param.11) | copy-start | bytes 49156
  8.8 40.4 %all-to-all-start = ((bf16[64,56,128]{2,1,0:T(8,128)(2,1)}), bf16[64,56,128]{2,1,0:T(8,128)(2,1)S(1)}, u32[]{:S(2)}, u32[]{:S(2)}) async-start(bf16[64,56,128]{2,1,0:T(8,128)(2,1)} %pack.1), calls=%async_computation | async-start | bytes 1835008 | tf_op jit(solution)/shard_map/all_to_all | solution.py:355
  22.0 6.7 %collective-permute-start.2 = (bf16[128,320]{0,1:T(8,128)(2,1)S(1)}, bf16[128,320]{0,1:T(8,128)(2,1)S(1)}, u32[]{:S(2)}, u32[]{:S(2)}) collective-permute-start(bf16[128,320]{0,1:T(8,128)(2,1)S(1)} %pad_maximum_fusion), channel_id=1, source_target_pairs={{0,1},{1,0},{2,3},{3,2},{4,5},{5,4},{6,7},{7,6},{8,9},{9,8},{10,11... | collective-permute-start | bytes 245768 | tf_op jit(solution)/shard_map/ppermute | solution.py:357
  49.6 6.5 %collective-permute-start.4 = (bf16[12,192,128]{2,1,0:T(8,128)(2,1)S(1)}, bf16[12,192,128]{2,1,0:T(8,128)(2,1)S(1)}, u32[]{:S(2)}, u32[]{:S(2)}) collective-permute-start(bf16[12,192,128]{2,1,0:T(8,128)(2,1)S(1)} %get-tuple-element.32.own_ref), channel_id=1, source_target_pairs={{0,2},{2,0},{1,3},{3,1},{4,6},{6,4},{5,7},{7,5},{8,10},{10,8},{9,1... | collective-permute-start | bytes 1769480 | tf_op jit(solution)/shard_map/ppermute | solution.py:371
  49.7 18.9 %collective-permute-start.5 = (bf16[12,192,128]{2,1,0:T(8,128)(2,1)S(1)}, bf16[12,192,128]{2,1,0:T(8,128)(2,1)S(1)}, u32[]{:S(2)}, u32[]{:S(2)}) collective-permute-start(bf16[12,192,128]{2,1,0:T(8,128)(2,1)S(1)} %get-tuple-element.32.own_ref), channel_id=1, source_target_pairs={{0,1},{1,0},{2,3},{3,2},{4,5},{5,4},{6,7},{7,6},{8,9},{9,8},{10,11... | collective-permute-start | bytes 1769480 | tf_op jit(solution)/shard_map/ppermute | solution.py:368
  51.2 9.9 %collective-permute-start.3 = (bf16[1152,128]{1,0:T(8,128)(2,1)S(1)}, bf16[1152,128]{1,0:T(8,128)(2,1)S(1)}, u32[]{:S(2)}, u32[]{:S(2)}) collective-permute-start(bf16[1152,128]{1,0:T(8,128)(2,1)S(1)} %get-tuple-element.31.part_ref), channel_id=1, source_target_pairs={{0,96},{32,0},{64,32},{96,64},{1,97},{33,1},{65,33},{97,65},{2,98}... | collective-permute-start | bytes 884744 | tf_op jit(solution)/shard_map/ppermute | solution.py:369
  52.0 11.4 %collective-permute-start.7 = (bf16[1152,128]{1,0:T(8,128)(2,1)S(1)}, bf16[1152,128]{1,0:T(8,128)(2,1)S(1)}, u32[]{:S(2)}, u32[]{:S(2)}) collective-permute-start(bf16[1152,128]{1,0:T(8,128)(2,1)S(1)} %get-tuple-element.31.part_ref), channel_id=1, source_target_pairs={{0,64},{32,96},{64,0},{96,32},{1,65},{33,97},{65,1},{97,33},{2,66}... | collective-permute-start | bytes 884744 | tf_op jit(solution)/shard_map/ppermute | solution.py:369
  53.8 14.7 %collective-permute-start.6 = (bf16[1152,128]{1,0:T(8,128)(2,1)S(1)}, bf16[1152,128]{1,0:T(8,128)(2,1)S(1)}, u32[]{:S(2)}, u32[]{:S(2)}) collective-permute-start(bf16[1152,128]{1,0:T(8,128)(2,1)S(1)} %get-tuple-element.31.part_ref), channel_id=1, source_target_pairs={{0,32},{32,64},{64,96},{96,0},{1,33},{33,65},{65,97},{97,1},{2,34}... | collective-permute-start | bytes 884744 | tf_op jit(solution)/shard_map/ppermute | solution.py:369
  68.6 2.0 %collective-permute-start.8 = (bf16[12,192,128]{2,1,0:T(8,128)(2,1)S(1)}, bf16[12,192,128]{2,1,0:T(8,128)(2,1)S(1)}, u32[]{:S(2)}, u32[]{:S(2)}) collective-permute-start(bf16[12,192,128]{2,1,0:T(8,128)(2,1)S(1)} %collective-permute-done.5.far_ref), channel_id=1, source_target_pairs={{0,2},{2,0},{1,3},{3,1},{4,6},{6,4},{5,7},{7,5},{8,10},{10,8},{9,1... | collective-permute-start | bytes 1769480 | tf_op jit(solution)/shard_map/ppermute | solution.py:378

commit v8 on v7

--- a/solution.py
+++ b/solution.py
@@ -180,42 +180,28 @@
     )(arrived)
 
 
-def place_kernel(where_ref, norm_ref, w_own_ref, w_other_ref, part_ref, *refs):
+def place_kernel(step, where_ref, norm_ref, w_own_ref, w_other_ref, part_ref, *refs):
     out_ref = refs[-1]
     reaches = [bias_range(w_ref[...], norm_ref[0:1], norm_ref[1:2])[1] for w_ref in (w_own_ref, w_other_ref)]
     scale = [jnp.broadcast_to(reach[g : g + 1] * ROOT, (8, QR)) for reach in reaches for g in range(2)]
     scale = jnp.concatenate(scale, axis=1)[:1]
+    quarter = lax.rem(where_ref[2] - step + 4, 4) * QR
     for a in range(3):
+        to = pl.multiple_of(quarter + a * CHIPS, CHIPS)
         for s in range(6):
             lanes = slice(s * C, (s + 1) * C)
             at = (a * 6 + s) * CHIPS
-            out_ref[a * CHIPS : (a + 1) * CHIPS, lanes] = decode(part_ref[at : at + CHIPS, :]) * scale[:, lanes]
+            out_ref[pl.ds(to, CHIPS), lanes] = decode(part_ref[at : at + CHIPS, :]) * scale[:, lanes]
 
 
 def place_bias(where, norm, w_own, w_other, part, step, bias):
-    small = lambda g, w: (0, 0)
-    in_specs = [
-        pl.BlockSpec((2, C), small),
-        pl.BlockSpec((16, C), small),
-        pl.BlockSpec((16, C), small),
-        pl.BlockSpec((SHARE * CHIPS, C), small),
-    ]
-    operands = [where, norm, w_own, w_other, part]
-    aliases = {}
-    if bias is not None:
-        in_specs.append(pl.BlockSpec(memory_space=pl.ANY))
-        operands.append(bias)
-        aliases = {5: 0}
-    return pl.pallas_call(
-        place_kernel,
-        grid_spec=pltpu.PrefetchScalarGridSpec(
-            num_scalar_prefetch=1,
-            grid=(1,),
-            in_specs=in_specs,
-            out_specs=pl.BlockSpec((QR, 4 * QR), lambda g, w: (lax.rem(w[2] - step + 4, 4), 0)),
-        ),
+    operands = [where, norm, w_own, w_other, part] + ([] if bias is None else [bias])
+    return pl.pallas_call(
+        functools.partial(place_kernel, step),
+        in_specs=[SMEM] + [VMEM] * (len(operands) - 1),
+        out_specs=VMEM,
         out_shape=jax.ShapeDtypeStruct((N, 4 * QR), F32),
-        input_output_aliases=aliases,
+        input_output_aliases={} if bias is None else {5: 0},
         compiler_params=params(16),
         cost_estimate=pl.CostEstimate(flops=5 * N * N, bytes_accessed=2 * N * N, transcendentals=0),
         name="place",

time: 110 us -> 110 us (level)
  no operation moved by 1% of the time
where the time goes in v8:
time: 110 us
  waiting for transfers between devices  36.4 us (33%)
  blocking collectives  27.3 us (25%)
  starting transfers between devices  21.1 us (19%)
  Pallas kernels  20.4 us (19%)
  local copies, waits for them, and re-layouts  3.81 us (3%)
    all_to_all x1, blocking collectives, local(): returned = lax.all_to_all(sent, CHIP, 0, 0, tiled=True)  27.3 us
    all_to_all x1, waiting for transfers between devices, local(): arrived = lax.all_to_all(blocks, CHIP, 0, 0, tiled=True)  20.4 us
    all_to_all x1, starting transfers between devices, local(): arrived = lax.all_to_all(blocks, CHIP, 0, 0, tiled=True)  13.2 us
    pallas_call x1, Pallas kernels, attend(): pl.pallas_call(attend_kernel, in_specs=[VMEM] * 10, out_specs=VMEM, out_s...  10.4 us
    ppermute x3, waiting for transfers between devices, local(): lax.ppermute(share, 'y', [(i, (i + o) % 4) for i in range(4)])  9.66 us
    ppermute x1, waiting for transfers between devices, local(): weights_other = swap_heads(weights)  5.23 us
    pallas_call x4, Pallas kernels, place_bias(): pl.pallas_call(functools.partial(place_kernel, step), in_specs=[SMEM] + [...  3.37 us
    ppermute x3, starting transfers between devices, local(): lax.ppermute(share, 'y', [(i, (i + o) % 4) for i in range(4)])  2.69 us
  transfers between devices with their start and end apart: 10, of which 6 were waited for; matrix products, arithmetic and copies ran while one was open for 1% of the time, Pallas kernels for 7%

profile of v8, /device:TPU:2, one launch (start us, length us, event | category | flops | bytes accessed | tf_op | source)
XLA Modules:
  0.0 110.0 jit_solution(13265675619706325147)
XLA Ops:
  0.0 0.0 collective-permute-start
  0.0 0.7 pad.4.w_own_ref
  0.7 2.1 %collective-permute-start.1 = (bf16[16,128]{1,0:T(8,128)(2,1)S(1)}, bf16[16,128]{1,0:T(8,128)(2,1)S(1)}, u32[]{:S(2)}, u32[]{:S(2)}) collective-permute-start(bf16[16,128]{1,0:T(8,128)(2,1)S(1)} %pad.4.w_own_ref), channel_id=1, source_target_pairs={{0,1},{1,0},{2,3},{3,2},{4,5},{5,4},{6,7},{7,6},{8,9},{9,8},{10,11... | collective-permute-start | bytes 12296 | tf_op jit(solution)/shard_map/ppermute | solution.py:338
  2.8 0.7 pad_maximum_fusion.3.norm_ref
  3.5 0.1 stack.32.where_ref
  3.6 0.0 copy-start
  3.6 1.3 %copy-done = bf16[6,768,128]{2,1,0:T(8,128)(2,1)S(1)} copy-done((bf16[6,768,128]{2,1,0:T(8,128)(2,1)S(1)}, bf16[6,768,128]{2,1,0:T(8,128)(2,1)}, u32[]{:S(2)}) %copy-start) | copy-done | bytes 1179672
  4.8 1.6 %lay.1 = (f32[2304,128]{1,0:T(8,128)S(1)}, bf16[1152,128]{1,0:T(8,128)(2,1)S(1)}) custom-call(s32[5]{0:T(128)S(1)} %stack.32.where_ref, bf16[6,768,128]{2,1,0:T(8,128)(2,1)S(1)} %copy-done, f32[2,128]{1,0:T(2,128)S(1)} %pad_maximum_fusion.3.norm_ref), custom_call_target="tpu_custom_call" | custom-call | flops 11796480 | bytes 3538944 | tf_op jit(solution)/shard_map/lay/pallas_call | solution.py:93
  6.5 0.0 collective-permute-done.1.w_other_ref
  6.5 0.0 collective-permute-done.other_ref
  6.5 0.0 copy-start.1
  6.5 0.0 copy-start.2
  6.5 2.3 %pack.1 = bf16[64,56,128]{2,1,0:T(8,128)(2,1)} custom-call(s32[5]{0:T(128)S(1)} %stack.32.where_ref, f32[2304,128]{1,0:T(8,128)S(1)} %get-tuple-element.28.laid_ref, bf16[1152,128]{1,0:T(8,128)(2,1)S(1)} %get-tuple-element.29.picked_ref, bf16[6,768,128]{2,1,0:T(8,128)(2,1)S(1)} %collective-permute-done.other_ref, f32[2,128]{1,0:T(2,128)S(1)} %pad_maximum_fusion.3.norm_ref, ...), custom_call_target="tpu_custom_call" | custom-call | flops 35389440 | bytes 3538944 | tf_op jit(solution)/shard_map/pack/pallas_call | solution.py:142
  8.8 13.2 %all-to-all-start = ((bf16[64,56,128]{2,1,0:T(8,128)(2,1)}), bf16[64,56,128]{2,1,0:T(8,128)(2,1)S(1)}, u32[]{:S(2)}, u32[]{:S(2)}) async-start(bf16[64,56,128]{2,1,0:T(8,128)(2,1)} %pack.1), calls=%async_computation | async-start | bytes 1835008 | tf_op jit(solution)/shard_map/all_to_all | solution.py:341
  22.0 0.0 copy-done.1
  22.0 0.0 copy-done.2
  22.0 1.5 %collective-permute-start.2 = (bf16[128,320]{0,1:T(8,128)(2,1)S(1)}, bf16[128,320]{0,1:T(8,128)(2,1)S(1)}, u32[]{:S(2)}, u32[]{:S(2)}) collective-permute-start(bf16[128,320]{0,1:T(8,128)(2,1)S(1)} %pad_maximum_fusion), channel_id=1, source_target_pairs={{0,1},{1,0},{2,3},{3,2},{4,5},{5,4},{6,7},{7,6},{8,9},{9,8},{10,11... | collective-permute-start | bytes 245768 | tf_op jit(solution)/shard_map/ppermute | solution.py:343
  23.5 5.2 %collective-permute-done.2 = bf16[128,320]{0,1:T(8,128)(2,1)S(1)} collective-permute-done((bf16[128,320]{0,1:T(8,128)(2,1)S(1)}, bf16[128,320]{0,1:T(8,128)(2,1)S(1)}, u32[]{:S(2)}, u32[]{:S(2)}) %collective-permute-start.2) | collective-permute-done | bytes 81952 | tf_op jit(solution)/shard_map/ppermute | solution.py:343
  28.8 20.4 %all-to-all-done.arrived_ref = bf16[64,56,128]{2,1,0:T(8,128)(2,1)S(1)} async-done(((bf16[64,56,128]{2,1,0:T(8,128)(2,1)}), bf16[64,56,128]{2,1,0:T(8,128)(2,1)S(1)}, u32[]{:S(2)}, u32[]{:S(2)}) %all-to-all-start) | async-done | bytes 917536 | tf_op jit(solution)/shard_map/all_to_all | solution.py:341
  49.2 0.4 unpack.1
  49.6 0.1 collective-permute-start.4
  49.7 1.5 %collective-permute-start.5 = (bf16[12,192,128]{2,1,0:T(8,128)(2,1)S(1)}, bf16[12,192,128]{2,1,0:T(8,128)(2,1)S(1)}, u32[]{:S(2)}, u32[]{:S(2)}) collective-permute-start(bf16[12,192,128]{2,1,0:T(8,128)(2,1)S(1)} %get-tuple-element.32.own_ref), channel_id=1, source_target_pairs={{0,1},{1,0},{2,3},{3,2},{4,5},{5,4},{6,7},{7,6},{8,9},{9,8},{10,11... | collective-permute-start | bytes 1769480 | tf_op jit(solution)/shard_map/ppermute | solution.py:354
  51.2 0.8 collective-permute-start.3
  52.0 1.9 %collective-permute-start.7 = (bf16[1152,128]{1,0:T(8,128)(2,1)S(1)}, bf16[1152,128]{1,0:T(8,128)(2,1)S(1)}, u32[]{:S(2)}, u32[]{:S(2)}) collective-permute-start(bf16[1152,128]{1,0:T(8,128)(2,1)S(1)} %get-tuple-element.31.part_ref), channel_id=1, source_target_pairs={{0,64},{32,96},{64,0},{96,32},{1,65},{33,97},{65,1},{97,33},{2,66}... | collective-permute-start | bytes 884744 | tf_op jit(solution)/shard_map/ppermute | solution.py:355
  53.8 0.0 collective-permute-start.6
  53.8 0.1 copy.24.wk_ref
  54.0 0.9 place.4.refs_0_
  54.8 1.3 %ask.1 = (bf16[12,128,768]{2,1,0:T(8,128)(2,1)S(1)}, bf16[12,64,384]{2,1,0:T(8,128)(2,1)S(1)}) custom-call(bf16[12,192,128]{2,1,0:T(8,128)(2,1)S(1)} %get-tuple-element.32.own_ref, bf16[128,128]{1,0:T(8,128)(2,1)S(1)} %get-tuple-element.33.wq_ref, bf16[128,128]{1,0:T(8,128)(2,1)S(1)} %get-tuple-element.34.wg_ref), custom_call_target="tpu_custom_call" | custom-call | flops 301989888 | bytes 5898240 | tf_op jit(solution)/shard_map/ask/pallas_call | solution.py:252
  56.1 0.0 collective-permute-done.4.other_ref
  56.1 1.1 project.1
  57.2 3.8 %collective-permute-done.3.part_ref = bf16[1152,128]{1,0:T(8,128)(2,1)S(1)} collective-permute-done((bf16[1152,128]{1,0:T(8,128)(2,1)S(1)}, bf16[1152,128]{1,0:T(8,128)(2,1)S(1)}, u32[]{:S(2)}, u32[]{:S(2)}) %collective-permute-start.3) | collective-permute-done | bytes 294944 | tf_op jit(solution)/shard_map/ppermute | solution.py:355
  61.0 0.8 place.5.refs_0_
  61.9 1.5 %collective-permute-done.7.part_ref = bf16[1152,128]{1,0:T(8,128)(2,1)S(1)} collective-permute-done((bf16[1152,128]{1,0:T(8,128)(2,1)S(1)}, bf16[1152,128]{1,0:T(8,128)(2,1)S(1)}, u32[]{:S(2)}, u32[]{:S(2)}) %collective-permute-start.7) | collective-permute-done | bytes 294944 | tf_op jit(solution)/shard_map/ppermute | solution.py:355
  63.4 0.8 place.6.refs_0_
  64.2 4.3 %collective-permute-done.6.part_ref = bf16[1152,128]{1,0:T(8,128)(2,1)S(1)} collective-permute-done((bf16[1152,128]{1,0:T(8,128)(2,1)S(1)}, bf16[1152,128]{1,0:T(8,128)(2,1)S(1)}, u32[]{:S(2)}, u32[]{:S(2)}) %collective-permute-start.6) | collective-permute-done | bytes 294944 | tf_op jit(solution)/shard_map/ppermute | solution.py:355
  68.6 0.0 collective-permute-done.5.far_ref
  68.6 0.0 collective-permute-start.8
  68.6 0.8 place.7.bias_ref
  69.4 1.1 %collective-permute-done.8.other_ref = bf16[12,192,128]{2,1,0:T(8,128)(2,1)S(1)} collective-permute-done((bf16[12,192,128]{2,1,0:T(8,128)(2,1)S(1)}, bf16[12,192,128]{2,1,0:T(8,128)(2,1)S(1)}, u32[]{:S(2)}, u32[]{:S(2)}) %collective-permute-start.8) | collective-permute-done | bytes 589856 | tf_op jit(solution)/shard_map/ppermute | solution.py:364
  70.6 10.4 %attend.1 = bf16[12,192,128]{2,1,0:T(8,128)(2,1)S(1)} custom-call(bf16[12,384,128]{2,1,0:T(8,128)(2,1)S(1)} %get-tuple-element.41.k0_ref, bf16[12,128,384]{2,1,0:T(8,128)(2,1)S(1)} %get-tuple-element.42.v0_ref, bf16[12,192,128]{2,1,0:T(8,128)(2,1)S(1)} %collective-permute-done.5.far_ref, bf16[12,192,128]{2,1,0:T(8,128)(2,1)S(1)} %collective-permute-done.8.other_ref, ...), custom_call_target="tpu_custom_call" | custom-call | flops 7247757312 | bytes 7077888 | tf_op jit(solution)/shard_map/attend/pallas_call | solution.py:317
  81.0 0.5 copy.26
  81.5 27.3 %all_to_all.10 = bf16[64,9,4,128]{3,2,1,0:T(4,128)(2,1)S(1)} all-to-all(bf16[64,9,4,128]{3,2,1,0:T(4,128)(2,1)S(1)} %copy.26), channel_id=1, replica_groups=mesh['xl'=2,'y'=4,'z'=8,'c'=2,'h'=2] {'xl','y','z'}, dimensions={0} | all-to-all | bytes 1179648 | tf_op jit(solution)/shard_map/all_to_all | solution.py:369
  108.8 0.3 reshape.23
  109.1 0.9 copy.27
  (7 shorter events, 0.0 us)
Async XLA Ops:
  0.0 6.5 %collective-permute-start = (bf16[6,768,128]{2,1,0:T(8,128)(2,1)}, bf16[6,768,128]{2,1,0:T(8,128)(2,1)S(1)}, u32[]{:S(2)}, u32[]{:S(2)}) collective-permute-start(bf16[6,768,128]{2,1,0:T(8,128)(2,1)} %own_ref.1), channel_id=1, source_target_pairs={{0,2},{2,0},{1,3},{3,1},{4,6},{6,4},{5,7},{7,5},{8,10},{10,8},{9,1... | collective-permute-start | bytes 3538952 | tf_op jit(solution)/shard_map/ppermute | solution.py:340
  0.7 5.8 %collective-permute-start.1 = (bf16[16,128]{1,0:T(8,128)(2,1)S(1)}, bf16[16,128]{1,0:T(8,128)(2,1)S(1)}, u32[]{:S(2)}, u32[]{:S(2)}) collective-permute-start(bf16[16,128]{1,0:T(8,128)(2,1)S(1)} %pad.4.w_own_ref), channel_id=1, source_target_pairs={{0,1},{1,0},{2,3},{3,2},{4,5},{5,4},{6,7},{7,6},{8,9},{9,8},{10,11... | collective-permute-start | bytes 12296 | tf_op jit(solution)/shard_map/ppermute | solution.py:338
  3.6 1.3 %copy-start = (bf16[6,768,128]{2,1,0:T(8,128)(2,1)S(1)}, bf16[6,768,128]{2,1,0:T(8,128)(2,1)}, u32[]{:S(2)}) copy-start(bf16[6,768,128]{2,1,0:T(8,128)(2,1)} %own_ref.1) | copy-start | bytes 3538948
  6.5 15.5 %copy-start.1 = (bf16[128,4,64]{0,2,1:T(8,128)(2,1)S(1)}, bf16[128,4,64]{0,2,1:T(8,128)(2,1)}, u32[]{:S(2)}) copy-start(bf16[128,4,64]{0,2,1:T(8,128)(2,1)} %param.9) | copy-start | bytes 196612
  6.5 15.5 %copy-start.2 = (bf16[64,128]{1,0:T(8,128)(2,1)S(1)}, bf16[64,128]{1,0:T(8,128)(2,1)}, u32[]{:S(2)}) copy-start(bf16[64,128]{1,0:T(8,128)(2,1)} %param.11) | copy-start | bytes 49156
  8.8 40.4 %all-to-all-start = ((bf16[64,56,128]{2,1,0:T(8,128)(2,1)}), bf16[64,56,128]{2,1,0:T(8,128)(2,1)S(1)}, u32[]{:S(2)}, u32[]{:S(2)}) async-start(bf16[64,56,128]{2,1,0:T(8,128)(2,1)} %pack.1), calls=%async_computation | async-start | bytes 1835008 | tf_op jit(solution)/shard_map/all_to_all | solution.py:341
  22.0 6.7 %collective-permute-start.2 = (bf16[128,320]{0,1:T(8,128)(2,1)S(1)}, bf16[128,320]{0,1:T(8,128)(2,1)S(1)}, u32[]{:S(2)}, u32[]{:S(2)}) collective-permute-start(bf16[128,320]{0,1:T(8,128)(2,1)S(1)} %pad_maximum_fusion), channel_id=1, source_target_pairs={{0,1},{1,0},{2,3},{3,2},{4,5},{5,4},{6,7},{7,6},{8,9},{9,8},{10,11... | collective-permute-start | bytes 245768 | tf_op jit(solution)/shard_map/ppermute | solution.py:343
  49.6 6.5 %collective-permute-start.4 = (bf16[12,192,128]{2,1,0:T(8,128)(2,1)S(1)}, bf16[12,192,128]{2,1,0:T(8,128)(2,1)S(1)}, u32[]{:S(2)}, u32[]{:S(2)}) collective-permute-start(bf16[12,192,128]{2,1,0:T(8,128)(2,1)S(1)} %get-tuple-element.32.own_ref), channel_id=1, source_target_pairs={{0,2},{2,0},{1,3},{3,1},{4,6},{6,4},{5,7},{7,5},{8,10},{10,8},{9,1... | collective-permute-start | bytes 1769480 | tf_op jit(solution)/shard_map/ppermute | solution.py:357
  49.7 18.9 %collective-permute-start.5 = (bf16[12,192,128]{2,1,0:T(8,128)(2,1)S(1)}, bf16[12,192,128]{2,1,0:T(8,128)(2,1)S(1)}, u32[]{:S(2)}, u32[]{:S(2)}) collective-permute-start(bf16[12,192,128]{2,1,0:T(8,128)(2,1)S(1)} %get-tuple-element.32.own_ref), channel_id=1, source_target_pairs={{0,1},{1,0},{2,3},{3,2},{4,5},{5,4},{6,7},{7,6},{8,9},{9,8},{10,11... | collective-permute-start | bytes 1769480 | tf_op jit(solution)/shard_map/ppermute | solution.py:354
  51.2 9.9 %collective-permute-start.3 = (bf16[1152,128]{1,0:T(8,128)(2,1)S(1)}, bf16[1152,128]{1,0:T(8,128)(2,1)S(1)}, u32[]{:S(2)}, u32[]{:S(2)}) collective-permute-start(bf16[1152,128]{1,0:T(8,128)(2,1)S(1)} %get-tuple-element.31.part_ref), channel_id=1, source_target_pairs={{0,96},{32,0},{64,32},{96,64},{1,97},{33,1},{65,33},{97,65},{2,98}... | collective-permute-start | bytes 884744 | tf_op jit(solution)/shard_map/ppermute | solution.py:355
  52.0 11.4 %collective-permute-start.7 = (bf16[1152,128]{1,0:T(8,128)(2,1)S(1)}, bf16[1152,128]{1,0:T(8,128)(2,1)S(1)}, u32[]{:S(2)}, u32[]{:S(2)}) collective-permute-start(bf16[1152,128]{1,0:T(8,128)(2,1)S(1)} %get-tuple-element.31.part_ref), channel_id=1, source_target_pairs={{0,64},{32,96},{64,0},{96,32},{1,65},{33,97},{65,1},{97,33},{2,66}... | collective-permute-start | bytes 884744 | tf_op jit(solution)/shard_map/ppermute | solution.py:355
  53.8 14.7 %collective-permute-start.6 = (bf16[1152,128]{1,0:T(8,128)(2,1)S(1)}, bf16[1152,128]{1,0:T(8,128)(2,1)S(1)}, u32[]{:S(2)}, u32[]{:S(2)}) collective-permute-start(bf16[1152,128]{1,0:T(8,128)(2,1)S(1)} %get-tuple-element.31.part_ref), channel_id=1, source_target_pairs={{0,32},{32,64},{64,96},{96,0},{1,33},{33,65},{65,97},{97,1},{2,34}... | collective-permute-start | bytes 884744 | tf_op jit(solution)/shard_map/ppermute | solution.py:355
  68.6 2.0 %collective-permute-start.8 = (bf16[12,192,128]{2,1,0:T(8,128)(2,1)S(1)}, bf16[12,192,128]{2,1,0:T(8,128)(2,1)S(1)}, u32[]{:S(2)}, u32[]{:S(2)}) collective-permute-start(bf16[12,192,128]{2,1,0:T(8,128)(2,1)S(1)} %collective-permute-done.5.far_ref), channel_id=1, source_target_pairs={{0,2},{2,0},{1,3},{3,1},{4,6},{6,4},{5,7},{7,5},{8,10},{10,8},{9,1... | collective-permute-start | bytes 1769480 | tf_op jit(solution)/shard_map/ppermute | solution.py:364
